TPU v7x, 512 devices: a whole 4x8x8 slice. The times are simulated.
512 devices in a mesh: dp: 8 (over z_lo, core), ctx: 64 (over x, y, z_hi).
Axes of the slice: x: 4, y: 8, z: 8 (z_hi: 2, z_lo: 4; z = z_hi * 4 + z_lo), core: 2. Of those that a mesh axis runs over, the one named last changes fastest.
Arguments:
- offsets: int32 [8], P('dp'), may hold values from 0 to 8176, as said below
- lengths: int32 [8], P('dp'), may hold values from 4 to 8192, as said below
- queries: bfloat16 [8, 16, 64, 576], P('dp', None, 'ctx'), may hold values from -2000 to 2000
- cotangent: bfloat16 [8, 16, 64, 512], P('dp', None, 'ctx'), may hold values from -6 to 6
- kv_rows: bfloat16 [8, 8192, 576], P('dp', 'ctx'), may hold values from -400 to 400
- kv_tangent: bfloat16 [8, 8192, 576], P('dp', 'ctx'), may hold values from -6 to 6
- norm_gain: float32 [512], replicated, may hold values from 0.5 to 1.5
- gain_tangent: float32 [512], replicated, may hold values from -6 to 6
Outputs:
- hv_rows: float32 [8, 8192, 576], P('dp', 'ctx')
- gain_pair: float32 [2, 512], replicated
Inputs may be any that keep to these rules, and one draw needn't show every extreme that they name: offsets[d] + 16 <= 8192. lengths[d] - offsets[d] lies between 4 and 16.
All inputs are finite; a program needn't handle non-finite values.
Results may differ from a plain program's by a relative error of at most 0.0067.
Values may be sent and summed in bfloat16 or wider, within the bound.
No kernel may reach another device: no remote copies, remote signals or barrier semaphores. Data moves between devices by JAX's collectives and lax.ppermute only.
A program may use at most 64 MiB of HBM per device.

v0:
```python
import jax
import jax.numpy as jnp
from jax import lax
from jax.sharding import PartitionSpec as P

score_scale = 192.0 ** (-0.5)
tiny_eps = 1e-06
masked_score = -1e30


def key_side(kv_rows, kv_tangent, norm_gain, gain_tangent, latent_width):
    latent = kv_rows[:, :latent_width].astype(jnp.float32)
    rope_part = kv_rows[:, latent_width:].astype(jnp.float32)
    latent_dot = kv_tangent[:, :latent_width].astype(jnp.float32)
    rope_dot = kv_tangent[:, latent_width:].astype(jnp.float32)
    inv_rms = lax.rsqrt(jnp.mean(latent * latent, axis=-1, keepdims=True) + tiny_eps)
    normed = latent * inv_rms
    inv_dot = -(inv_rms * inv_rms * inv_rms) * jnp.mean(latent * latent_dot, axis=-1, keepdims=True)
    normed_dot = latent_dot * inv_rms + latent * inv_dot
    key_rows = jnp.concatenate([normed * norm_gain, rope_part], axis=-1).astype(jnp.bfloat16)
    key_dots = jnp.concatenate(
        [gain_tangent * normed + norm_gain * normed_dot, rope_dot], axis=-1
    ).astype(jnp.bfloat16)
    return (key_rows, key_dots, (latent, latent_dot, inv_rms, inv_dot, normed, normed_dot))


def block_terms(query_blk, cot_blk, query_pos, key_rows, key_dots, key_pos, latent_width):
    scores = score_scale * jnp.einsum(
        "rc,kc->rk", query_blk, key_rows, preferred_element_type=jnp.float32
    )
    score_dot = score_scale * jnp.einsum(
        "rc,kc->rk", query_blk, key_dots, preferred_element_type=jnp.float32
    )
    value_grad = jnp.einsum(
        "rc,kc->rk", cot_blk, key_rows[:, :latent_width], preferred_element_type=jnp.float32
    )
    value_dot = jnp.einsum(
        "rc,kc->rk", cot_blk, key_dots[:, :latent_width], preferred_element_type=jnp.float32
    )
    visible = key_pos[None, :] <= query_pos[:, None]
    return (scores, score_dot, value_grad, value_dot, visible)


def local_stats(query_blk, cot_blk, query_pos, key_rows, key_dots, key_pos, latent_width):
    scores, score_dot, value_grad, value_dot, visible = block_terms(
        query_blk, cot_blk, query_pos, key_rows, key_dots, key_pos, latent_width
    )
    maxima = jnp.max(jnp.where(visible, scores, masked_score), axis=1)
    weights = jnp.where(visible, jnp.exp(scores - maxima[:, None]), 0.0)
    return (
        maxima,
        (
            jnp.sum(weights, axis=1),
            jnp.sum(weights * score_dot, axis=1),
            jnp.sum(weights * value_grad, axis=1),
            jnp.sum(weights * score_dot * value_grad, axis=1),
            jnp.sum(weights * value_dot, axis=1),
        ),
    )


def grad_terms(
    query_blk, cot_blk, query_pos, softmax_stats, key_rows, key_dots, key_pos, latent_width
):
    scores, score_dot, value_grad, value_dot, visible = block_terms(
        query_blk, cot_blk, query_pos, key_rows, key_dots, key_pos, latent_width
    )
    maxima, totals, moment_a, moment_b, moment_c, moment_e = softmax_stats
    attention = jnp.where(visible, jnp.exp(scores - maxima[:, None]), 0.0) / totals[:, None]
    shift_mean = moment_a / totals
    grad_mean = moment_b / totals
    grad_mean_dot = (moment_c - shift_mean * moment_b + moment_e) / totals
    attention_dot = attention * (score_dot - shift_mean[:, None])
    score_grad = attention * (value_grad - grad_mean[:, None])
    score_grad_dot = attention_dot * (value_grad - grad_mean[:, None]) + attention * (
        value_dot - grad_mean_dot[:, None]
    )
    key_grad = score_scale * jnp.einsum(
        "rk,rc->kc", score_grad.astype(jnp.bfloat16), query_blk, preferred_element_type=jnp.float32
    )
    key_grad_dot = score_scale * jnp.einsum(
        "rk,rc->kc",
        score_grad_dot.astype(jnp.bfloat16),
        query_blk,
        preferred_element_type=jnp.float32,
    )
    value_sum = jnp.einsum(
        "rk,rc->kc", attention.astype(jnp.bfloat16), cot_blk, preferred_element_type=jnp.float32
    )
    value_sum_dot = jnp.einsum(
        "rk,rc->kc", attention_dot.astype(jnp.bfloat16), cot_blk, preferred_element_type=jnp.float32
    )
    return (key_grad, key_grad_dot, value_sum, value_sum_dot)


def zero_grads(key_rows, latent_width):
    key_count, full_width = key_rows.shape
    return (
        jnp.zeros((key_count, full_width), jnp.float32),
        jnp.zeros((key_count, full_width), jnp.float32),
        jnp.zeros((key_count, latent_width), jnp.float32),
        jnp.zeros((key_count, latent_width), jnp.float32),
    )


def accumulate(
    flat_queries, flat_cot, flat_pos, softmax_stats, key_rows, key_dots, key_pos, latent_width
):

    def advance(running, block_items):
        partial_terms = grad_terms(
            block_items[0],
            block_items[1],
            block_items[2],
            block_items[3],
            key_rows,
            key_dots,
            key_pos,
            latent_width,
        )
        return (tuple((former + latter for former, latter in zip(running, partial_terms))), None)

    result, leftover = lax.scan(
        advance,
        zero_grads(key_rows, latent_width),
        (flat_queries, flat_cot, flat_pos, softmax_stats),
    )
    return result


def finish(totals, norm_saved, norm_gain, gain_tangent, latent_width):
    key_grad, key_grad_dot, value_sum, value_sum_dot = totals
    latent, latent_dot, inv_rms, inv_dot, normed, normed_dot = norm_saved
    latent_grad = key_grad[:, :latent_width] + value_sum
    latent_grad_dot = key_grad_dot[:, :latent_width] + value_sum_dot
    gain_grad = jnp.sum(latent_grad * normed, axis=0)
    gain_grad_dot = jnp.sum(latent_grad_dot * normed + latent_grad * normed_dot, axis=0)
    normed_grad = latent_grad * norm_gain
    normed_grad_dot = latent_grad_dot * norm_gain + latent_grad * gain_tangent
    inner_grad = jnp.mean(normed_grad * latent, axis=-1, keepdims=True)
    inner_grad_dot = jnp.mean(
        normed_grad_dot * latent + normed_grad * latent_dot, axis=-1, keepdims=True
    )
    rms_cubed = inv_rms * inv_rms * inv_rms
    rms_cubed_dot = 3.0 * inv_rms * inv_rms * inv_dot
    row_dot = (
        inv_dot * normed_grad
        + inv_rms * normed_grad_dot
        - rms_cubed_dot * latent * inner_grad
        - rms_cubed * latent_dot * inner_grad
        - rms_cubed * latent * inner_grad_dot
    )
    hv_rows = jnp.concatenate([row_dot, key_grad_dot[:, latent_width:]], axis=-1)
    return (hv_rows, gain_grad, gain_grad_dot)


def settle(local_maxima, partial_value):
    maxima = lax.pmax(local_maxima, "ctx")
    factor = jnp.exp(local_maxima - maxima)
    summed = lax.psum(
        (
            factor * partial_value[0],
            factor * partial_value[1],
            factor * partial_value[2],
            factor * partial_value[3],
            factor * partial_value[4],
        ),
        "ctx",
    )
    return (maxima, summed[0], summed[1], summed[2], summed[3], summed[4])


def shards(offsets, lengths, queries, cotangent, kv_rows, kv_tangent, norm_gain, gain_tangent):
    latent_width = norm_gain.shape[0]
    slab_rows = queries.shape[1]
    key_count = kv_rows.shape[1]
    start_pos = offsets[0]
    live_rows = jnp.arange(slab_rows, dtype=jnp.int32) < lengths[0] - start_pos
    masked_cot = jnp.where(live_rows[None, :, None, None], cotangent, jnp.zeros_like(cotangent))
    key_pos = lax.axis_index("ctx") * key_count + jnp.arange(key_count, dtype=jnp.int32)
    key_rows, key_dots, norm_saved = key_side(
        kv_rows[0], kv_tangent[0], norm_gain, gain_tangent, latent_width
    )
    all_queries, all_cot = (
        lax.all_gather(queries, "ctx", axis=2, tiled=True),
        lax.all_gather(masked_cot, "ctx", axis=2, tiled=True),
    )
    head_count = all_queries.shape[2]
    row_count = slab_rows * head_count
    block_rows = min(512, row_count)
    block_count = row_count // block_rows
    flat_queries = all_queries.reshape(block_count, block_rows, -1)
    flat_cot = all_cot.reshape(block_count, block_rows, -1)
    flat_pos = (start_pos + jnp.arange(row_count, dtype=jnp.int32) // head_count).reshape(
        block_count, block_rows
    )

    def first_pass(block_items):
        return local_stats(
            block_items[0],
            block_items[1],
            block_items[2],
            key_rows,
            key_dots,
            key_pos,
            latent_width,
        )

    local_maxima, partial_value = lax.map(first_pass, (flat_queries, flat_cot, flat_pos))
    softmax_stats = settle(local_maxima, partial_value)
    totals = accumulate(
        flat_queries, flat_cot, flat_pos, softmax_stats, key_rows, key_dots, key_pos, latent_width
    )
    hv_rows, gain_grad, gain_grad_dot = finish(
        totals, norm_saved, norm_gain, gain_tangent, latent_width
    )
    summed = lax.psum((gain_grad, gain_grad_dot), ("dp", "ctx"))
    return (hv_rows[None], jnp.stack([summed[0], summed[1]]))


def solution(mesh):
    in_specs = (
        P("dp"),
        P("dp"),
        P("dp", None, "ctx", None),
        P("dp", None, "ctx", None),
        P("dp", "ctx", None),
        P("dp", "ctx", None),
        P(),
        P(),
    )
    out_specs = (P("dp", "ctx", None), P())
    return jax.shard_map(shards, mesh=mesh, in_specs=in_specs, out_specs=out_specs, check_vma=False)
```

profile of v0, /device:TPU:1, one launch (start us, length us, event | category | flops | bytes accessed | tf_op | source)
XLA Modules:
  0.0 1052.3 jit_solution(13161632976589654196)
XLA Ops:
  8.5 1.4 bitcast_select_fusion
  10.0 0.7 all-gather.3.cloned.1.call-update
  10.8 0.7 slice.46
  11.5 0.7 slice.47
  12.2 1.1 fusion.84
  13.3 1.2 fusion.73
  14.5 0.2 copy.32
  14.7 0.2 copy.31
  14.9 129.0 %all-gather.5.cloned.1.call-done = bf16[1,16,64,512]{3,1,0,2:T(8,128)(2,1)} async-done(((bf16[1,16,1,512]{3,1,0,2:T(8,128)(2,1)}), bf16[1,16,64,512]{3,1,0,2:T(8,128)(2,1)}) %all-gather.5.cloned.1.call-update) | async-done | bytes 1048592 | tf_op jit(solution)/shard_map/all_gather | solution.py:186
  143.9 1.8 copy.29
  145.7 128.8 %all-gather.3.cloned.1.call-done = bf16[1,16,64,576]{3,1,0,2:T(8,128)(2,1)} async-done(((bf16[1,16,1,576]{3,1,0,2:T(8,128)(2,1)}), bf16[1,16,64,576]{3,1,0,2:T(8,128)(2,1)}) %all-gather.3.cloned.1.call-update) | async-done | bytes 1179664 | tf_op jit(solution)/shard_map/all_gather | solution.py:185
  274.5 1.6 copy.27
  276.1 3.4 while.38
  276.2 0.4 fusion.128
  276.5 0.3 fusion.130
  277.0 0.4 fusion.129
  277.3 0.3 multiply_reduce_fusion.3
  277.9 0.4 fusion.128
  278.2 0.3 fusion.130
  278.7 0.4 fusion.129
  279.0 0.3 multiply_reduce_fusion.3
  279.5 187.3 %pmax.7 = f32[2,512]{1,0:T(2,128)S(1)} all-reduce(f32[2,512]{1,0:T(2,128)S(1)} %get-tuple-element.164), channel_id=1, replica_groups=mesh['dp'=8,'ctx'=64] {'ctx'}, use_global_device_ids=true, to_apply=%region_10.11 | all-reduce | flops 1024 | bytes 8192 | tf_op jit(solution)/shard_map/pmax | solution.py:158
  466.9 378.4 %all-reduce.1 = (f32[2,512]{1,0:T(2,128)S(1)}, f32[2,512]{1,0:T(2,128)S(1)}, f32[2,512]{1,0:T(2,128)S(1)}, f32[2,512]{1,0:T(2,128)S(1)}, f32[2,512]{1,0:T(2,128)S(1)}) all-reduce(f32[2,512]{1,0:T(2,128)S(1)} %get-tuple-element.448, f32[2,512]{1,0:T(2,128)S(1)} %get-tuple-element.447, ...), channel_id=1, replica_groups=mesh['dp'=8,'ctx'=64] {'ctx'}, use_global_device_ids=true, to_apply=%region_11.12 | all-reduce | flops 5120 | bytes 40960 | tf_op jit(solution)/shard_map/psum | solution.py:160
  845.3 14.3 %while.39 = (s32[]{:T(128)}, f32[128,576]{0,1:T(8,128)}, f32[128,576]{0,1:T(8,128)}, f32[128,512]{1,0:T(8,128)}, f32[128,512]{1,0:T(8,128)}, /*index=5*/s32[2,51...) while((s32[]{:T(128)}, f32[128,576]{0,1:T(8,128)}, ...), condition=%wide.region_17.18_spmd.clone, body=%wide.region_16.17_spmd.clone.sunk | while | flops 572312704 | bytes 12577573 | solution.py:123
  845.4 0.4 fusion.145
  845.7 0.3 fusion.147
  846.1 0.3 convolution_subtract_fusion.3
  846.4 1.0 convolution_add_fusion.5
  847.4 1.5 fusion.148
  848.9 1.1 fusion.146
  850.0 0.3 convolution_add_fusion.4
  850.3 0.7 copy-done.2
  851.1 0.4 fusion.145
  851.5 0.3 fusion.147
  851.8 0.3 convolution_subtract_fusion.3
  852.1 1.9 convolution_add_fusion.5
  854.1 2.4 fusion.148
  856.5 2.1 fusion.146
  858.6 0.3 convolution_add_fusion.4
  858.9 0.7 copy-done.2
  859.6 1.1 copy.35
  860.8 0.8 slice.39
  861.5 1.1 copy.34
  862.6 1.6 fusion.76
  864.2 179.7 %all-reduce = (f32[1,512]{1,0:T(1,128)S(1)}, f32[1,512]{1,0:T(1,128)S(1)}) all-reduce(f32[1,512]{1,0:T(1,128)S(1)} %bitcast.158, f32[1,512]{1,0:T(1,128)S(1)} %bitcast.159), channel_id=1, replica_groups=mesh['dp'=8,'ctx'=64] {'dp','ctx'}, use_global_device_ids=true, to_apply=%region_23.24 | all-reduce | flops 1024 | bytes 8192 | tf_op jit(solution)/shard_map/psum | solution.py:217
  1043.9 0.6 pad_maximum_fusion.2
  1044.5 0.2 fusion.80
  1044.7 0.7 maximum_bitcast_fusion
  (65 shorter events, 0.9 us)
Async XLA Ops:
  7.2 136.7 %all-gather.5.cloned.1.call-start = ((), (), s32[]{:S(2)}) async-start(), calls=%async_computation.1 | async-start | bytes 1064960 | tf_op jit(solution)/shard_map/all_gather | solution.py:186
  9.9 264.6 %all-gather.3.cloned.1.call-start = ((), (), s32[]{:S(2)}) async-start(), calls=%async_computation | async-start | bytes 1331200 | tf_op jit(solution)/shard_map/all_gather | solution.py:185
  845.3 17.3 %copy-start.5 = (f32[512]{0:T(512)S(1)}, f32[512]{0:T(512)}, u32[]{:S(2)}) copy-start(f32[512]{0:T(512)} %param.19) | copy-start | bytes 6148
  845.3 17.3 %copy-start.6 = (f32[512]{0:T(512)S(1)}, f32[512]{0:T(512)}, u32[]{:S(2)}) copy-start(f32[512]{0:T(512)} %param.18) | copy-start | bytes 6148
  848.9 1.1 copy-start.1
  850.3 0.7 copy-start.2
  856.5 2.1 copy-start.1
  858.9 0.7 copy-start.2
  859.6 184.9 %copy-start = (f32[128,576]{0,1:T(8,128)S(1)}, f32[128,576]{0,1:T(8,128)}, u32[]{:S(2)}) copy-start(f32[128,576]{0,1:T(8,128)} %get-tuple-element.172) | copy-start | bytes 884740
  859.6 184.9 %copy-start.3 = (bf16[1,128,576]{1,2,0:T(8,128)(2,1)S(1)}, bf16[1,128,576]{1,2,0:T(8,128)(2,1)}, u32[]{:S(2)}) copy-start(bf16[1,128,576]{1,2,0:T(8,128)(2,1)} %param.16) | copy-start | bytes 442372
  859.6 184.9 %copy-start.4 = (bf16[1,128,576]{1,2,0:T(8,128)(2,1)S(1)}, bf16[1,128,576]{1,2,0:T(8,128)(2,1)}, u32[]{:S(2)}) copy-start(bf16[1,128,576]{1,2,0:T(8,128)(2,1)} %param.17) | copy-start | bytes 442372
Sparse Core Ops, SparseCore 0:
  12.5 131.3 all-gather.4
  148.5 125.9 all-gather.2
where the time goes:
time: 1050 us
  blocking collectives  745 us (71%)
  waiting for transfers between devices  259 us (25%)
  between operations  15.5 us (1%)
  matrix products  15.4 us (1%)
    psum x1, blocking collectives, settle(): lax.psum((factor * partial_value[0], factor * partial_value[1], factor *...  378 us
    pmax x1, blocking collectives, settle(): maxima = lax.pmax(local_maxima, 'ctx')  187 us
    psum x1, blocking collectives, shards(): summed = lax.psum((gain_grad, gain_grad_dot), ('dp', 'ctx'))  180 us
    all_gather x1, waiting for transfers between devices, shards(): lax.all_gather(masked_cot, 'ctx', axis=2, tiled=True)  129 us
    all_gather x1, waiting for transfers between devices, shards(): lax.all_gather(queries, 'ctx', axis=2, tiled=True)  129 us
  transfers between devices with their start and end apart: 2, of which 2 were waited for; matrix products, arithmetic and copies ran while one was open for 1% of the time, Pallas kernels for 0%

commit v1 on v0

v1 whole, which is shorter than its diff:
```python
import functools

import jax
import jax.numpy as jnp
from jax import lax
from jax.experimental import pallas as pl
from jax.experimental.pallas import tpu as pltpu
from jax.sharding import PartitionSpec as P

score_scale = 192.0 ** (-0.5)
tiny_eps = 1e-06
masked_score = -1e30

X, Y, ZH = 4, 8, 2
ZL, CORE = 4, 2
CTX = X * Y * ZH
Z = ZH * ZL


def ctx_index(x, y, zh):
    return (x * Y + y) * ZH + zh


def ctx_shift(dx, dy, dz):
    return [
        (ctx_index(x, y, z), ctx_index((x + dx) % X, (y + dy) % Y, (z + dz) % ZH))
        for x in range(X)
        for y in range(Y)
        for z in range(ZH)
    ]


def all_shift(dx, dy, dz, dc):
    pairs = []
    for x in range(X):
        for y in range(Y):
            for z in range(Z):
                for c in range(CORE):
                    x2, y2, z2, c2 = (x + dx) % X, (y + dy) % Y, (z + dz) % Z, (c + dc) % CORE
                    source = ((z % ZL) * CORE + c) * CTX + ctx_index(x, y, z // ZL)
                    target = ((z2 % ZL) * CORE + c2) * CTX + ctx_index(x2, y2, z2 // ZL)
                    pairs.append((source, target))
    return pairs


def ctx_permute(value, dx=0, dy=0, dz=0):
    return lax.ppermute(value, "ctx", ctx_shift(dx, dy, dz))


def all_permute(value, dx=0, dy=0, dz=0, dc=0):
    return lax.ppermute(value, ("dp", "ctx"), all_shift(dx, dy, dz, dc))


def ring_sum(parts):
    while len(parts) > 1:
        half = len(parts) // 2
        parts = [parts[k] + parts[k + half] for k in range(half)]
    return parts[0]


def key_side(kv_rows, kv_tangent, norm_gain, gain_tangent, latent_width):
    latent = kv_rows[:, :latent_width].astype(jnp.float32)
    latent_dot = kv_tangent[:, :latent_width].astype(jnp.float32)
    inv_rms = lax.rsqrt(jnp.mean(latent * latent, axis=-1, keepdims=True) + tiny_eps)
    normed = latent * inv_rms
    inv_dot = -(inv_rms * inv_rms * inv_rms) * jnp.mean(latent * latent_dot, axis=-1, keepdims=True)
    normed_dot = latent_dot * inv_rms + latent * inv_dot
    return (latent, latent_dot, inv_rms, inv_dot, normed, normed_dot)


def nt_dot(left, right):
    return lax.dot_general(
        left, right, (((1,), (1,)), ((), ())), preferred_element_type=jnp.float32
    )


def nn_dot(left, right):
    return lax.dot_general(
        left, right, (((1,), (0,)), ((), ())), preferred_element_type=jnp.float32
    )


def place_cotangents(cot_refs, cot_buf, slab):
    rows = ZH * slab
    for dy in range(Y):
        for dx in range(X):
            cot_buf[(dx * Y + dy) * rows : (dx * Y + dy + 1) * rows, :] = cot_refs[dy][
                dx * rows : (dx + 1) * rows, :
            ]


def block_terms(pos_ref, keys, query_blk, cot_blk, latent_width, slab):
    key_count = keys.shape[0] // 2
    row_count = query_blk.shape[0]
    offset, live_count, key_base = pos_ref[0], pos_ref[1], pos_ref[2]
    by_query = score_scale * nt_dot(keys, query_blk)
    by_cot = nt_dot(keys[:, :latent_width], cot_blk)
    slab_row = lax.broadcasted_iota(jnp.int32, (key_count, row_count), 1) % slab
    key_pos = key_base + lax.broadcasted_iota(jnp.int32, (key_count, row_count), 0)
    visible = key_pos <= offset + slab_row
    live = slab_row < live_count
    return (
        by_query[:key_count],
        by_query[key_count:],
        jnp.where(live, by_cot[:key_count], 0.0),
        jnp.where(live, by_cot[key_count:], 0.0),
        visible,
        live,
    )


def stats_kernel(latent_width, slab, *refs):
    pos_ref, keys_ref = refs[:2]
    query_refs, cot_refs = refs[2 : 2 + X], refs[2 + X : 2 + X + Y]
    stats_ref, cot_buf = refs[2 + X + Y :]
    place_cotangents(cot_refs, cot_buf, slab)
    block = Y * ZH * slab
    keys = keys_ref[...]
    for dx in range(X):
        lanes = slice(dx * block, (dx + 1) * block)
        scores, score_dot, value_grad, value_dot, visible, _ = block_terms(
            pos_ref, keys, query_refs[dx][...], cot_buf[lanes, :], latent_width, slab
        )
        maxima = jnp.max(jnp.where(visible, scores, masked_score), axis=0, keepdims=True)
        weights = jnp.where(visible, jnp.exp(scores - maxima), 0.0)
        weighted = weights * score_dot
        rows = [
            maxima,
            jnp.sum(weights, axis=0, keepdims=True),
            jnp.sum(weighted, axis=0, keepdims=True),
            jnp.sum(weights * value_grad, axis=0, keepdims=True),
            jnp.sum(weighted * value_grad, axis=0, keepdims=True),
            jnp.sum(weights * value_dot, axis=0, keepdims=True),
            jnp.zeros((2, block), jnp.float32),
        ]
        stats_ref[:, lanes] = jnp.concatenate(rows, axis=0)


def merge_kernel(turn, *refs):
    parts = [refs[0][...]] + [turn(ref[...], step + 1) for step, ref in enumerate(refs[1:-1])]
    maxima = functools.reduce(jnp.maximum, [part[0:1] for part in parts])
    total = sum(jnp.exp(part[0:1] - maxima) * part for part in parts)
    row = lax.broadcasted_iota(jnp.int32, total.shape, 0)
    refs[-1][...] = jnp.where(row == 0, maxima, total)


def turn_x(part, step):
    block = part.shape[1] // X
    return jnp.concatenate([part[:, (X - step) * block :], part[:, : (X - step) * block]], axis=1)


def turn_y(part, step):
    block = part.shape[1] // X
    each = block // Y
    return jnp.concatenate(
        [
            pltpu.roll(part[:, dx * block : (dx + 1) * block], step * each, 1)
            for dx in range(X)
        ],
        axis=1,
    )


def turn_z(part, step):
    width = part.shape[1]
    each = width // CTX
    lane = lax.broadcasted_iota(jnp.int32, part.shape, 1)
    return jnp.where(
        lane % (2 * each) < each, pltpu.roll(part, width - each, 1), pltpu.roll(part, each, 1)
    )


def merge(turn, parts):
    return pl.pallas_call(
        functools.partial(merge_kernel, turn),
        out_shape=jax.ShapeDtypeStruct(parts[0].shape, jnp.float32),
        name="merge_stats",
    )(*parts)


def grads_kernel(latent_width, slab, *refs):
    pos_ref, keys_ref, stats_ref, rows_ref, tangent_ref, gain_ref, gain_tangent_ref = refs[:7]
    query_refs, cot_refs = refs[7 : 7 + X], refs[7 + X : 7 + X + Y]
    hv_ref, pair_ref, cot_buf = refs[7 + X + Y :]
    place_cotangents(cot_refs, cot_buf, slab)
    block = Y * ZH * slab
    keys = keys_ref[...]
    key_count = keys.shape[0] // 2
    by_query = jnp.zeros(keys.shape, jnp.float32)
    by_cot = jnp.zeros((keys.shape[0], latent_width), jnp.float32)
    for dx in range(X):
        lanes = slice(dx * block, (dx + 1) * block)
        query_blk, cot_blk = query_refs[dx][...], cot_buf[lanes, :]
        scores, score_dot, value_grad, value_dot, visible, live = block_terms(
            pos_ref, keys, query_blk, cot_blk, latent_width, slab
        )
        stats = stats_ref[:, lanes]
        maxima, totals = stats[0:1], stats[1:2]
        moment_a, moment_b, moment_c, moment_e = stats[2:3], stats[3:4], stats[4:5], stats[5:6]
        inv_totals = 1.0 / totals
        shift_mean = moment_a * inv_totals
        grad_mean = moment_b * inv_totals
        grad_mean_dot = (moment_c - shift_mean * moment_b + moment_e) * inv_totals
        attention = jnp.where(visible, jnp.exp(scores - maxima), 0.0) * inv_totals
        attention_dot = attention * (score_dot - shift_mean)
        centred = value_grad - grad_mean
        score_grad = attention * centred
        score_grad_dot = attention_dot * centred + attention * (value_dot - grad_mean_dot)
        left = jnp.concatenate([score_grad, score_grad_dot], axis=0).astype(jnp.bfloat16)
        by_query = by_query + nn_dot(left, query_blk)
        live_left = jnp.concatenate(
            [jnp.where(live, attention, 0.0), jnp.where(live, attention_dot, 0.0)], axis=0
        ).astype(jnp.bfloat16)
        by_cot = by_cot + nn_dot(live_left, cot_blk)
    by_query = score_scale * by_query
    latent_grad = by_query[:key_count, :latent_width] + by_cot[:key_count]
    latent_grad_dot = by_query[key_count:, :latent_width] + by_cot[key_count:]
    norm_gain, gain_tangent = gain_ref[...], gain_tangent_ref[...]
    latent, latent_dot, inv_rms, inv_dot, normed, normed_dot = key_side(
        rows_ref[...], tangent_ref[...], norm_gain, gain_tangent, latent_width
    )
    pair_ref[0:1, :] = jnp.sum(latent_grad * normed, axis=0, keepdims=True)
    pair_ref[1:2, :] = jnp.sum(
        latent_grad_dot * normed + latent_grad * normed_dot, axis=0, keepdims=True
    )
    normed_grad = latent_grad * norm_gain
    normed_grad_dot = latent_grad_dot * norm_gain + latent_grad * gain_tangent
    inner_grad = jnp.mean(normed_grad * latent, axis=-1, keepdims=True)
    inner_grad_dot = jnp.mean(
        normed_grad_dot * latent + normed_grad * latent_dot, axis=-1, keepdims=True
    )
    rms_cubed = inv_rms * inv_rms * inv_rms
    rms_cubed_dot = 3.0 * inv_rms * inv_rms * inv_dot
    row_dot = (
        inv_dot * normed_grad
        + inv_rms * normed_grad_dot
        - (rms_cubed_dot * inner_grad + rms_cubed * inner_grad_dot) * latent
        - (rms_cubed * inner_grad) * latent_dot
    )
    hv_ref[:latent_width, :] = row_dot.T
    hv_ref[latent_width:, :] = by_query[key_count:, latent_width:].T


def in_vmem(count):
    return [pl.BlockSpec(memory_space=pltpu.VMEM)] * count


def shards(offsets, lengths, queries, cotangent, kv_rows, kv_tangent, norm_gain, gain_tangent):
    latent_width = norm_gain.shape[0]
    slab, full_width = queries.shape[1], queries.shape[3]
    key_count = kv_rows.shape[1]
    row_count = slab * CTX

    own_query = queries.reshape(slab, full_width)
    own_cot = cotangent.reshape(slab, latent_width)
    with jax.named_scope("gather_z"):
        query_z = jnp.concatenate([own_query, ctx_permute(own_query, dz=1)], axis=0)
        cot_z = jnp.concatenate([own_cot, ctx_permute(own_cot, dz=1)], axis=0)
    with jax.named_scope("gather_mid"):
        query_y = jnp.concatenate(
            [query_z] + [ctx_permute(query_z, dy=step) for step in range(1, Y)], axis=0
        )
        cot_x = jnp.concatenate(
            [cot_z] + [ctx_permute(cot_z, dx=step) for step in range(1, X)], axis=0
        )
    with jax.named_scope("gather_last"):
        query_parts = [query_y] + [ctx_permute(query_y, dx=step) for step in range(1, X)]
        cot_parts = [cot_x] + [ctx_permute(cot_x, dy=step) for step in range(1, Y)]

    rows, tangent = kv_rows[0], kv_tangent[0]
    normed, normed_dot = key_side(rows, tangent, norm_gain, gain_tangent, latent_width)[4:]
    keys = jnp.concatenate(
        [
            jnp.concatenate([normed * norm_gain, rows[:, latent_width:].astype(jnp.float32)], 1),
            jnp.concatenate(
                [
                    gain_tangent * normed + norm_gain * normed_dot,
                    tangent[:, latent_width:].astype(jnp.float32),
                ],
                1,
            ),
        ],
        axis=0,
    ).astype(jnp.bfloat16)
    positions = jnp.stack(
        [offsets[0], lengths[0] - offsets[0], lax.axis_index("ctx").astype(jnp.int32) * key_count]
    )
    smem = [pl.BlockSpec(memory_space=pltpu.SMEM)]
    flops = 4 * key_count * row_count * (full_width + latent_width)

    stats = pl.pallas_call(
        functools.partial(stats_kernel, latent_width, slab),
        out_shape=jax.ShapeDtypeStruct((8, row_count), jnp.float32),
        in_specs=smem + in_vmem(1 + X + Y),
        out_specs=pl.BlockSpec(memory_space=pltpu.VMEM),
        scratch_shapes=[pltpu.VMEM((row_count, latent_width), jnp.bfloat16)],
        compiler_params=pltpu.CompilerParams(vmem_limit_bytes=40 * 2**20),
        cost_estimate=pl.CostEstimate(
            flops=flops, bytes_accessed=3 * 2**20, transcendentals=key_count * row_count
        ),
        name="local_stats",
    )(positions, keys, *query_parts, *cot_parts)

    with jax.named_scope("stats_x"):
        stats = merge(turn_x, [stats] + [ctx_permute(stats, dx=step) for step in range(1, X)])
    with jax.named_scope("stats_y"):
        stats = merge(turn_y, [stats] + [ctx_permute(stats, dy=step) for step in range(1, Y)])
    with jax.named_scope("stats_z"):
        stats = merge(turn_z, [stats, ctx_permute(stats, dz=1)])

    hv_rows, pair = pl.pallas_call(
        functools.partial(grads_kernel, latent_width, slab),
        out_shape=(
            jax.ShapeDtypeStruct((full_width, key_count), jnp.float32),
            jax.ShapeDtypeStruct((2, latent_width), jnp.float32),
        ),
        in_specs=smem + in_vmem(6 + X + Y),
        out_specs=(pl.BlockSpec(memory_space=pltpu.VMEM),) * 2,
        scratch_shapes=[pltpu.VMEM((row_count, latent_width), jnp.bfloat16)],
        compiler_params=pltpu.CompilerParams(vmem_limit_bytes=40 * 2**20),
        cost_estimate=pl.CostEstimate(
            flops=2 * flops, bytes_accessed=4 * 2**20, transcendentals=key_count * row_count
        ),
        name="gradients",
    )(
        positions,
        keys,
        stats,
        rows,
        tangent,
        norm_gain[None],
        gain_tangent[None],
        *query_parts,
        *cot_parts,
    )

    with jax.named_scope("pair_core"):
        pair = ring_sum([pair, all_permute(pair, dc=1)])
    with jax.named_scope("pair_z"):
        pair = ring_sum([pair] + [all_permute(pair, dz=step) for step in range(1, Z)])
    with jax.named_scope("pair_y"):
        pair = ring_sum([pair] + [all_permute(pair, dy=step) for step in range(1, Y)])
    with jax.named_scope("pair_x"):
        pair = ring_sum([pair] + [all_permute(pair, dx=step) for step in range(1, X)])
    return (hv_rows.T[None], pair)


def solution(mesh):
    in_specs = (
        P("dp"),
        P("dp"),
        P("dp", None, "ctx", None),
        P("dp", None, "ctx", None),
        P("dp", "ctx", None),
        P("dp", "ctx", None),
        P(),
        P(),
    )
    out_specs = (P("dp", "ctx", None), P())
    return jax.shard_map(shards, mesh=mesh, in_specs=in_specs, out_specs=out_specs, check_vma=False)
```

time: 1050 us -> 263 us (0.25)
  the two profiles are of different devices: /device:TPU:1 before, /device:TPU:24 now
where the time goes in v1:
time: 263 us; the launch traced here: 261 us
  starting transfers between devices  207 us (79%)
  waiting for transfers between devices  35.3 us (13%)
  Pallas kernels  9.64 us (4%)
  local copies, waits for them, and re-layouts  5.3 us (2%)
  between operations  2.89 us (1%)
    ppermute x33, starting transfers between devices, ctx_permute(): return lax.ppermute(value, 'ctx', ctx_shift(dx, dy, dz))  138 us
    ppermute x18, starting transfers between devices, all_permute(): return lax.ppermute(value, ('dp', 'ctx'), all_shift(dx, dy, dz, dc))  68.7 us
    ppermute x33, waiting for transfers between devices, ctx_permute(): return lax.ppermute(value, 'ctx', ctx_shift(dx, dy, dz))  20.2 us
    ppermute x18, waiting for transfers between devices, all_permute(): return lax.ppermute(value, ('dp', 'ctx'), all_shift(dx, dy, dz, dc))  15.1 us
    unnamed x50, local copies, waits for them, and re-layouts  5.28 us
  transfers between devices with their start and end apart: 51, of which 14 were waited for; matrix products, arithmetic and copies ran while one was open for 1% of the time, Pallas kernels for 0%

profile of v1, /device:TPU:24, one launch (start us, length us, event | category | flops | bytes accessed | tf_op | source)
XLA Modules:
  0.0 260.8 jit_solution(14335452774656540706)
XLA Ops:
  0.6 10.9 %collective-permute-start.11 = (bf16[16,512]{1,0:T(8,128)(2,1)}, bf16[16,512]{1,0:T(8,128)(2,1)S(1)}, u32[]{:S(2)}, u32[]{:S(2)}) collective-permute-start(bf16[16,512]{1,0:T(8,128)(2,1)} %bitcast.24), channel_id=1, source_target_pairs={{0,1},{1,0},{2,3},{3,2},{4,5},{5,4},{6,7},{7,6},{8,9},{9,8},{10,11... | collective-permute-start | bytes 49160 | tf_op jit(solution)/shard_map/gather_z/ppermute | solution.py:47
  16.2 4.7 %collective-permute-start.14 = (bf16[32,512]{1,0:T(8,128)(2,1)S(1)}, bf16[32,512]{1,0:T(8,128)(2,1)S(1)}, u32[]{:S(2)}, u32[]{:S(2)}) collective-permute-start(bf16[32,512]{1,0:T(8,128)(2,1)S(1)} %pad_maximum_fusion.1), channel_id=1, source_target_pairs={{0,48},{1,49},{2,50},{3,51},{4,52},{5,53},{6,54},{7,55},{8,56},{9,... | collective-permute-start | bytes 98312 | tf_op jit(solution)/shard_map/gather_mid/ppermute | solution.py:47
  20.9 2.7 %collective-permute-start.13 = (bf16[32,512]{1,0:T(8,128)(2,1)S(1)}, bf16[32,512]{1,0:T(8,128)(2,1)S(1)}, u32[]{:S(2)}, u32[]{:S(2)}) collective-permute-start(bf16[32,512]{1,0:T(8,128)(2,1)S(1)} %pad_maximum_fusion.1), channel_id=1, source_target_pairs={{0,32},{1,33},{2,34},{3,35},{4,36},{5,37},{6,38},{7,39},{8,40},{9,... | collective-permute-start | bytes 98312 | tf_op jit(solution)/shard_map/gather_mid/ppermute | solution.py:47
  23.6 2.8 %collective-permute-start.12 = (bf16[32,512]{1,0:T(8,128)(2,1)S(1)}, bf16[32,512]{1,0:T(8,128)(2,1)S(1)}, u32[]{:S(2)}, u32[]{:S(2)}) collective-permute-start(bf16[32,512]{1,0:T(8,128)(2,1)S(1)} %pad_maximum_fusion.1), channel_id=1, source_target_pairs={{0,16},{1,17},{2,18},{3,19},{4,20},{5,21},{6,22},{7,23},{8,24},{9,... | collective-permute-start | bytes 98312 | tf_op jit(solution)/shard_map/gather_mid/ppermute | solution.py:47
  31.1 6.9 %collective-permute-start.5 = (bf16[32,576]{1,0:T(8,128)(2,1)S(1)}, bf16[32,576]{1,0:T(8,128)(2,1)S(1)}, u32[]{:S(2)}, u32[]{:S(2)}) collective-permute-start(bf16[32,576]{1,0:T(8,128)(2,1)S(1)} %pad_maximum_fusion), channel_id=1, source_target_pairs={{0,10},{1,11},{2,12},{3,13},{4,14},{5,15},{6,0},{7,1},{8,2},{9,3},... | collective-permute-start | bytes 110600 | tf_op jit(solution)/shard_map/gather_mid/ppermute | solution.py:47
  38.1 2.9 %collective-permute-start.4 = (bf16[32,576]{1,0:T(8,128)(2,1)S(1)}, bf16[32,576]{1,0:T(8,128)(2,1)S(1)}, u32[]{:S(2)}, u32[]{:S(2)}) collective-permute-start(bf16[32,576]{1,0:T(8,128)(2,1)S(1)} %pad_maximum_fusion), channel_id=1, source_target_pairs={{0,8},{1,9},{2,10},{3,11},{4,12},{5,13},{6,14},{7,15},{8,0},{9,1},... | collective-permute-start | bytes 110600 | tf_op jit(solution)/shard_map/gather_mid/ppermute | solution.py:47
  41.0 4.7 %collective-permute-start.1 = (bf16[32,576]{1,0:T(8,128)(2,1)S(1)}, bf16[32,576]{1,0:T(8,128)(2,1)S(1)}, u32[]{:S(2)}, u32[]{:S(2)}) collective-permute-start(bf16[32,576]{1,0:T(8,128)(2,1)S(1)} %pad_maximum_fusion), channel_id=1, source_target_pairs={{0,2},{1,3},{2,4},{3,5},{4,6},{5,7},{6,8},{7,9},{8,10},{9,11},{10,... | collective-permute-start | bytes 110600 | tf_op jit(solution)/shard_map/gather_mid/ppermute | solution.py:47
  47.4 5.2 %collective-permute-start.2 = (bf16[32,576]{1,0:T(8,128)(2,1)S(1)}, bf16[32,576]{1,0:T(8,128)(2,1)S(1)}, u32[]{:S(2)}, u32[]{:S(2)}) collective-permute-start(bf16[32,576]{1,0:T(8,128)(2,1)S(1)} %pad_maximum_fusion), channel_id=1, source_target_pairs={{0,4},{1,5},{2,6},{3,7},{4,8},{5,9},{6,10},{7,11},{8,12},{9,13},{1... | collective-permute-start | bytes 110600 | tf_op jit(solution)/shard_map/gather_mid/ppermute | solution.py:47
  54.3 6.1 %collective-permute-start.3 = (bf16[32,576]{1,0:T(8,128)(2,1)S(1)}, bf16[32,576]{1,0:T(8,128)(2,1)S(1)}, u32[]{:S(2)}, u32[]{:S(2)}) collective-permute-start(bf16[32,576]{1,0:T(8,128)(2,1)S(1)} %pad_maximum_fusion), channel_id=1, source_target_pairs={{0,6},{1,7},{2,8},{3,9},{4,10},{5,11},{6,12},{7,13},{8,14},{9,15},... | collective-permute-start | bytes 110600 | tf_op jit(solution)/shard_map/gather_mid/ppermute | solution.py:47
  60.4 3.8 %collective-permute-done.3 = bf16[32,576]{1,0:T(8,128)(2,1)S(1)} collective-permute-done((bf16[32,576]{1,0:T(8,128)(2,1)S(1)}, bf16[32,576]{1,0:T(8,128)(2,1)S(1)}, u32[]{:S(2)}, u32[]{:S(2)}) %collective-permute-start.3) | collective-permute-done | bytes 36896 | tf_op jit(solution)/shard_map/gather_mid/ppermute | solution.py:47
  64.2 3.3 %collective-permute-start.21 = (bf16[128,512]{1,0:T(8,128)(2,1)S(1)}, bf16[128,512]{1,0:T(8,128)(2,1)S(1)}, u32[]{:S(2)}, u32[]{:S(2)}) collective-permute-start(bf16[128,512]{1,0:T(8,128)(2,1)S(1)} %constant_dynamic-update-slice_fusion.9.refs_6_.refs_11_), channel_id=1, source_target_pairs={{0,14},{1,15},{2,0},{3,1},{4,2},{5,3},{6,4},{7,5},{8,6},{9,7},{10,... | collective-permute-start | bytes 393224 | tf_op jit(solution)/shard_map/gather_last/ppermute | solution.py:47
  67.6 6.0 %collective-permute-start.20 = (bf16[128,512]{1,0:T(8,128)(2,1)S(1)}, bf16[128,512]{1,0:T(8,128)(2,1)S(1)}, u32[]{:S(2)}, u32[]{:S(2)}) collective-permute-start(bf16[128,512]{1,0:T(8,128)(2,1)S(1)} %constant_dynamic-update-slice_fusion.9.refs_6_.refs_11_), channel_id=1, source_target_pairs={{0,12},{1,13},{2,14},{3,15},{4,0},{5,1},{6,2},{7,3},{8,4},{9,5},{1... | collective-permute-start | bytes 393224 | tf_op jit(solution)/shard_map/gather_last/ppermute | solution.py:47
  73.6 3.2 %collective-permute-start.19 = (bf16[128,512]{1,0:T(8,128)(2,1)S(1)}, bf16[128,512]{1,0:T(8,128)(2,1)S(1)}, u32[]{:S(2)}, u32[]{:S(2)}) collective-permute-start(bf16[128,512]{1,0:T(8,128)(2,1)S(1)} %constant_dynamic-update-slice_fusion.9.refs_6_.refs_11_), channel_id=1, source_target_pairs={{0,10},{1,11},{2,12},{3,13},{4,14},{5,15},{6,0},{7,1},{8,2},{9,3},... | collective-permute-start | bytes 393224 | tf_op jit(solution)/shard_map/gather_last/ppermute | solution.py:47
  76.8 4.6 %collective-permute-start.18 = (bf16[128,512]{1,0:T(8,128)(2,1)S(1)}, bf16[128,512]{1,0:T(8,128)(2,1)S(1)}, u32[]{:S(2)}, u32[]{:S(2)}) collective-permute-start(bf16[128,512]{1,0:T(8,128)(2,1)S(1)} %constant_dynamic-update-slice_fusion.9.refs_6_.refs_11_), channel_id=1, source_target_pairs={{0,8},{1,9},{2,10},{3,11},{4,12},{5,13},{6,14},{7,15},{8,0},{9,1},... | collective-permute-start | bytes 393224 | tf_op jit(solution)/shard_map/gather_last/ppermute | solution.py:47
  81.4 5.3 %collective-permute-start.17 = (bf16[128,512]{1,0:T(8,128)(2,1)S(1)}, bf16[128,512]{1,0:T(8,128)(2,1)S(1)}, u32[]{:S(2)}, u32[]{:S(2)}) collective-permute-start(bf16[128,512]{1,0:T(8,128)(2,1)S(1)} %constant_dynamic-update-slice_fusion.9.refs_6_.refs_11_), channel_id=1, source_target_pairs={{0,6},{1,7},{2,8},{3,9},{4,10},{5,11},{6,12},{7,13},{8,14},{9,15},... | collective-permute-start | bytes 393224 | tf_op jit(solution)/shard_map/gather_last/ppermute | solution.py:47
  86.7 4.3 %collective-permute-start.10 = (bf16[256,576]{1,0:T(8,128)(2,1)S(1)}, bf16[256,576]{1,0:T(8,128)(2,1)S(1)}, u32[]{:S(2)}, u32[]{:S(2)}) collective-permute-start(bf16[256,576]{1,0:T(8,128)(2,1)S(1)} %constant_dynamic-update-slice_fusion.refs_2_.refs_7_), channel_id=1, source_target_pairs={{0,48},{1,49},{2,50},{3,51},{4,52},{5,53},{6,54},{7,55},{8,56},{9,... | collective-permute-start | bytes 884744 | tf_op jit(solution)/shard_map/gather_last/ppermute | solution.py:47
  91.0 3.4 %collective-permute-start.9 = (bf16[256,576]{1,0:T(8,128)(2,1)S(1)}, bf16[256,576]{1,0:T(8,128)(2,1)S(1)}, u32[]{:S(2)}, u32[]{:S(2)}) collective-permute-start(bf16[256,576]{1,0:T(8,128)(2,1)S(1)} %constant_dynamic-update-slice_fusion.refs_2_.refs_7_), channel_id=1, source_target_pairs={{0,32},{1,33},{2,34},{3,35},{4,36},{5,37},{6,38},{7,39},{8,40},{9,... | collective-permute-start | bytes 884744 | tf_op jit(solution)/shard_map/gather_last/ppermute | solution.py:47
  97.9 3.2 %collective-permute-start.16 = (bf16[128,512]{1,0:T(8,128)(2,1)S(1)}, bf16[128,512]{1,0:T(8,128)(2,1)S(1)}, u32[]{:S(2)}, u32[]{:S(2)}) collective-permute-start(bf16[128,512]{1,0:T(8,128)(2,1)S(1)} %constant_dynamic-update-slice_fusion.9.refs_6_.refs_11_), channel_id=1, source_target_pairs={{0,4},{1,5},{2,6},{3,7},{4,8},{5,9},{6,10},{7,11},{8,12},{9,13},{1... | collective-permute-start | bytes 393224 | tf_op jit(solution)/shard_map/gather_last/ppermute | solution.py:47
  101.1 3.4 %collective-permute-start.15 = (bf16[128,512]{1,0:T(8,128)(2,1)S(1)}, bf16[128,512]{1,0:T(8,128)(2,1)S(1)}, u32[]{:S(2)}, u32[]{:S(2)}) collective-permute-start(bf16[128,512]{1,0:T(8,128)(2,1)S(1)} %constant_dynamic-update-slice_fusion.9.refs_6_.refs_11_), channel_id=1, source_target_pairs={{0,2},{1,3},{2,4},{3,5},{4,6},{5,7},{6,8},{7,9},{8,10},{9,11},{10,... | collective-permute-start | bytes 393224 | tf_op jit(solution)/shard_map/gather_last/ppermute | solution.py:47
  109.6 5.1 %collective-permute-start.24 = (f32[8,1024]{1,0:T(8,128)S(1)}, f32[8,1024]{1,0:T(8,128)S(1)}, u32[]{:S(2)}, u32[]{:S(2)}) collective-permute-start(f32[8,1024]{1,0:T(8,128)S(1)} %local_stats.1.refs_0_), channel_id=1, source_target_pairs={{0,48},{1,49},{2,50},{3,51},{4,52},{5,53},{6,54},{7,55},{8,56},{9,... | collective-permute-start | bytes 98312 | tf_op jit(solution)/shard_map/stats_x/ppermute | solution.py:47
  114.7 2.7 %collective-permute-start.23 = (f32[8,1024]{1,0:T(8,128)S(1)}, f32[8,1024]{1,0:T(8,128)S(1)}, u32[]{:S(2)}, u32[]{:S(2)}) collective-permute-start(f32[8,1024]{1,0:T(8,128)S(1)} %local_stats.1.refs_0_), channel_id=1, source_target_pairs={{0,32},{1,33},{2,34},{3,35},{4,36},{5,37},{6,38},{7,39},{8,40},{9,... | collective-permute-start | bytes 98312 | tf_op jit(solution)/shard_map/stats_x/ppermute | solution.py:47
  119.5 2.6 collective-permute-done.23.refs_2_
  126.5 2.5 collective-permute-start.31
  129.0 4.1 %collective-permute-start.30 = (f32[8,1024]{1,0:T(8,128)}, f32[8,1024]{1,0:T(8,128)S(1)}, u32[]{:S(2)}, u32[]{:S(2)}) collective-permute-start(f32[8,1024]{1,0:T(8,128)} %merge_stats.3.refs_0_), channel_id=1, source_target_pairs={{0,12},{1,13},{2,14},{3,15},{4,0},{5,1},{6,2},{7,3},{8,4},{9,5},{1... | collective-permute-start | bytes 98312 | tf_op jit(solution)/shard_map/stats_y/ppermute | solution.py:47
  133.2 5.0 %collective-permute-start.29 = (f32[8,1024]{1,0:T(8,128)}, f32[8,1024]{1,0:T(8,128)S(1)}, u32[]{:S(2)}, u32[]{:S(2)}) collective-permute-start(f32[8,1024]{1,0:T(8,128)} %merge_stats.3.refs_0_), channel_id=1, source_target_pairs={{0,10},{1,11},{2,12},{3,13},{4,14},{5,15},{6,0},{7,1},{8,2},{9,3},... | collective-permute-start | bytes 98312 | tf_op jit(solution)/shard_map/stats_y/ppermute | solution.py:47
  138.2 4.3 %collective-permute-start.28 = (f32[8,1024]{1,0:T(8,128)}, f32[8,1024]{1,0:T(8,128)S(1)}, u32[]{:S(2)}, u32[]{:S(2)}) collective-permute-start(f32[8,1024]{1,0:T(8,128)} %merge_stats.3.refs_0_), channel_id=1, source_target_pairs={{0,8},{1,9},{2,10},{3,11},{4,12},{5,13},{6,14},{7,15},{8,0},{9,1},... | collective-permute-start | bytes 98312 | tf_op jit(solution)/shard_map/stats_y/ppermute | solution.py:47
  142.5 5.1 %collective-permute-start.27 = (f32[8,1024]{1,0:T(8,128)}, f32[8,1024]{1,0:T(8,128)S(1)}, u32[]{:S(2)}, u32[]{:S(2)}) collective-permute-start(f32[8,1024]{1,0:T(8,128)} %merge_stats.3.refs_0_), channel_id=1, source_target_pairs={{0,6},{1,7},{2,8},{3,9},{4,10},{5,11},{6,12},{7,13},{8,14},{9,15},... | collective-permute-start | bytes 98312 | tf_op jit(solution)/shard_map/stats_y/ppermute | solution.py:47
  147.7 3.7 %collective-permute-start.26 = (f32[8,1024]{1,0:T(8,128)}, f32[8,1024]{1,0:T(8,128)S(1)}, u32[]{:S(2)}, u32[]{:S(2)}) collective-permute-start(f32[8,1024]{1,0:T(8,128)} %merge_stats.3.refs_0_), channel_id=1, source_target_pairs={{0,4},{1,5},{2,6},{3,7},{4,8},{5,9},{6,10},{7,11},{8,12},{9,13},{1... | collective-permute-start | bytes 98312 | tf_op jit(solution)/shard_map/stats_y/ppermute | solution.py:47
  151.4 3.4 %collective-permute-start.25 = (f32[8,1024]{1,0:T(8,128)}, f32[8,1024]{1,0:T(8,128)S(1)}, u32[]{:S(2)}, u32[]{:S(2)}) collective-permute-start(f32[8,1024]{1,0:T(8,128)} %merge_stats.3.refs_0_), channel_id=1, source_target_pairs={{0,2},{1,3},{2,4},{3,5},{4,6},{5,7},{6,8},{7,9},{8,10},{9,11},{10,... | collective-permute-start | bytes 98312 | tf_op jit(solution)/shard_map/stats_y/ppermute | solution.py:47
  154.9 2.5 collective-permute-done.25.refs_1_
  159.7 7.9 %collective-permute-start.32 = (f32[8,1024]{1,0:T(8,128)}, f32[8,1024]{1,0:T(8,128)S(1)}, u32[]{:S(2)}, u32[]{:S(2)}) collective-permute-start(f32[8,1024]{1,0:T(8,128)} %merge_stats.4.refs_0_), channel_id=1, source_target_pairs={{0,1},{1,0},{2,3},{3,2},{4,5},{5,4},{6,7},{7,6},{8,9},{9,8},{10,11... | collective-permute-start | bytes 98312 | tf_op jit(solution)/shard_map/stats_z/ppermute | solution.py:47
  172.6 3.5 %gradients.1 = (f32[576,128]{1,0:T(8,128)}, f32[2,512]{1,0:T(2,128)S(1)}) custom-call(s32[3]{0:T(128)S(1)} %pad_add_fusion.refs_0_, bf16[256,576]{1,0:T(8,128)(2,1)S(1)} %maximum_maximum_fusion.refs_1_, f32[8,1024]{1,0:T(8,128)S(1)} %copy-done.1, bf16[128,576]{1,0:T(8,128)(2,1)S(1)} %bitcast.15, bf16[128,576]{1,0:T(8,128)(2,1)S(1)} %bitcast.19, ...), custom_call_target="tpu_custom_call" | custom-call | flops 1140850688 | bytes 4194304 | tf_op jit(solution)/shard_map/gradients/pallas_call | solution.py:311
  179.2 7.8 %collective-permute-start.40 = (f32[2,512]{1,0:T(2,128)S(1)}, f32[2,512]{1,0:T(2,128)S(1)}, u32[]{:S(2)}, u32[]{:S(2)}) collective-permute-start(f32[2,512]{1,0:T(2,128)S(1)} %add.78), channel_id=1, source_target_pairs={{0,385},{64,449},{128,0},{192,64},{256,128},{320,192},{384,256},{4... | collective-permute-start | bytes 12296 | tf_op jit(solution)/shard_map/pair_z/ppermute | solution.py:51
  188.9 6.9 %collective-permute-start.38 = (f32[2,512]{1,0:T(2,128)S(1)}, f32[2,512]{1,0:T(2,128)S(1)}, u32[]{:S(2)}, u32[]{:S(2)}) collective-permute-start(f32[2,512]{1,0:T(2,128)S(1)} %add.78), channel_id=1, source_target_pairs={{0,129},{64,193},{128,257},{192,321},{256,385},{320,449},{384,0},{... | collective-permute-start | bytes 12296 | tf_op jit(solution)/shard_map/pair_z/ppermute | solution.py:51
  197.8 3.0 %collective-permute-start.36 = (f32[2,512]{1,0:T(2,128)S(1)}, f32[2,512]{1,0:T(2,128)S(1)}, u32[]{:S(2)}, u32[]{:S(2)}) collective-permute-start(f32[2,512]{1,0:T(2,128)S(1)} %add.78), channel_id=1, source_target_pairs={{0,257},{64,321},{128,385},{192,449},{256,0},{320,64},{384,128},{4... | collective-permute-start | bytes 12296 | tf_op jit(solution)/shard_map/pair_z/ppermute | solution.py:51
  200.8 3.7 %collective-permute-start.35 = (f32[2,512]{1,0:T(2,128)S(1)}, f32[2,512]{1,0:T(2,128)S(1)}, u32[]{:S(2)}, u32[]{:S(2)}) collective-permute-start(f32[2,512]{1,0:T(2,128)S(1)} %add.78), channel_id=1, source_target_pairs={{0,256},{64,320},{128,384},{192,448},{256,1},{320,65},{384,129},{4... | collective-permute-start | bytes 12296 | tf_op jit(solution)/shard_map/pair_z/ppermute | solution.py:51
  204.6 4.1 %collective-permute-start.34 = (f32[2,512]{1,0:T(2,128)S(1)}, f32[2,512]{1,0:T(2,128)S(1)}, u32[]{:S(2)}, u32[]{:S(2)}) collective-permute-start(f32[2,512]{1,0:T(2,128)S(1)} %add.78), channel_id=1, source_target_pairs={{0,1},{64,65},{128,129},{192,193},{256,257},{320,321},{384,385},{4... | collective-permute-start | bytes 12296 | tf_op jit(solution)/shard_map/pair_z/ppermute | solution.py:51
  208.8 5.2 %collective-permute-done.34 = f32[2,512]{1,0:T(2,128)S(1)} collective-permute-done((f32[2,512]{1,0:T(2,128)S(1)}, f32[2,512]{1,0:T(2,128)S(1)}, u32[]{:S(2)}, u32[]{:S(2)}) %collective-permute-start.34) | collective-permute-done | bytes 4128 | tf_op jit(solution)/shard_map/pair_z/ppermute | solution.py:51
  214.0 2.4 collective-permute-start.47
  216.4 3.9 %collective-permute-start.46 = (f32[2,512]{1,0:T(2,128)S(1)}, f32[2,512]{1,0:T(2,128)S(1)}, u32[]{:S(2)}, u32[]{:S(2)}) collective-permute-start(f32[2,512]{1,0:T(2,128)S(1)} %add_add_fusion.2), channel_id=1, source_target_pairs={{0,6},{64,70},{128,134},{192,198},{256,262},{320,326},{384,390},{4... | collective-permute-start | bytes 12296 | tf_op jit(solution)/shard_map/pair_y/ppermute | solution.py:51
  220.3 3.8 %collective-permute-start.45 = (f32[2,512]{1,0:T(2,128)S(1)}, f32[2,512]{1,0:T(2,128)S(1)}, u32[]{:S(2)}, u32[]{:S(2)}) collective-permute-start(f32[2,512]{1,0:T(2,128)S(1)} %add_add_fusion.2), channel_id=1, source_target_pairs={{0,10},{64,74},{128,138},{192,202},{256,266},{320,330},{384,394},{... | collective-permute-start | bytes 12296 | tf_op jit(solution)/shard_map/pair_y/ppermute | solution.py:51
  224.1 5.8 %collective-permute-start.44 = (f32[2,512]{1,0:T(2,128)S(1)}, f32[2,512]{1,0:T(2,128)S(1)}, u32[]{:S(2)}, u32[]{:S(2)}) collective-permute-start(f32[2,512]{1,0:T(2,128)S(1)} %add_add_fusion.2), channel_id=1, source_target_pairs={{0,2},{64,66},{128,130},{192,194},{256,258},{320,322},{384,386},{4... | collective-permute-start | bytes 12296 | tf_op jit(solution)/shard_map/pair_y/ppermute | solution.py:51
  231.9 6.0 %collective-permute-start.42 = (f32[2,512]{1,0:T(2,128)S(1)}, f32[2,512]{1,0:T(2,128)S(1)}, u32[]{:S(2)}, u32[]{:S(2)}) collective-permute-start(f32[2,512]{1,0:T(2,128)S(1)} %add_add_fusion.2), channel_id=1, source_target_pairs={{0,4},{64,68},{128,132},{192,196},{256,260},{320,324},{384,388},{4... | collective-permute-start | bytes 12296 | tf_op jit(solution)/shard_map/pair_y/ppermute | solution.py:51
  237.9 4.2 %collective-permute-start.41 = (f32[2,512]{1,0:T(2,128)S(1)}, f32[2,512]{1,0:T(2,128)S(1)}, u32[]{:S(2)}, u32[]{:S(2)}) collective-permute-start(f32[2,512]{1,0:T(2,128)S(1)} %add_add_fusion.2), channel_id=1, source_target_pairs={{0,8},{64,72},{128,136},{192,200},{256,264},{320,328},{384,392},{4... | collective-permute-start | bytes 12296 | tf_op jit(solution)/shard_map/pair_y/ppermute | solution.py:51
  242.2 5.1 %collective-permute-done.41 = f32[2,512]{1,0:T(2,128)S(1)} collective-permute-done((f32[2,512]{1,0:T(2,128)S(1)}, f32[2,512]{1,0:T(2,128)S(1)}, u32[]{:S(2)}, u32[]{:S(2)}) %collective-permute-start.41) | collective-permute-done | bytes 4128 | tf_op jit(solution)/shard_map/pair_y/ppermute | solution.py:51
  249.3 3.9 %collective-permute-start.49 = (f32[2,512]{1,0:T(2,128)S(1)}, f32[2,512]{1,0:T(2,128)S(1)}, u32[]{:S(2)}, u32[]{:S(2)}) collective-permute-start(f32[2,512]{1,0:T(2,128)S(1)} %add_add_fusion.1), channel_id=1, source_target_pairs={{0,16},{64,80},{128,144},{192,208},{256,272},{320,336},{384,400},{... | collective-permute-start | bytes 12296 | tf_op jit(solution)/shard_map/pair_x/ppermute | solution.py:51
  253.2 3.4 %collective-permute-start.48 = (f32[2,512]{1,0:T(2,128)S(1)}, f32[2,512]{1,0:T(2,128)S(1)}, u32[]{:S(2)}, u32[]{:S(2)}) collective-permute-start(f32[2,512]{1,0:T(2,128)S(1)} %add_add_fusion.1), channel_id=1, source_target_pairs={{0,32},{64,96},{128,160},{192,224},{256,288},{320,352},{384,416},{... | collective-permute-start | bytes 12296 | tf_op jit(solution)/shard_map/pair_x/ppermute | solution.py:51
  256.6 3.5 %collective-permute-done.48 = f32[2,512]{1,0:T(2,128)S(1)} collective-permute-done((f32[2,512]{1,0:T(2,128)S(1)}, f32[2,512]{1,0:T(2,128)S(1)}, u32[]{:S(2)}, u32[]{:S(2)}) %collective-permute-start.48) | collective-permute-done | bytes 4128 | tf_op jit(solution)/shard_map/pair_x/ppermute | solution.py:51
  (124 shorter events, 45.1 us)
Async XLA Ops:
  0.6 15.0 %collective-permute-start.11 = (bf16[16,512]{1,0:T(8,128)(2,1)}, bf16[16,512]{1,0:T(8,128)(2,1)S(1)}, u32[]{:S(2)}, u32[]{:S(2)}) collective-permute-start(bf16[16,512]{1,0:T(8,128)(2,1)} %bitcast.24), channel_id=1, source_target_pairs={{0,1},{1,0},{2,3},{3,2},{4,5},{5,4},{6,7},{7,6},{8,9},{9,8},{10,11... | collective-permute-start | bytes 49160 | tf_op jit(solution)/shard_map/gather_z/ppermute | solution.py:47
  11.6 14.9 %collective-permute-start = (bf16[16,576]{1,0:T(8,128)(2,1)}, bf16[16,576]{1,0:T(8,128)(2,1)S(1)}, u32[]{:S(2)}, u32[]{:S(2)}) collective-permute-start(bf16[16,576]{1,0:T(8,128)(2,1)} %bitcast.22), channel_id=1, source_target_pairs={{0,1},{1,0},{2,3},{3,2},{4,5},{5,4},{6,7},{7,6},{8,9},{9,8},{10,11... | collective-permute-start | bytes 55304 | tf_op jit(solution)/shard_map/gather_z/ppermute | solution.py:47
  16.2 24.8 %collective-permute-start.14 = (bf16[32,512]{1,0:T(8,128)(2,1)S(1)}, bf16[32,512]{1,0:T(8,128)(2,1)S(1)}, u32[]{:S(2)}, u32[]{:S(2)}) collective-permute-start(bf16[32,512]{1,0:T(8,128)(2,1)S(1)} %pad_maximum_fusion.1), channel_id=1, source_target_pairs={{0,48},{1,49},{2,50},{3,51},{4,52},{5,53},{6,54},{7,55},{8,56},{9,... | collective-permute-start | bytes 98312 | tf_op jit(solution)/shard_map/gather_mid/ppermute | solution.py:47
  20.9 17.2 %collective-permute-start.13 = (bf16[32,512]{1,0:T(8,128)(2,1)S(1)}, bf16[32,512]{1,0:T(8,128)(2,1)S(1)}, u32[]{:S(2)}, u32[]{:S(2)}) collective-permute-start(bf16[32,512]{1,0:T(8,128)(2,1)S(1)} %pad_maximum_fusion.1), channel_id=1, source_target_pairs={{0,32},{1,33},{2,34},{3,35},{4,36},{5,37},{6,38},{7,39},{8,40},{9,... | collective-permute-start | bytes 98312 | tf_op jit(solution)/shard_map/gather_mid/ppermute | solution.py:47
  23.6 7.5 %collective-permute-start.12 = (bf16[32,512]{1,0:T(8,128)(2,1)S(1)}, bf16[32,512]{1,0:T(8,128)(2,1)S(1)}, u32[]{:S(2)}, u32[]{:S(2)}) collective-permute-start(bf16[32,512]{1,0:T(8,128)(2,1)S(1)} %pad_maximum_fusion.1), channel_id=1, source_target_pairs={{0,16},{1,17},{2,18},{3,19},{4,20},{5,21},{6,22},{7,23},{8,24},{9,... | collective-permute-start | bytes 98312 | tf_op jit(solution)/shard_map/gather_mid/ppermute | solution.py:47
  26.4 55.0 %collective-permute-start.7 = (bf16[32,576]{1,0:T(8,128)(2,1)S(1)}, bf16[32,576]{1,0:T(8,128)(2,1)S(1)}, u32[]{:S(2)}, u32[]{:S(2)}) collective-permute-start(bf16[32,576]{1,0:T(8,128)(2,1)S(1)} %pad_maximum_fusion), channel_id=1, source_target_pairs={{0,14},{1,15},{2,0},{3,1},{4,2},{5,3},{6,4},{7,5},{8,6},{9,7},{10,... | collective-permute-start | bytes 110600 | tf_op jit(solution)/shard_map/gather_mid/ppermute | solution.py:47
  28.8 48.0 %collective-permute-start.6 = (bf16[32,576]{1,0:T(8,128)(2,1)S(1)}, bf16[32,576]{1,0:T(8,128)(2,1)S(1)}, u32[]{:S(2)}, u32[]{:S(2)}) collective-permute-start(bf16[32,576]{1,0:T(8,128)(2,1)S(1)} %pad_maximum_fusion), channel_id=1, source_target_pairs={{0,12},{1,13},{2,14},{3,15},{4,0},{5,1},{6,2},{7,3},{8,4},{9,5},{1... | collective-permute-start | bytes 110600 | tf_op jit(solution)/shard_map/gather_mid/ppermute | solution.py:47
  31.1 42.5 %collective-permute-start.5 = (bf16[32,576]{1,0:T(8,128)(2,1)S(1)}, bf16[32,576]{1,0:T(8,128)(2,1)S(1)}, u32[]{:S(2)}, u32[]{:S(2)}) collective-permute-start(bf16[32,576]{1,0:T(8,128)(2,1)S(1)} %pad_maximum_fusion), channel_id=1, source_target_pairs={{0,10},{1,11},{2,12},{3,13},{4,14},{5,15},{6,0},{7,1},{8,2},{9,3},... | collective-permute-start | bytes 110600 | tf_op jit(solution)/shard_map/gather_mid/ppermute | solution.py:47
  38.1 29.5 %collective-permute-start.4 = (bf16[32,576]{1,0:T(8,128)(2,1)S(1)}, bf16[32,576]{1,0:T(8,128)(2,1)S(1)}, u32[]{:S(2)}, u32[]{:S(2)}) collective-permute-start(bf16[32,576]{1,0:T(8,128)(2,1)S(1)} %pad_maximum_fusion), channel_id=1, source_target_pairs={{0,8},{1,9},{2,10},{3,11},{4,12},{5,13},{6,14},{7,15},{8,0},{9,1},... | collective-permute-start | bytes 110600 | tf_op jit(solution)/shard_map/gather_mid/ppermute | solution.py:47
  47.4 6.9 %collective-permute-start.2 = (bf16[32,576]{1,0:T(8,128)(2,1)S(1)}, bf16[32,576]{1,0:T(8,128)(2,1)S(1)}, u32[]{:S(2)}, u32[]{:S(2)}) collective-permute-start(bf16[32,576]{1,0:T(8,128)(2,1)S(1)} %pad_maximum_fusion), channel_id=1, source_target_pairs={{0,4},{1,5},{2,6},{3,7},{4,8},{5,9},{6,10},{7,11},{8,12},{9,13},{1... | collective-permute-start | bytes 110600 | tf_op jit(solution)/shard_map/gather_mid/ppermute | solution.py:47
  54.3 10.0 %collective-permute-start.3 = (bf16[32,576]{1,0:T(8,128)(2,1)S(1)}, bf16[32,576]{1,0:T(8,128)(2,1)S(1)}, u32[]{:S(2)}, u32[]{:S(2)}) collective-permute-start(bf16[32,576]{1,0:T(8,128)(2,1)S(1)} %pad_maximum_fusion), channel_id=1, source_target_pairs={{0,6},{1,7},{2,8},{3,9},{4,10},{5,11},{6,12},{7,13},{8,14},{9,15},... | collective-permute-start | bytes 110600 | tf_op jit(solution)/shard_map/gather_mid/ppermute | solution.py:47
  64.2 22.5 %collective-permute-start.21 = (bf16[128,512]{1,0:T(8,128)(2,1)S(1)}, bf16[128,512]{1,0:T(8,128)(2,1)S(1)}, u32[]{:S(2)}, u32[]{:S(2)}) collective-permute-start(bf16[128,512]{1,0:T(8,128)(2,1)S(1)} %constant_dynamic-update-slice_fusion.9.refs_6_.refs_11_), channel_id=1, source_target_pairs={{0,14},{1,15},{2,0},{3,1},{4,2},{5,3},{6,4},{7,5},{8,6},{9,7},{10,... | collective-permute-start | bytes 393224 | tf_op jit(solution)/shard_map/gather_last/ppermute | solution.py:47
  67.6 23.4 %collective-permute-start.20 = (bf16[128,512]{1,0:T(8,128)(2,1)S(1)}, bf16[128,512]{1,0:T(8,128)(2,1)S(1)}, u32[]{:S(2)}, u32[]{:S(2)}) collective-permute-start(bf16[128,512]{1,0:T(8,128)(2,1)S(1)} %constant_dynamic-update-slice_fusion.9.refs_6_.refs_11_), channel_id=1, source_target_pairs={{0,12},{1,13},{2,14},{3,15},{4,0},{5,1},{6,2},{7,3},{8,4},{9,5},{1... | collective-permute-start | bytes 393224 | tf_op jit(solution)/shard_map/gather_last/ppermute | solution.py:47
  73.6 20.9 %collective-permute-start.19 = (bf16[128,512]{1,0:T(8,128)(2,1)S(1)}, bf16[128,512]{1,0:T(8,128)(2,1)S(1)}, u32[]{:S(2)}, u32[]{:S(2)}) collective-permute-start(bf16[128,512]{1,0:T(8,128)(2,1)S(1)} %constant_dynamic-update-slice_fusion.9.refs_6_.refs_11_), channel_id=1, source_target_pairs={{0,10},{1,11},{2,12},{3,13},{4,14},{5,15},{6,0},{7,1},{8,2},{9,3},... | collective-permute-start | bytes 393224 | tf_op jit(solution)/shard_map/gather_last/ppermute | solution.py:47
  76.8 21.1 %collective-permute-start.18 = (bf16[128,512]{1,0:T(8,128)(2,1)S(1)}, bf16[128,512]{1,0:T(8,128)(2,1)S(1)}, u32[]{:S(2)}, u32[]{:S(2)}) collective-permute-start(bf16[128,512]{1,0:T(8,128)(2,1)S(1)} %constant_dynamic-update-slice_fusion.9.refs_6_.refs_11_), channel_id=1, source_target_pairs={{0,8},{1,9},{2,10},{3,11},{4,12},{5,13},{6,14},{7,15},{8,0},{9,1},... | collective-permute-start | bytes 393224 | tf_op jit(solution)/shard_map/gather_last/ppermute | solution.py:47
  81.4 19.7 %collective-permute-start.17 = (bf16[128,512]{1,0:T(8,128)(2,1)S(1)}, bf16[128,512]{1,0:T(8,128)(2,1)S(1)}, u32[]{:S(2)}, u32[]{:S(2)}) collective-permute-start(bf16[128,512]{1,0:T(8,128)(2,1)S(1)} %constant_dynamic-update-slice_fusion.9.refs_6_.refs_11_), channel_id=1, source_target_pairs={{0,6},{1,7},{2,8},{3,9},{4,10},{5,11},{6,12},{7,13},{8,14},{9,15},... | collective-permute-start | bytes 393224 | tf_op jit(solution)/shard_map/gather_last/ppermute | solution.py:47
  86.7 21.3 %collective-permute-start.10 = (bf16[256,576]{1,0:T(8,128)(2,1)S(1)}, bf16[256,576]{1,0:T(8,128)(2,1)S(1)}, u32[]{:S(2)}, u32[]{:S(2)}) collective-permute-start(bf16[256,576]{1,0:T(8,128)(2,1)S(1)} %constant_dynamic-update-slice_fusion.refs_2_.refs_7_), channel_id=1, source_target_pairs={{0,48},{1,49},{2,50},{3,51},{4,52},{5,53},{6,54},{7,55},{8,56},{9,... | collective-permute-start | bytes 884744 | tf_op jit(solution)/shard_map/gather_last/ppermute | solution.py:47
  91.0 17.0 %collective-permute-start.9 = (bf16[256,576]{1,0:T(8,128)(2,1)S(1)}, bf16[256,576]{1,0:T(8,128)(2,1)S(1)}, u32[]{:S(2)}, u32[]{:S(2)}) collective-permute-start(bf16[256,576]{1,0:T(8,128)(2,1)S(1)} %constant_dynamic-update-slice_fusion.refs_2_.refs_7_), channel_id=1, source_target_pairs={{0,32},{1,33},{2,34},{3,35},{4,36},{5,37},{6,38},{7,39},{8,40},{9,... | collective-permute-start | bytes 884744 | tf_op jit(solution)/shard_map/gather_last/ppermute | solution.py:47
  94.4 13.6 %collective-permute-start.8 = (bf16[256,576]{1,0:T(8,128)(2,1)S(1)}, bf16[256,576]{1,0:T(8,128)(2,1)S(1)}, u32[]{:S(2)}, u32[]{:S(2)}) collective-permute-start(bf16[256,576]{1,0:T(8,128)(2,1)S(1)} %constant_dynamic-update-slice_fusion.refs_2_.refs_7_), channel_id=1, source_target_pairs={{0,16},{1,17},{2,18},{3,19},{4,20},{5,21},{6,22},{7,23},{8,24},{9,... | collective-permute-start | bytes 884744 | tf_op jit(solution)/shard_map/gather_last/ppermute | solution.py:47
  97.9 8.6 %collective-permute-start.16 = (bf16[128,512]{1,0:T(8,128)(2,1)S(1)}, bf16[128,512]{1,0:T(8,128)(2,1)S(1)}, u32[]{:S(2)}, u32[]{:S(2)}) collective-permute-start(bf16[128,512]{1,0:T(8,128)(2,1)S(1)} %constant_dynamic-update-slice_fusion.9.refs_6_.refs_11_), channel_id=1, source_target_pairs={{0,4},{1,5},{2,6},{3,7},{4,8},{5,9},{6,10},{7,11},{8,12},{9,13},{1... | collective-permute-start | bytes 393224 | tf_op jit(solution)/shard_map/gather_last/ppermute | solution.py:47
  101.1 6.9 %collective-permute-start.15 = (bf16[128,512]{1,0:T(8,128)(2,1)S(1)}, bf16[128,512]{1,0:T(8,128)(2,1)S(1)}, u32[]{:S(2)}, u32[]{:S(2)}) collective-permute-start(bf16[128,512]{1,0:T(8,128)(2,1)S(1)} %constant_dynamic-update-slice_fusion.9.refs_6_.refs_11_), channel_id=1, source_target_pairs={{0,2},{1,3},{2,4},{3,5},{4,6},{5,7},{6,8},{7,9},{8,10},{9,11},{10,... | collective-permute-start | bytes 393224 | tf_op jit(solution)/shard_map/gather_last/ppermute | solution.py:47
  109.6 9.8 %collective-permute-start.24 = (f32[8,1024]{1,0:T(8,128)S(1)}, f32[8,1024]{1,0:T(8,128)S(1)}, u32[]{:S(2)}, u32[]{:S(2)}) collective-permute-start(f32[8,1024]{1,0:T(8,128)S(1)} %local_stats.1.refs_0_), channel_id=1, source_target_pairs={{0,48},{1,49},{2,50},{3,51},{4,52},{5,53},{6,54},{7,55},{8,56},{9,... | collective-permute-start | bytes 98312 | tf_op jit(solution)/shard_map/stats_x/ppermute | solution.py:47
  114.7 7.3 %collective-permute-start.23 = (f32[8,1024]{1,0:T(8,128)S(1)}, f32[8,1024]{1,0:T(8,128)S(1)}, u32[]{:S(2)}, u32[]{:S(2)}) collective-permute-start(f32[8,1024]{1,0:T(8,128)S(1)} %local_stats.1.refs_0_), channel_id=1, source_target_pairs={{0,32},{1,33},{2,34},{3,35},{4,36},{5,37},{6,38},{7,39},{8,40},{9,... | collective-permute-start | bytes 98312 | tf_op jit(solution)/shard_map/stats_x/ppermute | solution.py:47
  117.4 7.0 %collective-permute-start.22 = (f32[8,1024]{1,0:T(8,128)S(1)}, f32[8,1024]{1,0:T(8,128)S(1)}, u32[]{:S(2)}, u32[]{:S(2)}) collective-permute-start(f32[8,1024]{1,0:T(8,128)S(1)} %local_stats.1.refs_0_), channel_id=1, source_target_pairs={{0,16},{1,17},{2,18},{3,19},{4,20},{5,21},{6,22},{7,23},{8,24},{9,... | collective-permute-start | bytes 98312 | tf_op jit(solution)/shard_map/stats_x/ppermute | solution.py:47
  126.5 21.1 %collective-permute-start.31 = (f32[8,1024]{1,0:T(8,128)}, f32[8,1024]{1,0:T(8,128)S(1)}, u32[]{:S(2)}, u32[]{:S(2)}) collective-permute-start(f32[8,1024]{1,0:T(8,128)} %merge_stats.3.refs_0_), channel_id=1, source_target_pairs={{0,14},{1,15},{2,0},{3,1},{4,2},{5,3},{6,4},{7,5},{8,6},{9,7},{10,... | collective-permute-start | bytes 98312 | tf_op jit(solution)/shard_map/stats_y/ppermute | solution.py:47
  129.0 22.3 %collective-permute-start.30 = (f32[8,1024]{1,0:T(8,128)}, f32[8,1024]{1,0:T(8,128)S(1)}, u32[]{:S(2)}, u32[]{:S(2)}) collective-permute-start(f32[8,1024]{1,0:T(8,128)} %merge_stats.3.refs_0_), channel_id=1, source_target_pairs={{0,12},{1,13},{2,14},{3,15},{4,0},{5,1},{6,2},{7,3},{8,4},{9,5},{1... | collective-permute-start | bytes 98312 | tf_op jit(solution)/shard_map/stats_y/ppermute | solution.py:47
  133.2 21.6 %collective-permute-start.29 = (f32[8,1024]{1,0:T(8,128)}, f32[8,1024]{1,0:T(8,128)S(1)}, u32[]{:S(2)}, u32[]{:S(2)}) collective-permute-start(f32[8,1024]{1,0:T(8,128)} %merge_stats.3.refs_0_), channel_id=1, source_target_pairs={{0,10},{1,11},{2,12},{3,13},{4,14},{5,15},{6,0},{7,1},{8,2},{9,3},... | collective-permute-start | bytes 98312 | tf_op jit(solution)/shard_map/stats_y/ppermute | solution.py:47
  138.2 16.6 %collective-permute-start.28 = (f32[8,1024]{1,0:T(8,128)}, f32[8,1024]{1,0:T(8,128)S(1)}, u32[]{:S(2)}, u32[]{:S(2)}) collective-permute-start(f32[8,1024]{1,0:T(8,128)} %merge_stats.3.refs_0_), channel_id=1, source_target_pairs={{0,8},{1,9},{2,10},{3,11},{4,12},{5,13},{6,14},{7,15},{8,0},{9,1},... | collective-permute-start | bytes 98312 | tf_op jit(solution)/shard_map/stats_y/ppermute | solution.py:47
  142.5 12.3 %collective-permute-start.27 = (f32[8,1024]{1,0:T(8,128)}, f32[8,1024]{1,0:T(8,128)S(1)}, u32[]{:S(2)}, u32[]{:S(2)}) collective-permute-start(f32[8,1024]{1,0:T(8,128)} %merge_stats.3.refs_0_), channel_id=1, source_target_pairs={{0,6},{1,7},{2,8},{3,9},{4,10},{5,11},{6,12},{7,13},{8,14},{9,15},... | collective-permute-start | bytes 98312 | tf_op jit(solution)/shard_map/stats_y/ppermute | solution.py:47
  147.7 7.3 %collective-permute-start.26 = (f32[8,1024]{1,0:T(8,128)}, f32[8,1024]{1,0:T(8,128)S(1)}, u32[]{:S(2)}, u32[]{:S(2)}) collective-permute-start(f32[8,1024]{1,0:T(8,128)} %merge_stats.3.refs_0_), channel_id=1, source_target_pairs={{0,4},{1,5},{2,6},{3,7},{4,8},{5,9},{6,10},{7,11},{8,12},{9,13},{1... | collective-permute-start | bytes 98312 | tf_op jit(solution)/shard_map/stats_y/ppermute | solution.py:47
  159.7 10.0 %collective-permute-start.32 = (f32[8,1024]{1,0:T(8,128)}, f32[8,1024]{1,0:T(8,128)S(1)}, u32[]{:S(2)}, u32[]{:S(2)}) collective-permute-start(f32[8,1024]{1,0:T(8,128)} %merge_stats.4.refs_0_), channel_id=1, source_target_pairs={{0,1},{1,0},{2,3},{3,2},{4,5},{5,4},{6,7},{7,6},{8,9},{9,8},{10,11... | collective-permute-start | bytes 98312 | tf_op jit(solution)/shard_map/stats_z/ppermute | solution.py:47
  179.2 21.7 %collective-permute-start.40 = (f32[2,512]{1,0:T(2,128)S(1)}, f32[2,512]{1,0:T(2,128)S(1)}, u32[]{:S(2)}, u32[]{:S(2)}) collective-permute-start(f32[2,512]{1,0:T(2,128)S(1)} %add.78), channel_id=1, source_target_pairs={{0,385},{64,449},{128,0},{192,64},{256,128},{320,192},{384,256},{4... | collective-permute-start | bytes 12296 | tf_op jit(solution)/shard_map/pair_z/ppermute | solution.py:51
  187.0 17.6 %collective-permute-start.39 = (f32[2,512]{1,0:T(2,128)S(1)}, f32[2,512]{1,0:T(2,128)S(1)}, u32[]{:S(2)}, u32[]{:S(2)}) collective-permute-start(f32[2,512]{1,0:T(2,128)S(1)} %add.78), channel_id=1, source_target_pairs={{0,384},{64,448},{128,1},{192,65},{256,129},{320,193},{384,257},{4... | collective-permute-start | bytes 12296 | tf_op jit(solution)/shard_map/pair_z/ppermute | solution.py:51
  188.9 19.8 %collective-permute-start.38 = (f32[2,512]{1,0:T(2,128)S(1)}, f32[2,512]{1,0:T(2,128)S(1)}, u32[]{:S(2)}, u32[]{:S(2)}) collective-permute-start(f32[2,512]{1,0:T(2,128)S(1)} %add.78), channel_id=1, source_target_pairs={{0,129},{64,193},{128,257},{192,321},{256,385},{320,449},{384,0},{... | collective-permute-start | bytes 12296 | tf_op jit(solution)/shard_map/pair_z/ppermute | solution.py:51
  195.8 12.9 %collective-permute-start.37 = (f32[2,512]{1,0:T(2,128)S(1)}, f32[2,512]{1,0:T(2,128)S(1)}, u32[]{:S(2)}, u32[]{:S(2)}) collective-permute-start(f32[2,512]{1,0:T(2,128)S(1)} %add.78), channel_id=1, source_target_pairs={{0,128},{64,192},{128,256},{192,320},{256,384},{320,448},{384,1},{... | collective-permute-start | bytes 12296 | tf_op jit(solution)/shard_map/pair_z/ppermute | solution.py:51
  197.8 11.0 %collective-permute-start.36 = (f32[2,512]{1,0:T(2,128)S(1)}, f32[2,512]{1,0:T(2,128)S(1)}, u32[]{:S(2)}, u32[]{:S(2)}) collective-permute-start(f32[2,512]{1,0:T(2,128)S(1)} %add.78), channel_id=1, source_target_pairs={{0,257},{64,321},{128,385},{192,449},{256,0},{320,64},{384,128},{4... | collective-permute-start | bytes 12296 | tf_op jit(solution)/shard_map/pair_z/ppermute | solution.py:51
  200.8 7.9 %collective-permute-start.35 = (f32[2,512]{1,0:T(2,128)S(1)}, f32[2,512]{1,0:T(2,128)S(1)}, u32[]{:S(2)}, u32[]{:S(2)}) collective-permute-start(f32[2,512]{1,0:T(2,128)S(1)} %add.78), channel_id=1, source_target_pairs={{0,256},{64,320},{128,384},{192,448},{256,1},{320,65},{384,129},{4... | collective-permute-start | bytes 12296 | tf_op jit(solution)/shard_map/pair_z/ppermute | solution.py:51
  204.6 9.4 %collective-permute-start.34 = (f32[2,512]{1,0:T(2,128)S(1)}, f32[2,512]{1,0:T(2,128)S(1)}, u32[]{:S(2)}, u32[]{:S(2)}) collective-permute-start(f32[2,512]{1,0:T(2,128)S(1)} %add.78), channel_id=1, source_target_pairs={{0,1},{64,65},{128,129},{192,193},{256,257},{320,321},{384,385},{4... | collective-permute-start | bytes 12296 | tf_op jit(solution)/shard_map/pair_z/ppermute | solution.py:51
  214.0 17.9 %collective-permute-start.47 = (f32[2,512]{1,0:T(2,128)S(1)}, f32[2,512]{1,0:T(2,128)S(1)}, u32[]{:S(2)}, u32[]{:S(2)}) collective-permute-start(f32[2,512]{1,0:T(2,128)S(1)} %add_add_fusion.2), channel_id=1, source_target_pairs={{0,14},{64,78},{128,142},{192,206},{256,270},{320,334},{384,398},{... | collective-permute-start | bytes 12296 | tf_op jit(solution)/shard_map/pair_y/ppermute | solution.py:51
  216.4 21.5 %collective-permute-start.46 = (f32[2,512]{1,0:T(2,128)S(1)}, f32[2,512]{1,0:T(2,128)S(1)}, u32[]{:S(2)}, u32[]{:S(2)}) collective-permute-start(f32[2,512]{1,0:T(2,128)S(1)} %add_add_fusion.2), channel_id=1, source_target_pairs={{0,6},{64,70},{128,134},{192,198},{256,262},{320,326},{384,390},{4... | collective-permute-start | bytes 12296 | tf_op jit(solution)/shard_map/pair_y/ppermute | solution.py:51
  220.3 21.8 %collective-permute-start.45 = (f32[2,512]{1,0:T(2,128)S(1)}, f32[2,512]{1,0:T(2,128)S(1)}, u32[]{:S(2)}, u32[]{:S(2)}) collective-permute-start(f32[2,512]{1,0:T(2,128)S(1)} %add_add_fusion.2), channel_id=1, source_target_pairs={{0,10},{64,74},{128,138},{192,202},{256,266},{320,330},{384,394},{... | collective-permute-start | bytes 12296 | tf_op jit(solution)/shard_map/pair_y/ppermute | solution.py:51
  224.1 18.1 %collective-permute-start.44 = (f32[2,512]{1,0:T(2,128)S(1)}, f32[2,512]{1,0:T(2,128)S(1)}, u32[]{:S(2)}, u32[]{:S(2)}) collective-permute-start(f32[2,512]{1,0:T(2,128)S(1)} %add_add_fusion.2), channel_id=1, source_target_pairs={{0,2},{64,66},{128,130},{192,194},{256,258},{320,322},{384,386},{4... | collective-permute-start | bytes 12296 | tf_op jit(solution)/shard_map/pair_y/ppermute | solution.py:51
  229.9 12.2 %collective-permute-start.43 = (f32[2,512]{1,0:T(2,128)S(1)}, f32[2,512]{1,0:T(2,128)S(1)}, u32[]{:S(2)}, u32[]{:S(2)}) collective-permute-start(f32[2,512]{1,0:T(2,128)S(1)} %add_add_fusion.2), channel_id=1, source_target_pairs={{0,12},{64,76},{128,140},{192,204},{256,268},{320,332},{384,396},{... | collective-permute-start | bytes 12296 | tf_op jit(solution)/shard_map/pair_y/ppermute | solution.py:51
  231.9 10.3 %collective-permute-start.42 = (f32[2,512]{1,0:T(2,128)S(1)}, f32[2,512]{1,0:T(2,128)S(1)}, u32[]{:S(2)}, u32[]{:S(2)}) collective-permute-start(f32[2,512]{1,0:T(2,128)S(1)} %add_add_fusion.2), channel_id=1, source_target_pairs={{0,4},{64,68},{128,132},{192,196},{256,260},{320,324},{384,388},{4... | collective-permute-start | bytes 12296 | tf_op jit(solution)/shard_map/pair_y/ppermute | solution.py:51
  237.9 9.4 %collective-permute-start.41 = (f32[2,512]{1,0:T(2,128)S(1)}, f32[2,512]{1,0:T(2,128)S(1)}, u32[]{:S(2)}, u32[]{:S(2)}) collective-permute-start(f32[2,512]{1,0:T(2,128)S(1)} %add_add_fusion.2), channel_id=1, source_target_pairs={{0,8},{64,72},{128,136},{192,200},{256,264},{320,328},{384,392},{4... | collective-permute-start | bytes 12296 | tf_op jit(solution)/shard_map/pair_y/ppermute | solution.py:51
  247.3 9.3 %collective-permute-start.50 = (f32[2,512]{1,0:T(2,128)S(1)}, f32[2,512]{1,0:T(2,128)S(1)}, u32[]{:S(2)}, u32[]{:S(2)}) collective-permute-start(f32[2,512]{1,0:T(2,128)S(1)} %add_add_fusion.1), channel_id=1, source_target_pairs={{0,48},{64,112},{128,176},{192,240},{256,304},{320,368},{384,432},... | collective-permute-start | bytes 12296 | tf_op jit(solution)/shard_map/pair_x/ppermute | solution.py:51
  249.3 7.3 %collective-permute-start.49 = (f32[2,512]{1,0:T(2,128)S(1)}, f32[2,512]{1,0:T(2,128)S(1)}, u32[]{:S(2)}, u32[]{:S(2)}) collective-permute-start(f32[2,512]{1,0:T(2,128)S(1)} %add_add_fusion.1), channel_id=1, source_target_pairs={{0,16},{64,80},{128,144},{192,208},{256,272},{320,336},{384,400},{... | collective-permute-start | bytes 12296 | tf_op jit(solution)/shard_map/pair_x/ppermute | solution.py:51
  253.2 7.0 %collective-permute-start.48 = (f32[2,512]{1,0:T(2,128)S(1)}, f32[2,512]{1,0:T(2,128)S(1)}, u32[]{:S(2)}, u32[]{:S(2)}) collective-permute-start(f32[2,512]{1,0:T(2,128)S(1)} %add_add_fusion.1), channel_id=1, source_target_pairs={{0,32},{64,96},{128,160},{192,224},{256,288},{320,352},{384,416},{... | collective-permute-start | bytes 12296 | tf_op jit(solution)/shard_map/pair_x/ppermute | solution.py:51
  (21 other events, 101.3 us)

commit v2 on v1

v2 whole, which is shorter than its diff:
```python
import functools

import jax
import jax.numpy as jnp
from jax import lax
from jax.experimental import pallas as pl
from jax.experimental.pallas import tpu as pltpu
from jax.sharding import PartitionSpec as P

score_scale = 192.0 ** (-0.5)
tiny_eps = 1e-06
masked_score = -1e30

X, Y, ZH = 4, 8, 2
CTX = X * Y * ZH
LINE = 8


def ctx_index(x, y, zh):
    return (x * Y + y) * ZH + zh


Y_GROUPS = [[ctx_index(x, y, z) for y in range(Y)] for x in range(X) for z in range(ZH)]
XZ_GROUPS = [[ctx_index(x, y, z) for x in range(X) for z in range(ZH)] for y in range(Y)]


def ctx_permute(value, dx=0, dz=0):
    pairs = [
        (ctx_index(x, y, z), ctx_index((x + dx) % X, y, (z + dz) % ZH))
        for x in range(X)
        for y in range(Y)
        for z in range(ZH)
    ]
    return lax.ppermute(value, "ctx", pairs)


def exchange(copies, axis, groups=None):
    return lax.all_to_all(copies, axis, 0, 0, axis_index_groups=groups)


def key_side(kv_rows, kv_tangent, norm_gain, gain_tangent, latent_width):
    latent = kv_rows[:, :latent_width].astype(jnp.float32)
    latent_dot = kv_tangent[:, :latent_width].astype(jnp.float32)
    inv_rms = lax.rsqrt(jnp.mean(latent * latent, axis=-1, keepdims=True) + tiny_eps)
    normed = latent * inv_rms
    inv_dot = -(inv_rms * inv_rms * inv_rms) * jnp.mean(latent * latent_dot, axis=-1, keepdims=True)
    normed_dot = latent_dot * inv_rms + latent * inv_dot
    return (latent, latent_dot, inv_rms, inv_dot, normed, normed_dot)


def nt_dot(left, right):
    return lax.dot_general(
        left, right, (((1,), (1,)), ((), ())), preferred_element_type=jnp.float32
    )


def nn_dot(left, right):
    return lax.dot_general(
        left, right, (((1,), (0,)), ((), ())), preferred_element_type=jnp.float32
    )


def pair_kernel(place_ref, own_ref, other_ref, out_ref):
    z = place_ref[1]
    for copy in range(LINE):
        out_ref[copy, z] = own_ref[...]
        out_ref[copy, 1 - z] = other_ref[...]


def query_blocks(block_refs):
    own, *halves = block_refs
    blocks = [own[...]]
    for first, second in zip(halves[::2], halves[1::2]):
        blocks.append(jnp.concatenate([first[...], second[...]], axis=0))
    return blocks


def merge_sums(parts):
    maxima = jnp.max(parts[..., 0:1, :], axis=0)
    total = jnp.sum(jnp.exp(parts[..., 0:1, :] - maxima[None]) * parts, axis=0)
    row = lax.broadcasted_iota(jnp.int32, total.shape, total.ndim - 2)
    return jnp.where(row == 0, maxima, total)


def block_terms(place_ref, keys, block, latent_width, slab):
    key_count = keys.shape[0] // 2
    row_count = block.shape[0]
    cot_blk, query_blk = block[:, :latent_width], block[:, latent_width:]
    offset, live_count, key_base = place_ref[2], place_ref[3], place_ref[4]
    by_query = score_scale * nt_dot(keys, query_blk)
    by_cot = nt_dot(keys[:, :latent_width], cot_blk)
    slab_row = lax.broadcasted_iota(jnp.int32, (key_count, row_count), 1) % slab
    key_pos = key_base + lax.broadcasted_iota(jnp.int32, (key_count, row_count), 0)
    visible = key_pos <= offset + slab_row
    live = slab_row < live_count
    return (
        by_query[:key_count],
        by_query[key_count:],
        jnp.where(live, by_cot[:key_count], 0.0),
        jnp.where(live, by_cot[key_count:], 0.0),
        visible,
        live,
    )


def stats_kernel(latent_width, slab, place_ref, keys_ref, *refs):
    *block_refs, sums_ref = refs
    keys = keys_ref[...]
    for behind, block in enumerate(query_blocks(block_refs)):
        scores, score_dot, value_grad, value_dot, visible, _ = block_terms(
            place_ref, keys, block, latent_width, slab
        )
        maxima = jnp.max(jnp.where(visible, scores, masked_score), axis=0, keepdims=True)
        weights = jnp.where(visible, jnp.exp(scores - maxima), 0.0)
        weighted = weights * score_dot
        rows = [
            maxima,
            jnp.sum(weights, axis=0, keepdims=True),
            jnp.sum(weighted, axis=0, keepdims=True),
            jnp.sum(weights * value_grad, axis=0, keepdims=True),
            jnp.sum(weighted * value_grad, axis=0, keepdims=True),
            jnp.sum(weights * value_dot, axis=0, keepdims=True),
            jnp.zeros((2, block.shape[0]), jnp.float32),
        ]
        sums = jnp.concatenate(rows, axis=0)
        at = lax.rem(place_ref[0] + (X - behind), X)
        for copy in range(LINE):
            sums_ref[copy, at] = sums


def merge_kernel(parts_ref, out_ref):
    merged = merge_sums(parts_ref[...])
    for copy in range(LINE):
        out_ref[copy] = merged


def add_kernel(parts_ref, out_ref):
    total = jnp.sum(parts_ref[...], axis=0)
    for copy in range(LINE):
        out_ref[copy] = total


def grads_kernel(latent_width, slab, place_ref, keys_ref, parts_ref, *refs):
    rows_ref, tangent_ref, gain_ref, gain_tangent_ref, *block_refs = refs[:-3]
    hv_ref, pair_ref, sums_ref = refs[-3:]
    sums_ref[...] = merge_sums(parts_ref[...])
    keys = keys_ref[...]
    key_count = keys.shape[0] // 2
    by_query = jnp.zeros(keys.shape, jnp.float32)
    by_cot = jnp.zeros((keys.shape[0], latent_width), jnp.float32)
    for behind, block in enumerate(query_blocks(block_refs)):
        scores, score_dot, value_grad, value_dot, visible, live = block_terms(
            place_ref, keys, block, latent_width, slab
        )
        stats = sums_ref[lax.rem(place_ref[0] + (X - behind), X)]
        maxima, totals = stats[0:1], stats[1:2]
        moment_a, moment_b, moment_c, moment_e = stats[2:3], stats[3:4], stats[4:5], stats[5:6]
        inv_totals = 1.0 / totals
        shift_mean = moment_a * inv_totals
        grad_mean = moment_b * inv_totals
        grad_mean_dot = (moment_c - shift_mean * moment_b + moment_e) * inv_totals
        attention = jnp.where(visible, jnp.exp(scores - maxima), 0.0) * inv_totals
        attention_dot = attention * (score_dot - shift_mean)
        centred = value_grad - grad_mean
        score_grad = attention * centred
        score_grad_dot = attention_dot * centred + attention * (value_dot - grad_mean_dot)
        left = jnp.concatenate([score_grad, score_grad_dot], axis=0).astype(jnp.bfloat16)
        by_query = by_query + nn_dot(left, block[:, latent_width:])
        live_left = jnp.concatenate(
            [jnp.where(live, attention, 0.0), jnp.where(live, attention_dot, 0.0)], axis=0
        ).astype(jnp.bfloat16)
        by_cot = by_cot + nn_dot(live_left, block[:, :latent_width])
    by_query = score_scale * by_query
    latent_grad = by_query[:key_count, :latent_width] + by_cot[:key_count]
    latent_grad_dot = by_query[key_count:, :latent_width] + by_cot[key_count:]
    norm_gain, gain_tangent = gain_ref[...], gain_tangent_ref[...]
    latent, latent_dot, inv_rms, inv_dot, normed, normed_dot = key_side(
        rows_ref[...], tangent_ref[...], norm_gain, gain_tangent, latent_width
    )
    pair = jnp.concatenate(
        [
            jnp.sum(latent_grad * normed, axis=0, keepdims=True),
            jnp.sum(latent_grad_dot * normed + latent_grad * normed_dot, axis=0, keepdims=True),
        ],
        axis=0,
    )
    for copy in range(LINE):
        pair_ref[copy] = pair
    normed_grad = latent_grad * norm_gain
    normed_grad_dot = latent_grad_dot * norm_gain + latent_grad * gain_tangent
    inner_grad = jnp.mean(normed_grad * latent, axis=-1, keepdims=True)
    inner_grad_dot = jnp.mean(
        normed_grad_dot * latent + normed_grad * latent_dot, axis=-1, keepdims=True
    )
    rms_cubed = inv_rms * inv_rms * inv_rms
    rms_cubed_dot = 3.0 * inv_rms * inv_rms * inv_dot
    row_dot = (
        inv_dot * normed_grad
        + inv_rms * normed_grad_dot
        - (rms_cubed_dot * inner_grad + rms_cubed * inner_grad_dot) * latent
        - (rms_cubed * inner_grad) * latent_dot
    )
    hv_ref[:latent_width, :] = row_dot.T
    hv_ref[latent_width:, :] = by_query[key_count:, latent_width:].T


def in_vmem(count):
    return [pl.BlockSpec(memory_space=pltpu.VMEM)] * count


def shards(offsets, lengths, queries, cotangent, kv_rows, kv_tangent, norm_gain, gain_tangent):
    latent_width = norm_gain.shape[0]
    slab, full_width = queries.shape[1], queries.shape[3]
    key_count = kv_rows.shape[1]
    row_count = slab * CTX

    packed_width = latent_width + full_width
    smem = [pl.BlockSpec(memory_space=pltpu.SMEM)]
    ctx_at = lax.axis_index("ctx").astype(jnp.int32)
    place = jnp.stack(
        [
            ctx_at // (Y * ZH),
            ctx_at % ZH,
            offsets[0],
            lengths[0] - offsets[0],
            ctx_at * key_count,
        ]
    )

    packed = jnp.concatenate(
        [cotangent.reshape(slab, latent_width), queries.reshape(slab, full_width)], axis=1
    )
    with jax.named_scope("gather_z"):
        copies = pl.pallas_call(
            pair_kernel,
            out_shape=jax.ShapeDtypeStruct((LINE, ZH, slab, packed_width), packed.dtype),
            in_specs=smem + in_vmem(2),
            out_specs=pl.BlockSpec(memory_space=pltpu.VMEM),
            name="pair_rows",
        )(place, packed, ctx_permute(packed, dz=1))
    with jax.named_scope("gather_y"):
        block = exchange(copies, "ctx", Y_GROUPS).reshape(Y * ZH * slab, packed_width)
    with jax.named_scope("gather_x"):
        half = block.shape[0] // 2
        first, second = block[:half], block[half:]
        behind_first, ahead_second = ctx_permute(first, dx=1), ctx_permute(second, dx=-1)
        behind_second, ahead_first = ctx_permute(second, dx=1), ctx_permute(first, dx=-1)
        far_first, far_second = ctx_permute(behind_first, dx=1), ctx_permute(ahead_second, dx=-1)
        blocks = (
            block,
            behind_first,
            behind_second,
            far_first,
            far_second,
            ahead_first,
            ahead_second,
        )

    rows, tangent = kv_rows[0], kv_tangent[0]
    normed, normed_dot = key_side(rows, tangent, norm_gain, gain_tangent, latent_width)[4:]
    keys = jnp.concatenate(
        [
            jnp.concatenate([normed * norm_gain, rows[:, latent_width:].astype(jnp.float32)], 1),
            jnp.concatenate(
                [
                    gain_tangent * normed + norm_gain * normed_dot,
                    tangent[:, latent_width:].astype(jnp.float32),
                ],
                1,
            ),
        ],
        axis=0,
    ).astype(jnp.bfloat16)
    flops = 4 * key_count * row_count * (full_width + latent_width)

    sums_shape = jax.ShapeDtypeStruct((LINE, X, 8, Y * ZH * slab), jnp.float32)
    sums = pl.pallas_call(
        functools.partial(stats_kernel, latent_width, slab),
        out_shape=sums_shape,
        in_specs=smem + in_vmem(1 + len(blocks)),
        out_specs=pl.BlockSpec(memory_space=pltpu.VMEM),
        compiler_params=pltpu.CompilerParams(vmem_limit_bytes=40 * 2**20),
        cost_estimate=pl.CostEstimate(
            flops=flops, bytes_accessed=3 * 2**20, transcendentals=key_count * row_count
        ),
        name="local_stats",
    )(place, keys, *blocks)
    with jax.named_scope("stats_y"):
        sums = exchange(sums, "ctx", Y_GROUPS)
        sums = pl.pallas_call(merge_kernel, out_shape=sums_shape, name="merge_stats")(sums)
    with jax.named_scope("stats_xz"):
        sums = exchange(sums, "ctx", XZ_GROUPS)

    pair_shape = jax.ShapeDtypeStruct((LINE, 2, latent_width), jnp.float32)
    hv_rows, pair = pl.pallas_call(
        functools.partial(grads_kernel, latent_width, slab),
        out_shape=(jax.ShapeDtypeStruct((full_width, key_count), jnp.float32), pair_shape),
        in_specs=smem + in_vmem(6 + len(blocks)),
        out_specs=(pl.BlockSpec(memory_space=pltpu.VMEM),) * 2,
        scratch_shapes=[pltpu.VMEM(sums_shape.shape[1:], jnp.float32)],
        compiler_params=pltpu.CompilerParams(vmem_limit_bytes=40 * 2**20),
        cost_estimate=pl.CostEstimate(
            flops=2 * flops, bytes_accessed=4 * 2**20, transcendentals=key_count * row_count
        ),
        name="gradients",
    )(place, keys, sums, rows, tangent, norm_gain[None], gain_tangent[None], *blocks)

    add_copies = pl.pallas_call(add_kernel, out_shape=pair_shape, name="add_pair")
    with jax.named_scope("pair_dp"):
        pair = add_copies(exchange(pair, "dp"))
    with jax.named_scope("pair_y"):
        pair = add_copies(exchange(pair, "ctx", Y_GROUPS))
    with jax.named_scope("pair_xz"):
        pair = jnp.sum(exchange(pair, "ctx", XZ_GROUPS), axis=0)
    return (hv_rows.T[None], pair)


def solution(mesh):
    in_specs = (
        P("dp"),
        P("dp"),
        P("dp", None, "ctx", None),
        P("dp", None, "ctx", None),
        P("dp", "ctx", None),
        P("dp", "ctx", None),
        P(),
        P(),
    )
    out_specs = (P("dp", "ctx", None), P())
    return jax.shard_map(shards, mesh=mesh, in_specs=in_specs, out_specs=out_specs, check_vma=False)
```

time: 263 us -> 147 us (0.56)
  the two profiles are of different devices: /device:TPU:24 before, /device:TPU:1 now
where the time goes in v2:
time: 147 us; the launch traced here: 146 us
  blocking collectives  65.5 us (45%)
  starting transfers between devices  36.7 us (25%)
  waiting for transfers between devices  25.9 us (18%)
  Pallas kernels  11.2 us (8%)
  local copies, waits for them, and re-layouts  2.38 us (2%)
  between operations  2.13 us (1%)
  other arithmetic  1.7 us (1%)
    all_to_all x5, blocking collectives, exchange(): return lax.all_to_all(copies, axis, 0, 0, axis_index_groups=groups)  65.5 us
    ppermute x7, starting transfers between devices, ctx_permute(): return lax.ppermute(value, 'ctx', pairs)  29.7 us
    all_to_all x1, waiting for transfers between devices, exchange(): return lax.all_to_all(copies, axis, 0, 0, axis_index_groups=groups)  18.2 us
    ppermute x7, waiting for transfers between devices, ctx_permute(): return lax.ppermute(value, 'ctx', pairs)  7.67 us
    all_to_all x1, starting transfers between devices, exchange(): return lax.all_to_all(copies, axis, 0, 0, axis_index_groups=groups)  6.95 us
    pallas_call x1, Pallas kernels, shards(): pl.pallas_call(functools.partial(grads_kernel, latent_width, slab), out_s...  3.5 us
  transfers between devices with their start and end apart: 8, of which 4 were waited for; matrix products, arithmetic and copies ran while one was open for 1% of the time, Pallas kernels for 0%

profile of v2, /device:TPU:1, one launch (start us, length us, event | category | flops | bytes accessed | tf_op | source)
XLA Modules:
  0.0 145.6 jit_solution(5836681448839646300)
XLA Ops:
  0.6 0.7 pad_maximum_fusion.own_ref
  1.4 0.0 copy-start.3
  1.4 11.5 %collective-permute-start = (bf16[16,1088]{1,0:T(8,128)(2,1)S(1)}, bf16[16,1088]{1,0:T(8,128)(2,1)S(1)}, u32[]{:S(2)}, u32[]{:S(2)}) collective-permute-start(bf16[16,1088]{1,0:T(8,128)(2,1)S(1)} %pad_maximum_fusion.own_ref), channel_id=1, source_target_pairs={{0,1},{1,0},{2,3},{3,2},{4,5},{5,4},{6,7},{7,6},{8,9},{9,8},{10,11... | collective-permute-start | bytes 104456 | tf_op jit(solution)/shard_map/gather_z/ppermute | solution.py:34
  14.2 0.6 stack.16.place_ref
  14.8 0.0 collective-permute-done.other_ref
  14.8 0.0 copy-done.3
  14.8 0.0 copy-start.6
  14.8 0.6 copy-done.6
  15.4 1.7 %pair_rows.1 = bf16[8,2,16,1088]{3,2,1,0:T(8,128)(2,1)} custom-call(s32[5]{0:T(128)} %stack.16.place_ref, bf16[16,1088]{1,0:T(8,128)(2,1)} %copy-done.3, bf16[16,1088]{1,0:T(8,128)(2,1)} %copy-done.6), custom_call_target="tpu_custom_call" | custom-call | tf_op jit(solution)/shard_map/gather_z/pair_rows/pallas_call | solution.py:234
  17.1 0.0 copy-start.4
  17.1 7.0 %all-to-all-start = ((bf16[8,2,16,1088]{3,2,1,0:T(8,128)(2,1)}), bf16[8,2,16,1088]{3,2,1,0:T(8,128)(2,1)S(1)}, u32[]{:S(2)}, u32[]{:S(2)}) async-start(bf16[8,2,16,1088]{3,2,1,0:T(8,128)(2,1)} %pair_rows.1), calls=%async_computation | async-start | bytes 1179648 | tf_op jit(solution)/shard_map/gather_y/all_to_all | solution.py:38
  24.0 0.0 copy-done.4
  24.0 0.0 copy-start.5
  24.0 0.2 copy.10
  24.2 0.7 copy-done.5
  24.9 0.2 copy.11
  25.1 18.2 %all-to-all-done = bf16[8,2,16,1088]{3,2,1,0:T(8,128)(2,1)S(1)} async-done(((bf16[8,2,16,1088]{3,2,1,0:T(8,128)(2,1)}), bf16[8,2,16,1088]{3,2,1,0:T(8,128)(2,1)S(1)}, u32[]{:S(2)}, u32[]{:S(2)}) %all-to-all-start) | async-done | bytes 557088 | tf_op jit(solution)/shard_map/gather_y/all_to_all | solution.py:38
  43.4 3.1 %collective-permute-start.1 = (bf16[128,1088]{1,0:T(8,128)(2,1)S(1)}, bf16[128,1088]{1,0:T(8,128)(2,1)S(1)}, u32[]{:S(2)}, u32[]{:S(2)}) collective-permute-start(bf16[128,1088]{1,0:T(8,128)(2,1)S(1)} %bitcast.29), channel_id=1, source_target_pairs={{0,16},{1,17},{2,18},{3,19},{4,20},{5,21},{6,22},{7,23},{8,24},{9,... | collective-permute-start | bytes 835592 | tf_op jit(solution)/shard_map/gather_x/ppermute | solution.py:34
  46.5 3.4 %collective-permute-start.4 = (bf16[128,1088]{1,0:T(8,128)(2,1)S(1)}, bf16[128,1088]{1,0:T(8,128)(2,1)S(1)}, u32[]{:S(2)}, u32[]{:S(2)}) collective-permute-start(bf16[128,1088]{1,0:T(8,128)(2,1)S(1)} %bitcast.27), channel_id=1, source_target_pairs={{0,48},{1,49},{2,50},{3,51},{4,52},{5,53},{6,54},{7,55},{8,56},{9,... | collective-permute-start | bytes 835592 | tf_op jit(solution)/shard_map/gather_x/ppermute | solution.py:34
  49.9 0.1 fusion.7
  50.1 0.0 copy-start.2
  50.1 0.0 copy-start.1
  50.1 3.2 %collective-permute-start.6 = (bf16[128,1088]{1,0:T(8,128)(2,1)S(1)}, bf16[128,1088]{1,0:T(8,128)(2,1)S(1)}, u32[]{:S(2)}, u32[]{:S(2)}) collective-permute-start(bf16[128,1088]{1,0:T(8,128)(2,1)S(1)} %bitcast.30), channel_id=1, source_target_pairs={{0,48},{1,49},{2,50},{3,51},{4,52},{5,53},{6,54},{7,55},{8,56},{9,... | collective-permute-start | bytes 835592 | tf_op jit(solution)/shard_map/gather_x/ppermute | solution.py:34
  53.3 2.1 %collective-permute-start.2 = (bf16[128,1088]{1,0:T(8,128)(2,1)S(1)}, bf16[128,1088]{1,0:T(8,128)(2,1)S(1)}, u32[]{:S(2)}, u32[]{:S(2)}) collective-permute-start(bf16[128,1088]{1,0:T(8,128)(2,1)S(1)} %bitcast.28), channel_id=1, source_target_pairs={{0,16},{1,17},{2,18},{3,19},{4,20},{5,21},{6,22},{7,23},{8,24},{9,... | collective-permute-start | bytes 835592 | tf_op jit(solution)/shard_map/gather_x/ppermute | solution.py:34
  55.4 0.0 collective-permute-done.1.refs_1_.refs_5_
  55.4 1.9 %collective-permute-start.3 = (bf16[128,1088]{1,0:T(8,128)(2,1)S(1)}, bf16[128,1088]{1,0:T(8,128)(2,1)S(1)}, u32[]{:S(2)}, u32[]{:S(2)}) collective-permute-start(bf16[128,1088]{1,0:T(8,128)(2,1)S(1)} %collective-permute-done.1.refs_1_.refs_5_), channel_id=1, source_target_pairs={{0,16},{1,17},{2,18},{3,19},{4,20},{5,21},{6,22},{7,23},{8,24},{9,... | collective-permute-start | bytes 835592 | tf_op jit(solution)/shard_map/gather_x/ppermute | solution.py:34
  57.3 0.0 collective-permute-done.4.refs_6_.refs_10_
  57.3 4.6 %collective-permute-start.5 = (bf16[128,1088]{1,0:T(8,128)(2,1)S(1)}, bf16[128,1088]{1,0:T(8,128)(2,1)S(1)}, u32[]{:S(2)}, u32[]{:S(2)}) collective-permute-start(bf16[128,1088]{1,0:T(8,128)(2,1)S(1)} %collective-permute-done.4.refs_6_.refs_10_), channel_id=1, source_target_pairs={{0,48},{1,49},{2,50},{3,51},{4,52},{5,53},{6,54},{7,55},{8,56},{9,... | collective-permute-start | bytes 835592 | tf_op jit(solution)/shard_map/gather_x/ppermute | solution.py:34
  61.9 0.0 copy-done.2
  61.9 0.0 copy-done.1
  61.9 0.2 fusion.2
  62.2 0.0 copy-start
  62.2 0.3 collective-permute-done.6.refs_5_.refs_9_
  62.4 1.1 collective-permute-done.2.refs_2_.refs_6_
  63.5 6.3 %collective-permute-done.3.refs_3_.refs_7_ = bf16[128,1088]{1,0:T(8,128)(2,1)S(1)} collective-permute-done((bf16[128,1088]{1,0:T(8,128)(2,1)S(1)}, bf16[128,1088]{1,0:T(8,128)(2,1)S(1)}, u32[]{:S(2)}, u32[]{:S(2)}) %collective-permute-start.3) | collective-permute-done | bytes 278560 | tf_op jit(solution)/shard_map/gather_x/ppermute | solution.py:34
  69.8 0.0 collective-permute-done.5.refs_4_.refs_8_
  69.8 0.0 copy-done
  69.8 1.5 %local_stats.1 = f32[8,4,8,256]{3,2,1,0:T(8,128)S(1)} custom-call(s32[5]{0:T(128)S(1)} %copy-done, bf16[256,576]{1,0:T(8,128)(2,1)S(1)} %maximum_maximum_fusion.keys_ref, bf16[256,1088]{1,0:T(8,128)(2,1)S(1)} %bitcast.15, bf16[128,1088]{1,0:T(8,128)(2,1)S(1)} %collective-permute-done.1.refs_1_.refs_5_, ...), custom_call_target="tpu_custom_call" | custom-call | flops 570425344 | bytes 3145728 | tf_op jit(solution)/shard_map/local_stats/pallas_call | solution.py:277
  71.4 12.6 %all_to_all.30.parts_ref = f32[8,4,8,256]{3,2,1,0:T(8,128)} all-to-all(f32[8,4,8,256]{3,2,1,0:T(8,128)S(1)} %local_stats.1), channel_id=1, replica_groups={{0,2,4,6,8,10,12,14},{1,3,5,7,9,11,13,15},{16,18,20,22,24,26,28,30},{17..., dimensions={0} | all-to-all | bytes 524288 | tf_op jit(solution)/shard_map/stats_y/all_to_all | solution.py:38
  83.9 1.7 %merge_stats.1 = f32[8,4,8,256]{3,2,1,0:T(8,128)} custom-call(f32[8,4,8,256]{3,2,1,0:T(8,128)} %all_to_all.30.parts_ref), custom_call_target="tpu_custom_call" | custom-call | tf_op jit(solution)/shard_map/stats_y/merge_stats/pallas_call | solution.py:290
  85.7 13.6 %all_to_all.31.parts_ref = f32[8,4,8,256]{3,2,1,0:T(8,128)S(1)} all-to-all(f32[8,4,8,256]{3,2,1,0:T(8,128)} %merge_stats.1), channel_id=1, replica_groups={{0,1,16,17,32,33,48,49},{2,3,18,19,34,35,50,51},{4,5,20,21,36,37,52,53}..., dimensions={0} | all-to-all | bytes 524288 | tf_op jit(solution)/shard_map/stats_xz/all_to_all | solution.py:38
  99.3 3.5 %gradients.1 = (f32[576,128]{1,0:T(8,128)}, f32[8,2,512]{2,1,0:T(2,128)S(1)}) custom-call(s32[5]{0:T(128)S(1)} %copy-done, bf16[256,576]{1,0:T(8,128)(2,1)S(1)} %maximum_maximum_fusion.keys_ref, f32[8,4,8,256]{3,2,1,0:T(8,128)S(1)} %all_to_all.31.parts_ref, bf16[128,576]{1,0:T(8,128)(2,1)S(1)} %bitcast.20, bf16[128,576]{1,0:T(8,128)(2,1)S(1)} %bitcast.24, ...), custom_call_target="tpu_custom_call" | custom-call | flops 1140850688 | bytes 4194304 | tf_op jit(solution)/shard_map/gradients/pallas_call | solution.py:295
  102.8 16.3 %all_to_all.32.parts_ref = f32[8,2,512]{2,1,0:T(2,128)} all-to-all(f32[8,2,512]{2,1,0:T(2,128)S(1)} %get-tuple-element.5), channel_id=1, replica_groups=mesh['dp'=8,'ctx'=64] {'dp'}, dimensions={0} | all-to-all | bytes 65536 | tf_op jit(solution)/shard_map/pair_dp/all_to_all | solution.py:38
  119.1 1.4 add_pair.2
  120.5 10.8 %all_to_all.33.parts_ref = f32[8,2,512]{2,1,0:T(2,128)} all-to-all(f32[8,2,512]{2,1,0:T(2,128)} %add_pair.2), channel_id=1, replica_groups={{0,2,4,6,8,10,12,14},{1,3,5,7,9,11,13,15},{16,18,20,22,24,26,28,30},{17..., dimensions={0} | all-to-all | bytes 65536 | tf_op jit(solution)/shard_map/pair_y/all_to_all | solution.py:38
  131.3 1.4 add_pair.3
  132.7 12.2 %all_to_all.34 = f32[8,2,512]{2,1,0:T(2,128)S(1)} all-to-all(f32[8,2,512]{2,1,0:T(2,128)} %add_pair.3), channel_id=1, replica_groups={{0,1,16,17,32,33,48,49},{2,3,18,19,34,35,50,51},{4,5,20,21,36,37,52,53}..., dimensions={0} | all-to-all | bytes 65536 | tf_op jit(solution)/shard_map/pair_xz/all_to_all | solution.py:38
  144.9 0.6 reduce_sum.29
  (5 shorter events, 0.1 us)
Async XLA Ops:
  1.4 13.4 %copy-start.3 = (bf16[16,1088]{1,0:T(8,128)(2,1)}, bf16[16,1088]{1,0:T(8,128)(2,1)S(1)}, u32[]{:S(2)}) copy-start(bf16[16,1088]{1,0:T(8,128)(2,1)S(1)} %pad_maximum_fusion.own_ref) | copy-start | bytes 104452
  1.4 13.4 %collective-permute-start = (bf16[16,1088]{1,0:T(8,128)(2,1)S(1)}, bf16[16,1088]{1,0:T(8,128)(2,1)S(1)}, u32[]{:S(2)}, u32[]{:S(2)}) collective-permute-start(bf16[16,1088]{1,0:T(8,128)(2,1)S(1)} %pad_maximum_fusion.own_ref), channel_id=1, source_target_pairs={{0,1},{1,0},{2,3},{3,2},{4,5},{5,4},{6,7},{7,6},{8,9},{9,8},{10,11... | collective-permute-start | bytes 104456 | tf_op jit(solution)/shard_map/gather_z/ppermute | solution.py:34
  14.8 0.6 copy-start.6
  17.1 7.0 %copy-start.4 = (bf16[1,128,576]{1,2,0:T(8,128)(2,1)S(1)}, bf16[1,128,576]{1,2,0:T(8,128)(2,1)}, u32[]{:S(2)}) copy-start(bf16[1,128,576]{1,2,0:T(8,128)(2,1)} %param.12) | copy-start | bytes 442372
  17.1 26.3 %all-to-all-start = ((bf16[8,2,16,1088]{3,2,1,0:T(8,128)(2,1)}), bf16[8,2,16,1088]{3,2,1,0:T(8,128)(2,1)S(1)}, u32[]{:S(2)}, u32[]{:S(2)}) async-start(bf16[8,2,16,1088]{3,2,1,0:T(8,128)(2,1)} %pair_rows.1), calls=%async_computation | async-start | bytes 1179648 | tf_op jit(solution)/shard_map/gather_y/all_to_all | solution.py:38
  24.0 0.9 copy-start.5
  43.4 12.0 %collective-permute-start.1 = (bf16[128,1088]{1,0:T(8,128)(2,1)S(1)}, bf16[128,1088]{1,0:T(8,128)(2,1)S(1)}, u32[]{:S(2)}, u32[]{:S(2)}) collective-permute-start(bf16[128,1088]{1,0:T(8,128)(2,1)S(1)} %bitcast.29), channel_id=1, source_target_pairs={{0,16},{1,17},{2,18},{3,19},{4,20},{5,21},{6,22},{7,23},{8,24},{9,... | collective-permute-start | bytes 835592 | tf_op jit(solution)/shard_map/gather_x/ppermute | solution.py:34
  46.5 10.8 %collective-permute-start.4 = (bf16[128,1088]{1,0:T(8,128)(2,1)S(1)}, bf16[128,1088]{1,0:T(8,128)(2,1)S(1)}, u32[]{:S(2)}, u32[]{:S(2)}) collective-permute-start(bf16[128,1088]{1,0:T(8,128)(2,1)S(1)} %bitcast.27), channel_id=1, source_target_pairs={{0,48},{1,49},{2,50},{3,51},{4,52},{5,53},{6,54},{7,55},{8,56},{9,... | collective-permute-start | bytes 835592 | tf_op jit(solution)/shard_map/gather_x/ppermute | solution.py:34
  50.1 11.9 %copy-start.2 = (f32[512]{0:T(512)S(1)}, f32[512]{0:T(512)}, u32[]{:S(2)}) copy-start(f32[512]{0:T(512)} %param.15) | copy-start | bytes 6148
  50.1 11.9 %copy-start.1 = (f32[512]{0:T(512)S(1)}, f32[512]{0:T(512)}, u32[]{:S(2)}) copy-start(f32[512]{0:T(512)} %param.14) | copy-start | bytes 6148
  50.1 12.3 %collective-permute-start.6 = (bf16[128,1088]{1,0:T(8,128)(2,1)S(1)}, bf16[128,1088]{1,0:T(8,128)(2,1)S(1)}, u32[]{:S(2)}, u32[]{:S(2)}) collective-permute-start(bf16[128,1088]{1,0:T(8,128)(2,1)S(1)} %bitcast.30), channel_id=1, source_target_pairs={{0,48},{1,49},{2,50},{3,51},{4,52},{5,53},{6,54},{7,55},{8,56},{9,... | collective-permute-start | bytes 835592 | tf_op jit(solution)/shard_map/gather_x/ppermute | solution.py:34
  53.3 10.2 %collective-permute-start.2 = (bf16[128,1088]{1,0:T(8,128)(2,1)S(1)}, bf16[128,1088]{1,0:T(8,128)(2,1)S(1)}, u32[]{:S(2)}, u32[]{:S(2)}) collective-permute-start(bf16[128,1088]{1,0:T(8,128)(2,1)S(1)} %bitcast.28), channel_id=1, source_target_pairs={{0,16},{1,17},{2,18},{3,19},{4,20},{5,21},{6,22},{7,23},{8,24},{9,... | collective-permute-start | bytes 835592 | tf_op jit(solution)/shard_map/gather_x/ppermute | solution.py:34
  55.4 14.4 %collective-permute-start.3 = (bf16[128,1088]{1,0:T(8,128)(2,1)S(1)}, bf16[128,1088]{1,0:T(8,128)(2,1)S(1)}, u32[]{:S(2)}, u32[]{:S(2)}) collective-permute-start(bf16[128,1088]{1,0:T(8,128)(2,1)S(1)} %collective-permute-done.1.refs_1_.refs_5_), channel_id=1, source_target_pairs={{0,16},{1,17},{2,18},{3,19},{4,20},{5,21},{6,22},{7,23},{8,24},{9,... | collective-permute-start | bytes 835592 | tf_op jit(solution)/shard_map/gather_x/ppermute | solution.py:34
  57.3 12.5 %collective-permute-start.5 = (bf16[128,1088]{1,0:T(8,128)(2,1)S(1)}, bf16[128,1088]{1,0:T(8,128)(2,1)S(1)}, u32[]{:S(2)}, u32[]{:S(2)}) collective-permute-start(bf16[128,1088]{1,0:T(8,128)(2,1)S(1)} %collective-permute-done.4.refs_6_.refs_10_), channel_id=1, source_target_pairs={{0,48},{1,49},{2,50},{3,51},{4,52},{5,53},{6,54},{7,55},{8,56},{9,... | collective-permute-start | bytes 835592 | tf_op jit(solution)/shard_map/gather_x/ppermute | solution.py:34
  62.2 7.7 %copy-start = (s32[5]{0:T(128)S(1)}, s32[5]{0:T(128)}, u32[]{:S(2)}) copy-start(s32[5]{0:T(128)} %stack.16.place_ref) | copy-start | bytes 64

commit v3 on v2

v3 whole, which is shorter than its diff:
```python
import functools

import jax
import jax.numpy as jnp
from jax import lax
from jax.experimental import pallas as pl
from jax.experimental.pallas import tpu as pltpu
from jax.sharding import PartitionSpec as P

score_scale = 192.0 ** (-0.5)
tiny_eps = 1e-06
masked_score = -1e30

X, Y, ZH = 4, 8, 2
ZL, CORE = 4, 2
CTX = X * Y * ZH
Z = ZH * ZL
LANES = 128
SUBLANES = 8


def ctx_index(x, y, zh):
    return (x * Y + y) * ZH + zh


def device_index(x, y, z, core):
    return (z % ZL * CORE + core) * CTX + ctx_index(x, y, z // ZL)


Y_GROUPS = [[ctx_index(x, y, z) for y in range(Y)] for x in range(X) for z in range(ZH)]
YZ_GROUPS = [[ctx_index(x, y, z) for y in range(Y) for z in range(ZH)] for x in range(X)]
COLUMNS = [
    [device_index(x, y, z, core) for z in range(Z) for core in range(CORE)]
    for x in range(X)
    for y in range(Y)
]
PLANES = [
    [device_index(x, y, z, core) for x in range(X) for y in range(Y)]
    for z in range(Z)
    for core in range(CORE)
]


def ctx_permute(value, dx=0, dz=0):
    pairs = [
        (ctx_index(x, y, z), ctx_index((x + dx) % X, y, (z + dz) % ZH))
        for x in range(X)
        for y in range(Y)
        for z in range(ZH)
    ]
    return lax.ppermute(value, "ctx", pairs)


def exchange(copies, axis, groups=None):
    return lax.all_to_all(copies, axis, 0, 0, axis_index_groups=groups)


def dot(left, right):
    return jnp.dot(left, right, preferred_element_type=jnp.float32)


def pair_kernel(latent_width, place_ref, own_ref, other_ref, out_ref):
    z, live_count = place_ref[1], place_ref[3]
    shape = own_ref.shape
    row = lax.broadcasted_iota(jnp.int32, shape, 0)
    column = lax.broadcasted_iota(jnp.int32, shape, 1)
    kept = (row < live_count) | (column >= latent_width)
    for at, ref in ((z, own_ref), (1 - z, other_ref)):
        rows = jnp.where(kept, ref[...].astype(jnp.float32), 0.0).astype(ref.dtype)
        for copy in range(Y):
            out_ref[copy, at] = rows


def norm_side(block_ref, latent_width):
    full_width = block_ref.shape[0] // 2
    latent = block_ref[:latent_width, :].astype(jnp.float32)
    latent_dot = block_ref[full_width : full_width + latent_width, :].astype(jnp.float32)
    inv_rms = lax.rsqrt(jnp.mean(latent * latent, axis=0, keepdims=True) + tiny_eps)
    normed = latent * inv_rms
    inv_dot = -(inv_rms * inv_rms * inv_rms) * jnp.mean(latent * latent_dot, axis=0, keepdims=True)
    normed_dot = latent_dot * inv_rms + latent * inv_dot
    return (latent, latent_dot, inv_rms, inv_dot, normed, normed_dot)


def keys_kernel(gain_ref, gain_tangent_ref, *refs):
    *block_refs, keys_ref = refs
    latent_width, full_width = gain_ref.shape[0], keys_ref.shape[1]
    norm_gain, gain_tangent = gain_ref[...], gain_tangent_ref[...]
    for at, block_ref in enumerate(block_refs):
        normed, normed_dot = norm_side(block_ref, latent_width)[4:]
        count = block_ref.shape[1]
        keys_ref[at, :latent_width, :count] = (normed * norm_gain).astype(jnp.bfloat16)
        keys_ref[at, :latent_width, count:] = (
            gain_tangent * normed + norm_gain * normed_dot
        ).astype(jnp.bfloat16)
        keys_ref[at, latent_width:, :count] = block_ref[latent_width:full_width, :]
        keys_ref[at, latent_width:, count:] = block_ref[full_width + latent_width :, :]


def block_terms(behind, slab, place_ref, keys_ref, rows_ref):
    row_count, width = rows_ref.shape
    key_count = keys_ref.shape[2] // 2
    latent_width = width - keys_ref.shape[1]
    keys = keys_ref[behind]
    by_query = score_scale * dot(rows_ref[:, latent_width:], keys)
    by_cot = dot(rows_ref[:, :latent_width], keys[:latent_width])
    x = lax.rem(place_ref[0] + (X - behind), X)
    key_pos = (x * (Y * ZH) + place_ref[4]) * key_count
    key_pos += lax.broadcasted_iota(jnp.int32, (row_count, key_count), 1)
    slab_row = lax.broadcasted_iota(jnp.int32, (row_count, key_count), 0) % slab
    visible = key_pos <= place_ref[2] + slab_row
    return (
        by_query[:, :key_count],
        by_query[:, key_count:],
        by_cot[:, :key_count],
        by_cot[:, key_count:],
        visible,
    )


def as_rows(columns):
    shape = (columns[0].shape[0], LANES)
    lane = lax.broadcasted_iota(jnp.int32, shape, 1)
    filled = jnp.zeros(shape, jnp.float32)
    for at, column in enumerate(columns):
        filled = jnp.where(lane == at, column, filled)
    return filled.T[:SUBLANES]


def stats_kernel(slab, place_ref, keys_ref, rows_ref, out_ref):
    terms = [block_terms(behind, slab, place_ref, keys_ref, rows_ref) for behind in range(X)]
    maxima = [jnp.where(visible, scores, masked_score) for scores, _, _, _, visible in terms]
    maxima = jnp.max(functools.reduce(jnp.maximum, maxima), axis=1, keepdims=True)
    sums = [0.0] * 4
    for scores, score_dot, value_grad, value_dot, visible in terms:
        weights = jnp.where(visible, jnp.exp(scores - maxima), 0.0)
        sums[0] += weights
        sums[1] += weights * score_dot
        sums[2] += weights * value_grad
        sums[3] += weights * (score_dot * value_grad + value_dot)
    sums = as_rows([maxima] + [jnp.sum(each, axis=1, keepdims=True) for each in sums])
    for copy in range(out_ref.shape[0]):
        out_ref[copy] = sums


def merged_means(parts_ref):
    count = parts_ref.shape[0]
    maxima = functools.reduce(jnp.maximum, [parts_ref[at, 0:1, :] for at in range(count)])
    sums = sum(jnp.exp(parts_ref[at, 0:1, :] - maxima) * parts_ref[at] for at in range(count))
    inv_totals = 1.0 / sums[1:2]
    shift_mean = sums[2:3] * inv_totals
    grad_mean = sums[3:4] * inv_totals
    grad_mean_dot = (sums[4:5] - shift_mean * sums[3:4]) * inv_totals
    rows = [maxima, inv_totals, shift_mean, grad_mean, grad_mean_dot]
    rows.append(jnp.zeros((LANES - len(rows), maxima.shape[1]), jnp.float32))
    columns = jnp.concatenate(rows, axis=0).T
    return [columns[:, at : at + 1] for at in range(5)]


def grads_kernel(slab, place_ref, parts_ref, keys_ref, rows_ref, turned_ref, *refs):
    gain_ref, gain_tangent_ref, block_refs = refs[0], refs[1], refs[2 : 2 + X]
    share_refs, pair_ref = refs[2 + X : 2 + 2 * X], refs[-1]
    latent_width = gain_ref.shape[0]
    norm_gain, gain_tangent = gain_ref[...], gain_tangent_ref[...]
    maxima, inv_totals, shift_mean, grad_mean, grad_mean_dot = merged_means(parts_ref)
    gain_grad = gain_grad_dot = 0.0
    for behind in range(X):
        scores, score_dot, value_grad, value_dot, visible = block_terms(
            behind, slab, place_ref, keys_ref, rows_ref
        )
        attention = jnp.where(visible, jnp.exp(scores - maxima), 0.0) * inv_totals
        attention_dot = attention * (score_dot - shift_mean)
        centred = value_grad - grad_mean
        score_grad = attention * centred
        score_grad_dot = attention_dot * centred + attention * (value_dot - grad_mean_dot)
        right = jnp.concatenate([score_grad, score_grad_dot], axis=1).astype(jnp.bfloat16)
        by_query = score_scale * dot(turned_ref[latent_width:, :], right)
        right = jnp.concatenate([attention, attention_dot], axis=1).astype(jnp.bfloat16)
        by_cot = dot(turned_ref[:latent_width, :], right)

        key_count = scores.shape[1]
        latent_grad = by_query[:latent_width, :key_count] + by_cot[:, :key_count]
        latent_grad_dot = by_query[:latent_width, key_count:] + by_cot[:, key_count:]
        latent, latent_dot, inv_rms, inv_dot, normed, normed_dot = norm_side(
            block_refs[behind], latent_width
        )
        gain_grad += latent_grad * normed
        gain_grad_dot += latent_grad_dot * normed + latent_grad * normed_dot
        normed_grad = latent_grad * norm_gain
        normed_grad_dot = latent_grad_dot * norm_gain + latent_grad * gain_tangent
        inner_grad = jnp.mean(normed_grad * latent, axis=0, keepdims=True)
        inner_grad_dot = jnp.mean(
            normed_grad_dot * latent + normed_grad * latent_dot, axis=0, keepdims=True
        )
        rms_cubed = inv_rms * inv_rms * inv_rms
        rms_cubed_dot = 3.0 * inv_rms * inv_rms * inv_dot
        share_refs[behind][:latent_width, :] = (
            inv_dot * normed_grad
            + inv_rms * normed_grad_dot
            - (rms_cubed_dot * inner_grad + rms_cubed * inner_grad_dot) * latent
            - (rms_cubed * inner_grad) * latent_dot
        )
        share_refs[behind][latent_width:, :] = by_query[latent_width:, key_count:]
    pair = as_rows([jnp.sum(each, axis=1, keepdims=True) for each in (gain_grad, gain_grad_dot)])
    pair = jnp.concatenate(
        [
            pair[row : row + 1, at : at + LANES]
            for row in range(2)
            for at in range(0, latent_width, LANES)
        ],
        axis=0,
    )
    for copy in range(pair_ref.shape[0]):
        pair_ref[copy] = pair


def add_kernel(parts_ref, out_ref):
    total = jnp.sum(parts_ref[...], axis=0)
    for copy in range(out_ref.shape[0]):
        out_ref[copy] = total


def in_vmem(count):
    return [pl.BlockSpec(memory_space=pltpu.VMEM)] * count


def shards(offsets, lengths, queries, cotangent, kv_rows, kv_tangent, norm_gain, gain_tangent):
    latent_width = norm_gain.shape[0]
    slab, full_width = queries.shape[1], queries.shape[3]
    key_count = kv_rows.shape[1]
    packed_width = latent_width + full_width
    row_count = Y * ZH * slab
    smem = [pl.BlockSpec(memory_space=pltpu.SMEM)]
    limit = pltpu.CompilerParams(vmem_limit_bytes=40 * 2**20)
    flops = 4 * X * key_count * row_count * packed_width
    ctx_at = lax.axis_index("ctx").astype(jnp.int32)
    place = jnp.stack(
        [
            ctx_at // (Y * ZH),
            ctx_at % ZH,
            offsets[0],
            lengths[0] - offsets[0],
            ctx_at % (Y * ZH),
        ]
    )

    packed = jnp.concatenate(
        [cotangent.reshape(slab, latent_width), queries.reshape(slab, full_width)], axis=1
    )
    with jax.named_scope("rows_z"):
        copies = pl.pallas_call(
            functools.partial(pair_kernel, latent_width),
            out_shape=jax.ShapeDtypeStruct((Y, ZH, slab, packed_width), packed.dtype),
            in_specs=smem + in_vmem(2),
            out_specs=pl.BlockSpec(memory_space=pltpu.VMEM),
            name="pair_rows",
        )(place, packed, ctx_permute(packed, dz=1))
    with jax.named_scope("rows_y"):
        block = jnp.concatenate([kv_rows[0].T, kv_tangent[0].T], axis=0)
        block, copies = lax.optimization_barrier((block, copies))
        rows = exchange(copies, "ctx", Y_GROUPS).reshape(row_count, packed_width)

    with jax.named_scope("keys_x"):
        blocks = [block] + [ctx_permute(block, dx=step) for step in range(1, X)]
    gains = (norm_gain[:, None], gain_tangent[:, None])
    keys = pl.pallas_call(
        keys_kernel,
        out_shape=jax.ShapeDtypeStruct((X, full_width, 2 * key_count), jnp.bfloat16),
        in_specs=in_vmem(2 + X),
        out_specs=pl.BlockSpec(memory_space=pltpu.VMEM),
        compiler_params=limit,
        name="make_keys",
    )(*gains, *blocks)

    sums = pl.pallas_call(
        functools.partial(stats_kernel, slab),
        out_shape=jax.ShapeDtypeStruct((Y * ZH, SUBLANES, row_count), jnp.float32),
        in_specs=smem + in_vmem(2),
        out_specs=pl.BlockSpec(memory_space=pltpu.VMEM),
        compiler_params=limit,
        cost_estimate=pl.CostEstimate(
            flops=flops, bytes_accessed=3 * 2**20, transcendentals=X * key_count * row_count
        ),
        name="local_stats",
    )(place, keys, rows)
    with jax.named_scope("stats_yz"):
        sums = exchange(sums, "ctx", YZ_GROUPS)

    *shares, pair = pl.pallas_call(
        functools.partial(grads_kernel, slab),
        out_shape=[jax.ShapeDtypeStruct((full_width, key_count), jnp.float32)] * X
        + [jax.ShapeDtypeStruct((Z * CORE, SUBLANES, LANES), jnp.float32)],
        in_specs=smem + in_vmem(6 + X),
        out_specs=in_vmem(X + 1),
        compiler_params=limit,
        cost_estimate=pl.CostEstimate(
            flops=2 * flops, bytes_accessed=4 * 2**20, transcendentals=X * key_count * row_count
        ),
        name="gradients",
    )(place, sums, keys, rows, rows.T, *gains, *blocks)

    with jax.named_scope("shares_x"):
        hv_rows = sum([ctx_permute(shares[step], dx=-step) for step in range(1, X)], shares[0])
    with jax.named_scope("pair_column"):
        pair = pl.pallas_call(
            add_kernel,
            out_shape=jax.ShapeDtypeStruct((X * Y, SUBLANES, LANES), jnp.float32),
            name="add_pair",
        )(exchange(pair, ("dp", "ctx"), COLUMNS))
    with jax.named_scope("pair_plane"):
        pair = jnp.sum(exchange(pair, ("dp", "ctx"), PLANES), axis=0).reshape(2, latent_width)
    return (hv_rows.T[None], pair)


def solution(mesh):
    in_specs = (
        P("dp"),
        P("dp"),
        P("dp", None, "ctx", None),
        P("dp", None, "ctx", None),
        P("dp", "ctx", None),
        P("dp", "ctx", None),
        P(),
        P(),
    )
    out_specs = (P("dp", "ctx", None), P())
    return jax.shard_map(shards, mesh=mesh, in_specs=in_specs, out_specs=out_specs, check_vma=False)
```

time: 147 us -> 123 us (0.84)
  blocking collectives: 65.5 us -> 15.5 us
  starting transfers between devices: 36.7 us -> 49.8 us
  waiting for transfers between devices: 25.9 us -> 33.1 us
  local copies, waits for them, and re-layouts: 2.38 us -> 6.75 us
  other arithmetic: 1.7 us -> 3.51 us
    all_to_all x5 -> x1, blocking collectives: 65.5 us -> 15.5 us  [exchange(): return lax.all_to_all(copies, axis, 0, 0, axis_index_groups=groups)]
    all_to_all x1 -> x3, starting transfers between devices: 6.95 us -> 21.8 us  [exchange(): return lax.all_to_all(copies, axis, 0, 0, axis_index_groups=groups)]
    ppermute x7, waiting for transfers between devices: 7.67 us -> 13.4 us  [ctx_permute(): return lax.ppermute(value, 'ctx', pairs)]
    unnamed x16 -> x22, local copies, waits for them, and re-layouts: 1.7 us -> 4.95 us
    ppermute x7, starting transfers between devices: 29.7 us -> 28 us  [ctx_permute(): return lax.ppermute(value, 'ctx', pairs)]
    broadcast_in_dim x0 -> x1, other arithmetic: none -> 1.73 us  [shards(): return (hv_rows.T[None], pair)]
    all_to_all x1 -> x3, waiting for transfers between devices: 18.2 us -> 19.8 us  [exchange(): return lax.all_to_all(copies, axis, 0, 0, axis_index_groups=groups)]
    pallas_call x6 -> x5, Pallas kernels: 11.2 us -> 10.9 us  [the longest x1 4.66 us: shards(): pl.pallas_call(functools.partial(grads_kernel, slab), out_shape=[jax.Shap...]
  transfers between devices with their start and end apart: 8 -> 10, of which waited for: 4 -> 5; matrix products, arithmetic and copies ran while one was open for 1% -> 3% of each run, Pallas kernels for 0% -> 2%
where the time goes in v3:
time: 123 us; the launch traced here: 122 us
  starting transfers between devices  49.8 us (40%)
  waiting for transfers between devices  33.1 us (27%)
  blocking collectives  15.5 us (13%)
  Pallas kernels  10.9 us (9%)
  local copies, waits for them, and re-layouts  6.75 us (5%)
  other arithmetic  3.51 us (3%)
  between operations  2.15 us (2%)
    ppermute x7, starting transfers between devices, ctx_permute(): return lax.ppermute(value, 'ctx', pairs)  28 us
    all_to_all x3, starting transfers between devices, exchange(): return lax.all_to_all(copies, axis, 0, 0, axis_index_groups=groups)  21.8 us
    all_to_all x3, waiting for transfers between devices, exchange(): return lax.all_to_all(copies, axis, 0, 0, axis_index_groups=groups)  19.8 us
    all_to_all x1, blocking collectives, exchange(): return lax.all_to_all(copies, axis, 0, 0, axis_index_groups=groups)  15.5 us
    ppermute x7, waiting for transfers between devices, ctx_permute(): return lax.ppermute(value, 'ctx', pairs)  13.4 us
    unnamed x22, local copies, waits for them, and re-layouts  4.95 us
    pallas_call x1, Pallas kernels, shards(): pl.pallas_call(functools.partial(grads_kernel, slab), out_shape=[jax.Shap...  4.66 us
  transfers between devices with their start and end apart: 10, of which 5 were waited for; matrix products, arithmetic and copies ran while one was open for 3% of the time, Pallas kernels for 2%

profile of v3, /device:TPU:1, one launch (start us, length us, event | category | flops | bytes accessed | tf_op | source)
XLA Modules:
  0.0 121.8 jit_solution(17004903893621597194)
XLA Ops:
  0.6 0.7 pad_maximum_fusion.1.own_ref
  1.4 11.5 %collective-permute-start = (bf16[16,1088]{1,0:T(8,128)(2,1)S(1)}, bf16[16,1088]{1,0:T(8,128)(2,1)S(1)}, u32[]{:S(2)}, u32[]{:S(2)}) collective-permute-start(bf16[16,1088]{1,0:T(8,128)(2,1)S(1)} %pad_maximum_fusion.1.own_ref), channel_id=1, source_target_pairs={{0,1},{1,0},{2,3},{3,2},{4,5},{5,4},{6,7},{7,6},{8,9},{9,8},{10,11... | collective-permute-start | bytes 104456 | tf_op jit(solution)/shard_map/rows_z/ppermute | solution.py:51
  12.8 0.0 copy-start.9
  12.9 1.0 pad_maximum_fusion.refs_0_.refs_2_
  13.9 0.0 copy-start.10
  15.2 0.7 stack.16.place_ref
  15.9 0.0 collective-permute-done.other_ref
  15.9 0.0 copy-done.7
  15.9 0.6 copy-done.8
  16.5 1.7 %pair_rows.1 = bf16[8,2,16,1088]{3,2,1,0:T(8,128)(2,1)} custom-call(s32[5]{0:T(128)} %stack.16.place_ref, bf16[16,1088]{1,0:T(8,128)(2,1)} %copy-done.7, bf16[16,1088]{1,0:T(8,128)(2,1)} %copy-done.8), custom_call_target="tpu_custom_call" | custom-call | tf_op jit(solution)/shard_map/rows_z/pair_rows/pallas_call | solution.py:251
  18.2 6.8 %all-to-all-start = ((bf16[8,2,16,1088]{3,2,1,0:T(8,128)(2,1)}), bf16[8,2,16,1088]{3,2,1,0:T(8,128)(2,1)S(1)}, u32[]{:S(2)}, u32[]{:S(2)}) async-start(bf16[8,2,16,1088]{3,2,1,0:T(8,128)(2,1)} %pair_rows.1), calls=%async_computation | async-start | bytes 1179648 | tf_op jit(solution)/shard_map/rows_y/all_to_all | solution.py:55
  25.0 4.4 %collective-permute-start.3 = (bf16[1152,128]{1,0:T(8,128)(2,1)S(1)}, bf16[1152,128]{1,0:T(8,128)(2,1)S(1)}, u32[]{:S(2)}, u32[]{:S(2)}) collective-permute-start(bf16[1152,128]{1,0:T(8,128)(2,1)S(1)} %pad_maximum_fusion.refs_0_.refs_2_), channel_id=1, source_target_pairs={{0,48},{1,49},{2,50},{3,51},{4,52},{5,53},{6,54},{7,55},{8,56},{9,... | collective-permute-start | bytes 884744 | tf_op jit(solution)/shard_map/keys_x/ppermute | solution.py:51
  29.4 2.4 %collective-permute-start.2 = (bf16[1152,128]{1,0:T(8,128)(2,1)S(1)}, bf16[1152,128]{1,0:T(8,128)(2,1)S(1)}, u32[]{:S(2)}, u32[]{:S(2)}) collective-permute-start(bf16[1152,128]{1,0:T(8,128)(2,1)S(1)} %pad_maximum_fusion.refs_0_.refs_2_), channel_id=1, source_target_pairs={{0,32},{1,33},{2,34},{3,35},{4,36},{5,37},{6,38},{7,39},{8,40},{9,... | collective-permute-start | bytes 884744 | tf_op jit(solution)/shard_map/keys_x/ppermute | solution.py:51
  31.8 2.5 %collective-permute-start.1 = (bf16[1152,128]{1,0:T(8,128)(2,1)S(1)}, bf16[1152,128]{1,0:T(8,128)(2,1)S(1)}, u32[]{:S(2)}, u32[]{:S(2)}) collective-permute-start(bf16[1152,128]{1,0:T(8,128)(2,1)S(1)} %pad_maximum_fusion.refs_0_.refs_2_), channel_id=1, source_target_pairs={{0,16},{1,17},{2,18},{3,19},{4,20},{5,21},{6,22},{7,23},{8,24},{9,... | collective-permute-start | bytes 884744 | tf_op jit(solution)/shard_map/keys_x/ppermute | solution.py:51
  34.3 0.0 copy-done.9
  34.3 0.1 copy.13.gain_ref.refs_0_
  34.5 0.0 copy-done.10
  34.5 0.0 copy-start.6
  34.5 0.1 copy.14.gain_tangent_ref.refs_1_
  34.6 0.5 collective-permute-done.3.refs_3_.refs_5_
  35.2 4.6 %collective-permute-done.2.refs_2_.refs_4_ = bf16[1152,128]{1,0:T(8,128)(2,1)S(1)} collective-permute-done((bf16[1152,128]{1,0:T(8,128)(2,1)S(1)}, bf16[1152,128]{1,0:T(8,128)(2,1)S(1)}, u32[]{:S(2)}, u32[]{:S(2)}) %collective-permute-start.2) | collective-permute-done | bytes 294944 | tf_op jit(solution)/shard_map/keys_x/ppermute | solution.py:51
  39.8 8.2 %collective-permute-done.1.refs_1_.refs_3_ = bf16[1152,128]{1,0:T(8,128)(2,1)S(1)} collective-permute-done((bf16[1152,128]{1,0:T(8,128)(2,1)S(1)}, bf16[1152,128]{1,0:T(8,128)(2,1)S(1)}, u32[]{:S(2)}, u32[]{:S(2)}) %collective-permute-start.1) | collective-permute-done | bytes 294944 | tf_op jit(solution)/shard_map/keys_x/ppermute | solution.py:51
  48.0 0.7 copy-done.3
  48.7 1.0 copy-done.4
  49.7 0.7 make_keys.1.keys_ref
  50.4 0.0 copy-done.1
  50.4 0.0 all-to-all-done
  50.4 0.0 copy-done.6
  50.4 2.4 %local_stats.1 = f32[16,8,256]{2,1,0:T(8,128)} custom-call(s32[5]{0:T(128)S(1)} %copy-done.6, bf16[4,576,256]{2,1,0:T(8,128)(2,1)S(1)} %make_keys.1.keys_ref, bf16[256,1088]{1,0:T(8,128)(2,1)S(1)} %bitcast.19), custom_call_target="tpu_custom_call" | custom-call | flops 570425344 | bytes 3145728 | tf_op jit(solution)/shard_map/local_stats/pallas_call | solution.py:275
  52.8 9.4 %all-to-all-start.1 = ((f32[16,8,256]{2,1,0:T(8,128)}), f32[16,8,256]{2,1,0:T(8,128)}, u32[]{:S(2)}, u32[]{:S(2)}) async-start(f32[16,8,256]{2,1,0:T(8,128)} %local_stats.1), calls=%async_computation.1 | async-start | bytes 262144 | tf_op jit(solution)/shard_map/stats_yz/all_to_all | solution.py:55
  62.2 0.2 copy.15
  62.5 12.4 %all-to-all-done.1.parts_ref = f32[16,8,256]{2,1,0:T(8,128)} async-done(((f32[16,8,256]{2,1,0:T(8,128)}), f32[16,8,256]{2,1,0:T(8,128)}, u32[]{:S(2)}, u32[]{:S(2)}) %all-to-all-start.1) | async-done | bytes 131104 | tf_op jit(solution)/shard_map/stats_yz/all_to_all | solution.py:55
  74.9 1.0 copy-done.2
  75.8 1.0 copy-done.5
  76.8 4.7 %gradients.1 = (f32[576,128]{1,0:T(8,128)S(1)}, f32[576,128]{1,0:T(8,128)}, f32[576,128]{1,0:T(8,128)}, f32[576,128]{1,0:T(8,128)}, f32[16,8,128]{2,1,0:T(8,128)S(1)}) custom-call(s32[5]{0:T(128)S(1)} %copy-done.6, f32[16,8,256]{2,1,0:T(8,128)} %all-to-all-done.1.parts_ref, bf16[4,576,256]{2,1,0:T(8,128)(2,1)S(1)} %make_keys.1.keys_ref, ...), custom_call_target="tpu_custom_call" | custom-call | flops 1140850688 | bytes 4194304 | tf_op jit(solution)/shard_map/gradients/pallas_call | solution.py:289
  81.5 0.7 copy-done
  82.2 1.9 %collective-permute-start.4 = (f32[576,128]{1,0:T(8,128)}, f32[576,128]{1,0:T(8,128)S(1)}, u32[]{:S(2)}, u32[]{:S(2)}) collective-permute-start(f32[576,128]{1,0:T(8,128)} %get-tuple-element.12), channel_id=1, source_target_pairs={{0,48},{1,49},{2,50},{3,51},{4,52},{5,53},{6,54},{7,55},{8,56},{9,... | collective-permute-start | bytes 884744 | tf_op jit(solution)/shard_map/shares_x/ppermute | solution.py:51
  84.1 1.9 %collective-permute-start.5 = (f32[576,128]{1,0:T(8,128)}, f32[576,128]{1,0:T(8,128)S(1)}, u32[]{:S(2)}, u32[]{:S(2)}) collective-permute-start(f32[576,128]{1,0:T(8,128)} %get-tuple-element.13), channel_id=1, source_target_pairs={{0,32},{1,33},{2,34},{3,35},{4,36},{5,37},{6,38},{7,39},{8,40},{9,... | collective-permute-start | bytes 884744 | tf_op jit(solution)/shard_map/shares_x/ppermute | solution.py:51
  86.0 3.3 %collective-permute-start.6 = (f32[576,128]{1,0:T(8,128)}, f32[576,128]{1,0:T(8,128)S(1)}, u32[]{:S(2)}, u32[]{:S(2)}) collective-permute-start(f32[576,128]{1,0:T(8,128)} %get-tuple-element.14), channel_id=1, source_target_pairs={{0,16},{1,17},{2,18},{3,19},{4,20},{5,21},{6,22},{7,23},{8,24},{9,... | collective-permute-start | bytes 884744 | tf_op jit(solution)/shard_map/shares_x/ppermute | solution.py:51
  89.4 15.5 %all_to_all.20.parts_ref = f32[16,8,128]{2,1,0:T(8,128)} all-to-all(f32[16,8,128]{2,1,0:T(8,128)S(1)} %get-tuple-element.15), channel_id=1, replica_groups={{0,64,128,192,256,320,384,448,1,65,129,193,257,321,385,449},{2,66,130,1..., dimensions={0} | all-to-all | bytes 131072 | tf_op jit(solution)/shard_map/pair_column/all_to_all | solution.py:55
  104.9 1.5 %add_pair.1 = f32[32,8,128]{2,1,0:T(8,128)} custom-call(f32[16,8,128]{2,1,0:T(8,128)} %all_to_all.20.parts_ref), custom_call_target="tpu_custom_call" | custom-call | tf_op jit(solution)/shard_map/pair_column/add_pair/pallas_call | solution.py:305
  106.4 5.6 %all-to-all-start.3 = ((f32[32,8,128]{2,1,0:T(8,128)}), f32[32,8,128]{2,1,0:T(8,128)S(1)}, u32[]{:S(2)}, u32[]{:S(2)}) async-start(f32[32,8,128]{2,1,0:T(8,128)} %add_pair.1), calls=%async_computation.3 | async-start | bytes 262144 | tf_op jit(solution)/shard_map/pair_plane/all_to_all | solution.py:55
  112.0 0.0 collective-permute-done.4
  112.0 0.0 collective-permute-done.5
  112.0 0.0 collective-permute-done.6
  112.0 1.7 %add_bitcast_fusion = f32[1,128,576]{1,2,0:T(8,128)} fusion(f32[576,128]{1,0:T(8,128)S(1)} %collective-permute-done.6, f32[576,128]{1,0:T(8,128)S(1)} %collective-permute-done.5, f32[576,128]{1,0:T(8,128)} %copy-done, f32[576,128]{1,0:T(8,128)S(1)} %collective-permute-done.4), kind=kLoop, calls=%fused_computation.1 | loop fusion | flops 221184 | bytes 1474560 | tf_op jit(solution)/shard_map/broadcast_in_dim | solution.py:312
  113.8 7.4 %all-to-all-done.3 = f32[32,8,128]{2,1,0:T(8,128)S(1)} async-done(((f32[32,8,128]{2,1,0:T(8,128)}), f32[32,8,128]{2,1,0:T(8,128)S(1)}, u32[]{:S(2)}, u32[]{:S(2)}) %all-to-all-start.3) | async-done | bytes 131104 | tf_op jit(solution)/shard_map/pair_plane/all_to_all | solution.py:55
  121.2 0.6 reshape.21
  (9 shorter events, 0.0 us)
Async XLA Ops:
  1.4 14.5 %copy-start.7 = (bf16[16,1088]{1,0:T(8,128)(2,1)}, bf16[16,1088]{1,0:T(8,128)(2,1)S(1)}, u32[]{:S(2)}) copy-start(bf16[16,1088]{1,0:T(8,128)(2,1)S(1)} %pad_maximum_fusion.1.own_ref) | copy-start | bytes 104452
  1.4 14.5 %collective-permute-start = (bf16[16,1088]{1,0:T(8,128)(2,1)S(1)}, bf16[16,1088]{1,0:T(8,128)(2,1)S(1)}, u32[]{:S(2)}, u32[]{:S(2)}) collective-permute-start(bf16[16,1088]{1,0:T(8,128)(2,1)S(1)} %pad_maximum_fusion.1.own_ref), channel_id=1, source_target_pairs={{0,1},{1,0},{2,3},{3,2},{4,5},{5,4},{6,7},{7,6},{8,9},{9,8},{10,11... | collective-permute-start | bytes 104456 | tf_op jit(solution)/shard_map/rows_z/ppermute | solution.py:51
  12.8 21.5 %copy-start.9 = (f32[512]{0:T(512)S(1)}, f32[512]{0:T(512)}, u32[]{:S(2)}) copy-start(f32[512]{0:T(512)} %param.14) | copy-start | bytes 6148
  13.9 20.6 %copy-start.10 = (f32[512]{0:T(512)S(1)}, f32[512]{0:T(512)}, u32[]{:S(2)}) copy-start(f32[512]{0:T(512)} %param.15) | copy-start | bytes 6148
  15.9 0.6 copy-start.8
  18.2 32.2 %all-to-all-start = ((bf16[8,2,16,1088]{3,2,1,0:T(8,128)(2,1)}), bf16[8,2,16,1088]{3,2,1,0:T(8,128)(2,1)S(1)}, u32[]{:S(2)}, u32[]{:S(2)}) async-start(bf16[8,2,16,1088]{3,2,1,0:T(8,128)(2,1)} %pair_rows.1), calls=%async_computation | async-start | bytes 1179648 | tf_op jit(solution)/shard_map/rows_y/all_to_all | solution.py:55
  25.0 10.2 %collective-permute-start.3 = (bf16[1152,128]{1,0:T(8,128)(2,1)S(1)}, bf16[1152,128]{1,0:T(8,128)(2,1)S(1)}, u32[]{:S(2)}, u32[]{:S(2)}) collective-permute-start(bf16[1152,128]{1,0:T(8,128)(2,1)S(1)} %pad_maximum_fusion.refs_0_.refs_2_), channel_id=1, source_target_pairs={{0,48},{1,49},{2,50},{3,51},{4,52},{5,53},{6,54},{7,55},{8,56},{9,... | collective-permute-start | bytes 884744 | tf_op jit(solution)/shard_map/keys_x/ppermute | solution.py:51
  29.4 10.4 %collective-permute-start.2 = (bf16[1152,128]{1,0:T(8,128)(2,1)S(1)}, bf16[1152,128]{1,0:T(8,128)(2,1)S(1)}, u32[]{:S(2)}, u32[]{:S(2)}) collective-permute-start(bf16[1152,128]{1,0:T(8,128)(2,1)S(1)} %pad_maximum_fusion.refs_0_.refs_2_), channel_id=1, source_target_pairs={{0,32},{1,33},{2,34},{3,35},{4,36},{5,37},{6,38},{7,39},{8,40},{9,... | collective-permute-start | bytes 884744 | tf_op jit(solution)/shard_map/keys_x/ppermute | solution.py:51
  31.8 16.2 %collective-permute-start.1 = (bf16[1152,128]{1,0:T(8,128)(2,1)S(1)}, bf16[1152,128]{1,0:T(8,128)(2,1)S(1)}, u32[]{:S(2)}, u32[]{:S(2)}) collective-permute-start(bf16[1152,128]{1,0:T(8,128)(2,1)S(1)} %pad_maximum_fusion.refs_0_.refs_2_), channel_id=1, source_target_pairs={{0,16},{1,17},{2,18},{3,19},{4,20},{5,21},{6,22},{7,23},{8,24},{9,... | collective-permute-start | bytes 884744 | tf_op jit(solution)/shard_map/keys_x/ppermute | solution.py:51
  34.5 15.9 %copy-start.6 = (s32[5]{0:T(128)S(1)}, s32[5]{0:T(128)}, u32[]{:S(2)}) copy-start(s32[5]{0:T(128)} %stack.16.place_ref) | copy-start | bytes 64
  39.8 10.6 %copy-start.1 = (bf16[1152,128]{1,0:T(8,128)(2,1)}, bf16[1152,128]{1,0:T(8,128)(2,1)S(1)}, u32[]{:S(2)}) copy-start(bf16[1152,128]{1,0:T(8,128)(2,1)S(1)} %collective-permute-done.2.refs_2_.refs_4_) | copy-start | bytes 884740
  48.0 0.7 copy-start.3
  48.7 1.0 copy-start.4
  52.8 22.0 %all-to-all-start.1 = ((f32[16,8,256]{2,1,0:T(8,128)}), f32[16,8,256]{2,1,0:T(8,128)}, u32[]{:S(2)}, u32[]{:S(2)}) async-start(f32[16,8,256]{2,1,0:T(8,128)} %local_stats.1), calls=%async_computation.1 | async-start | bytes 262144 | tf_op jit(solution)/shard_map/stats_yz/all_to_all | solution.py:55
  74.9 1.0 copy-start.2
  75.8 1.0 copy-start.5
  81.4 0.7 copy-start
  82.2 29.8 %collective-permute-start.4 = (f32[576,128]{1,0:T(8,128)}, f32[576,128]{1,0:T(8,128)S(1)}, u32[]{:S(2)}, u32[]{:S(2)}) collective-permute-start(f32[576,128]{1,0:T(8,128)} %get-tuple-element.12), channel_id=1, source_target_pairs={{0,48},{1,49},{2,50},{3,51},{4,52},{5,53},{6,54},{7,55},{8,56},{9,... | collective-permute-start | bytes 884744 | tf_op jit(solution)/shard_map/shares_x/ppermute | solution.py:51
  84.1 27.9 %collective-permute-start.5 = (f32[576,128]{1,0:T(8,128)}, f32[576,128]{1,0:T(8,128)S(1)}, u32[]{:S(2)}, u32[]{:S(2)}) collective-permute-start(f32[576,128]{1,0:T(8,128)} %get-tuple-element.13), channel_id=1, source_target_pairs={{0,32},{1,33},{2,34},{3,35},{4,36},{5,37},{6,38},{7,39},{8,40},{9,... | collective-permute-start | bytes 884744 | tf_op jit(solution)/shard_map/shares_x/ppermute | solution.py:51
  86.0 26.0 %collective-permute-start.6 = (f32[576,128]{1,0:T(8,128)}, f32[576,128]{1,0:T(8,128)S(1)}, u32[]{:S(2)}, u32[]{:S(2)}) collective-permute-start(f32[576,128]{1,0:T(8,128)} %get-tuple-element.14), channel_id=1, source_target_pairs={{0,16},{1,17},{2,18},{3,19},{4,20},{5,21},{6,22},{7,23},{8,24},{9,... | collective-permute-start | bytes 884744 | tf_op jit(solution)/shard_map/shares_x/ppermute | solution.py:51
  106.4 14.8 %all-to-all-start.3 = ((f32[32,8,128]{2,1,0:T(8,128)}), f32[32,8,128]{2,1,0:T(8,128)S(1)}, u32[]{:S(2)}, u32[]{:S(2)}) async-start(f32[32,8,128]{2,1,0:T(8,128)} %add_pair.1), calls=%async_computation.3 | async-start | bytes 262144 | tf_op jit(solution)/shard_map/pair_plane/all_to_all | solution.py:55

commit v4 on v3

--- a/solution.py
+++ b/solution.py
@@ -17,6 +17,7 @@
 Z = ZH * ZL
 LANES = 128
 SUBLANES = 8
+MIB = 2**20
 
 
 def ctx_index(x, y, zh):
@@ -158,10 +159,8 @@
 
 
 def grads_kernel(slab, place_ref, parts_ref, keys_ref, rows_ref, turned_ref, *refs):
-    gain_ref, gain_tangent_ref, block_refs = refs[0], refs[1], refs[2 : 2 + X]
-    share_refs, pair_ref = refs[2 + X : 2 + 2 * X], refs[-1]
-    latent_width = gain_ref.shape[0]
-    norm_gain, gain_tangent = gain_ref[...], gain_tangent_ref[...]
+    *block_refs, grads_ref, pair_ref = refs
+    latent_width = rows_ref.shape[1] - keys_ref.shape[1]
     maxima, inv_totals, shift_mean, grad_mean, grad_mean_dot = merged_means(parts_ref)
     gain_grad = gain_grad_dot = 0.0
     for behind in range(X):
@@ -181,11 +180,33 @@
         key_count = scores.shape[1]
         latent_grad = by_query[:latent_width, :key_count] + by_cot[:, :key_count]
         latent_grad_dot = by_query[:latent_width, key_count:] + by_cot[:, key_count:]
-        latent, latent_dot, inv_rms, inv_dot, normed, normed_dot = norm_side(
-            block_refs[behind], latent_width
-        )
+        normed, normed_dot = norm_side(block_refs[behind], latent_width)[4:]
         gain_grad += latent_grad * normed
         gain_grad_dot += latent_grad_dot * normed + latent_grad * normed_dot
+        grads_ref[behind, :latent_width, :] = latent_grad
+        grads_ref[behind, latent_width : 2 * latent_width, :] = latent_grad_dot
+        grads_ref[behind, 2 * latent_width :, :] = by_query[latent_width:, key_count:]
+    pair = as_rows([jnp.sum(each, axis=1, keepdims=True) for each in (gain_grad, gain_grad_dot)])
+    pair = jnp.concatenate(
+        [
+            pair[row : row + 1, at : at + LANES]
+            for row in range(2)
+            for at in range(0, latent_width, LANES)
+        ],
+        axis=0,
+    )
+    for copy in range(pair_ref.shape[0]):
+        pair_ref[copy] = pair
+
+
+def shares_kernel(grads_ref, gain_ref, gain_tangent_ref, *refs):
+    block_refs, share_refs = refs[:X], refs[X:]
+    latent_width = gain_ref.shape[0]
+    norm_gain, gain_tangent = gain_ref[...], gain_tangent_ref[...]
+    for behind in range(X):
+        latent_grad = grads_ref[behind, :latent_width, :]
+        latent_grad_dot = grads_ref[behind, latent_width : 2 * latent_width, :]
+        latent, latent_dot, inv_rms, inv_dot, _, _ = norm_side(block_refs[behind], latent_width)
         normed_grad = latent_grad * norm_gain
         normed_grad_dot = latent_grad_dot * norm_gain + latent_grad * gain_tangent
         inner_grad = jnp.mean(normed_grad * latent, axis=0, keepdims=True)
@@ -200,18 +221,7 @@
             - (rms_cubed_dot * inner_grad + rms_cubed * inner_grad_dot) * latent
             - (rms_cubed * inner_grad) * latent_dot
         )
-        share_refs[behind][latent_width:, :] = by_query[latent_width:, key_count:]
-    pair = as_rows([jnp.sum(each, axis=1, keepdims=True) for each in (gain_grad, gain_grad_dot)])
-    pair = jnp.concatenate(
-        [
-            pair[row : row + 1, at : at + LANES]
-            for row in range(2)
-            for at in range(0, latent_width, LANES)
-        ],
-        axis=0,
-    )
-    for copy in range(pair_ref.shape[0]):
-        pair_ref[copy] = pair
+        share_refs[behind][latent_width:, :] = grads_ref[behind, 2 * latent_width :, :]
 
 
 def add_kernel(parts_ref, out_ref):
@@ -231,7 +241,6 @@
     packed_width = latent_width + full_width
     row_count = Y * ZH * slab
     smem = [pl.BlockSpec(memory_space=pltpu.SMEM)]
-    limit = pltpu.CompilerParams(vmem_limit_bytes=40 * 2**20)
     flops = 4 * X * key_count * row_count * packed_width
     ctx_at = lax.axis_index("ctx").astype(jnp.int32)
     place = jnp.stack(
@@ -253,22 +262,25 @@
             out_shape=jax.ShapeDtypeStruct((Y, ZH, slab, packed_width), packed.dtype),
             in_specs=smem + in_vmem(2),
             out_specs=pl.BlockSpec(memory_space=pltpu.VMEM),
+            compiler_params=pltpu.CompilerParams(vmem_limit_bytes=4 * MIB),
             name="pair_rows",
         )(place, packed, ctx_permute(packed, dz=1))
     with jax.named_scope("rows_y"):
         block = jnp.concatenate([kv_rows[0].T, kv_tangent[0].T], axis=0)
-        block, copies = lax.optimization_barrier((block, copies))
+        near_block, copies = lax.optimization_barrier((block, copies))
         rows = exchange(copies, "ctx", Y_GROUPS).reshape(row_count, packed_width)
 
     with jax.named_scope("keys_x"):
-        blocks = [block] + [ctx_permute(block, dx=step) for step in range(1, X)]
+        far_block = ctx_permute(block, dx=2)
+        near_blocks = [ctx_permute(near_block, dx=step) for step in (1, -1)]
+        blocks = [block, near_blocks[0], far_block, near_blocks[1]]
     gains = (norm_gain[:, None], gain_tangent[:, None])
     keys = pl.pallas_call(
         keys_kernel,
         out_shape=jax.ShapeDtypeStruct((X, full_width, 2 * key_count), jnp.bfloat16),
         in_specs=in_vmem(2 + X),
         out_specs=pl.BlockSpec(memory_space=pltpu.VMEM),
-        compiler_params=limit,
+        compiler_params=pltpu.CompilerParams(vmem_limit_bytes=8 * MIB),
         name="make_keys",
     )(*gains, *blocks)
 
@@ -277,27 +289,40 @@
         out_shape=jax.ShapeDtypeStruct((Y * ZH, SUBLANES, row_count), jnp.float32),
         in_specs=smem + in_vmem(2),
         out_specs=pl.BlockSpec(memory_space=pltpu.VMEM),
-        compiler_params=limit,
+        compiler_params=pltpu.CompilerParams(vmem_limit_bytes=12 * MIB),
         cost_estimate=pl.CostEstimate(
-            flops=flops, bytes_accessed=3 * 2**20, transcendentals=X * key_count * row_count
+            flops=flops, bytes_accessed=3 * MIB, transcendentals=X * key_count * row_count
         ),
         name="local_stats",
     )(place, keys, rows)
     with jax.named_scope("stats_yz"):
         sums = exchange(sums, "ctx", YZ_GROUPS)
 
-    *shares, pair = pl.pallas_call(
+    grads, pair = pl.pallas_call(
         functools.partial(grads_kernel, slab),
-        out_shape=[jax.ShapeDtypeStruct((full_width, key_count), jnp.float32)] * X
-        + [jax.ShapeDtypeStruct((Z * CORE, SUBLANES, LANES), jnp.float32)],
-        in_specs=smem + in_vmem(6 + X),
-        out_specs=in_vmem(X + 1),
-        compiler_params=limit,
+        out_shape=[
+            jax.ShapeDtypeStruct((X, latent_width + full_width, key_count), jnp.float32),
+            jax.ShapeDtypeStruct((Z * CORE, SUBLANES, LANES), jnp.float32),
+        ],
+        in_specs=smem + in_vmem(4 + X),
+        out_specs=in_vmem(2),
+        compiler_params=pltpu.CompilerParams(vmem_limit_bytes=16 * MIB),
         cost_estimate=pl.CostEstimate(
-            flops=2 * flops, bytes_accessed=4 * 2**20, transcendentals=X * key_count * row_count
+            flops=2 * flops, bytes_accessed=6 * MIB, transcendentals=X * key_count * row_count
         ),
         name="gradients",
-    )(place, sums, keys, rows, rows.T, *gains, *blocks)
+    )(place, sums, keys, rows, rows.T, *blocks)
+    shares = pl.pallas_call(
+        shares_kernel,
+        out_shape=[jax.ShapeDtypeStruct((full_width, key_count), jnp.float32)] * X,
+        in_specs=in_vmem(3 + X),
+        out_specs=in_vmem(X),
+        compiler_params=pltpu.CompilerParams(vmem_limit_bytes=12 * MIB),
+        cost_estimate=pl.CostEstimate(
+            flops=30 * X * key_count * latent_width, bytes_accessed=6 * MIB, transcendentals=0
+        ),
+        name="row_shares",
+    )(grads, *gains, *blocks)
 
     with jax.named_scope("shares_x"):
         hv_rows = sum([ctx_permute(shares[step], dx=-step) for step in range(1, X)], shares[0])
@@ -305,6 +330,7 @@
         pair = pl.pallas_call(
             add_kernel,
             out_shape=jax.ShapeDtypeStruct((X * Y, SUBLANES, LANES), jnp.float32),
+            compiler_params=pltpu.CompilerParams(vmem_limit_bytes=2 * MIB),
             name="add_pair",
         )(exchange(pair, ("dp", "ctx"), COLUMNS))
     with jax.named_scope("pair_plane"):

time: 123 us -> 114 us (0.927)
  waiting for transfers between devices: 33.1 us -> 28.2 us
  local copies, waits for them, and re-layouts: 6.75 us -> 3.74 us
  starting transfers between devices: 49.8 us -> 51.7 us
  Pallas kernels: 10.9 us -> 9.14 us
    ppermute x7, waiting for transfers between devices: 13.4 us -> 7.43 us  [ctx_permute(): return lax.ppermute(value, 'ctx', pairs)]
    ppermute x7, starting transfers between devices: 28 us -> 31.4 us  [ctx_permute(): return lax.ppermute(value, 'ctx', pairs)]
    unnamed x22 -> x8, local copies, waits for them, and re-layouts: 4.95 us -> 1.72 us
    all_to_all x3, starting transfers between devices: 21.8 us -> 20.4 us  [exchange(): return lax.all_to_all(copies, axis, 0, 0, axis_index_groups=groups)]
  transfers between devices with their start and end apart: 10 -> 10, of which waited for: 5 -> 5; matrix products, arithmetic and copies ran while one was open for 3% -> 3% of each run, Pallas kernels for 2% -> 1%
where the time goes in v4:
time: 114 us; the launch traced here: 113 us
  starting transfers between devices  51.7 us (45%)
  waiting for transfers between devices  28.2 us (25%)
  blocking collectives  15.9 us (14%)
  Pallas kernels  9.14 us (8%)
  local copies, waits for them, and re-layouts  3.74 us (3%)
  other arithmetic  2.56 us (2%)
  between operations  2.12 us (2%)
    ppermute x7, starting transfers between devices, ctx_permute(): return lax.ppermute(value, 'ctx', pairs)  31.4 us
    all_to_all x3, waiting for transfers between devices, exchange(): return lax.all_to_all(copies, axis, 0, 0, axis_index_groups=groups)  20.8 us
    all_to_all x3, starting transfers between devices, exchange(): return lax.all_to_all(copies, axis, 0, 0, axis_index_groups=groups)  20.4 us
    all_to_all x1, blocking collectives, exchange(): return lax.all_to_all(copies, axis, 0, 0, axis_index_groups=groups)  15.9 us
    ppermute x7, waiting for transfers between devices, ctx_permute(): return lax.ppermute(value, 'ctx', pairs)  7.43 us
    pallas_call x1, Pallas kernels, shards(): pl.pallas_call(functools.partial(grads_kernel, slab), out_shape=[jax.Shap...  3.57 us
  transfers between devices with their start and end apart: 10, of which 5 were waited for; matrix products, arithmetic and copies ran while one was open for 3% of the time, Pallas kernels for 1%

profile of v4, /device:TPU:1, one launch (start us, length us, event | category | flops | bytes accessed | tf_op | source)
XLA Modules:
  0.0 113.4 jit_solution(13678221029188577283)
XLA Ops:
  0.6 0.0 copy-start.2
  0.6 0.0 copy-start.3
  0.7 0.8 pad_maximum_fusion.1.own_ref
  1.4 11.5 %collective-permute-start = (bf16[16,1088]{1,0:T(8,128)(2,1)S(1)}, bf16[16,1088]{1,0:T(8,128)(2,1)S(1)}, u32[]{:S(2)}, u32[]{:S(2)}) collective-permute-start(bf16[16,1088]{1,0:T(8,128)(2,1)S(1)} %pad_maximum_fusion.1.own_ref), channel_id=1, source_target_pairs={{0,1},{1,0},{2,3},{3,2},{4,5},{5,4},{6,7},{7,6},{8,9},{9,8},{10,11... | collective-permute-start | bytes 104456 | tf_op jit(solution)/shard_map/rows_z/ppermute | solution.py:52
  12.9 1.0 pad_maximum_fusion.refs_0_
  15.2 0.1 stack.16.place_ref
  15.3 0.0 collective-permute-done.other_ref
  15.3 1.4 %pair_rows.1 = bf16[8,2,16,1088]{3,2,1,0:T(8,128)(2,1)} custom-call(s32[5]{0:T(128)S(1)} %stack.16.place_ref, bf16[16,1088]{1,0:T(8,128)(2,1)S(1)} %pad_maximum_fusion.1.own_ref, bf16[16,1088]{1,0:T(8,128)(2,1)S(1)} %collective-permute-done.other_ref), custom_call_target="tpu_custom_call" | custom-call | tf_op jit(solution)/shard_map/rows_z/pair_rows/pallas_call | solution.py:260
  16.7 6.8 %all-to-all-start = ((bf16[8,2,16,1088]{3,2,1,0:T(8,128)(2,1)}), bf16[8,2,16,1088]{3,2,1,0:T(8,128)(2,1)S(1)}, u32[]{:S(2)}, u32[]{:S(2)}) async-start(bf16[8,2,16,1088]{3,2,1,0:T(8,128)(2,1)} %pair_rows.1), calls=%async_computation | async-start | bytes 1179648 | tf_op jit(solution)/shard_map/rows_y/all_to_all | solution.py:56
  23.5 4.6 %collective-permute-start.2 = (bf16[1152,128]{1,0:T(8,128)(2,1)S(1)}, bf16[1152,128]{1,0:T(8,128)(2,1)S(1)}, u32[]{:S(2)}, u32[]{:S(2)}) collective-permute-start(bf16[1152,128]{1,0:T(8,128)(2,1)S(1)} %pad_maximum_fusion.refs_0_), channel_id=1, source_target_pairs={{0,32},{1,33},{2,34},{3,35},{4,36},{5,37},{6,38},{7,39},{8,40},{9,... | collective-permute-start | bytes 884744 | tf_op jit(solution)/shard_map/keys_x/ppermute | solution.py:52
  28.2 2.8 %collective-permute-start.3 = (bf16[1152,128]{1,0:T(8,128)(2,1)S(1)}, bf16[1152,128]{1,0:T(8,128)(2,1)S(1)}, u32[]{:S(2)}, u32[]{:S(2)}) collective-permute-start(bf16[1152,128]{1,0:T(8,128)(2,1)S(1)} %pad_maximum_fusion.refs_0_), channel_id=1, source_target_pairs={{0,48},{1,49},{2,50},{3,51},{4,52},{5,53},{6,54},{7,55},{8,56},{9,... | collective-permute-start | bytes 884744 | tf_op jit(solution)/shard_map/keys_x/ppermute | solution.py:52
  30.9 2.5 %collective-permute-start.1 = (bf16[1152,128]{1,0:T(8,128)(2,1)S(1)}, bf16[1152,128]{1,0:T(8,128)(2,1)S(1)}, u32[]{:S(2)}, u32[]{:S(2)}) collective-permute-start(bf16[1152,128]{1,0:T(8,128)(2,1)S(1)} %pad_maximum_fusion.refs_0_), channel_id=1, source_target_pairs={{0,16},{1,17},{2,18},{3,19},{4,20},{5,21},{6,22},{7,23},{8,24},{9,... | collective-permute-start | bytes 884744 | tf_op jit(solution)/shard_map/keys_x/ppermute | solution.py:52
  33.5 0.0 copy-done.2
  33.5 0.1 copy.13.gain_ref
  33.6 0.0 copy-done.3
  33.6 0.1 copy.14.gain_tangent_ref
  33.8 0.4 collective-permute-done.2.refs_2_
  34.2 7.0 %collective-permute-done.3.refs_3_ = bf16[1152,128]{1,0:T(8,128)(2,1)S(1)} collective-permute-done((bf16[1152,128]{1,0:T(8,128)(2,1)S(1)}, bf16[1152,128]{1,0:T(8,128)(2,1)S(1)}, u32[]{:S(2)}, u32[]{:S(2)}) %collective-permute-start.3) | collective-permute-done | bytes 294944 | tf_op jit(solution)/shard_map/keys_x/ppermute | solution.py:52
  41.2 0.0 collective-permute-done.1.refs_1_
  41.2 0.7 make_keys.1.keys_ref
  41.9 0.9 all-to-all-done
  42.8 1.7 %local_stats.1 = f32[16,8,256]{2,1,0:T(8,128)S(1)} custom-call(s32[5]{0:T(128)S(1)} %stack.16.place_ref, bf16[4,576,256]{2,1,0:T(8,128)(2,1)S(1)} %make_keys.1.keys_ref, bf16[256,1088]{1,0:T(8,128)(2,1)S(1)} %bitcast.19), custom_call_target="tpu_custom_call" | custom-call | flops 570425344 | bytes 3145728 | tf_op jit(solution)/shard_map/local_stats/pallas_call | solution.py:287
  44.6 0.0 copy-start.1
  44.6 0.7 copy-done.1
  45.2 9.1 %all-to-all-start.1 = ((f32[16,8,256]{2,1,0:T(8,128)}), f32[16,8,256]{2,1,0:T(8,128)}, u32[]{:S(2)}, u32[]{:S(2)}) async-start(f32[16,8,256]{2,1,0:T(8,128)} %copy-done.1), calls=%async_computation.1 | async-start | bytes 262144 | tf_op jit(solution)/shard_map/stats_yz/all_to_all | solution.py:56
  54.3 1.0 copy.15
  55.4 11.5 %all-to-all-done.1.parts_ref = f32[16,8,256]{2,1,0:T(8,128)} async-done(((f32[16,8,256]{2,1,0:T(8,128)}), f32[16,8,256]{2,1,0:T(8,128)}, u32[]{:S(2)}, u32[]{:S(2)}) %all-to-all-start.1) | async-done | bytes 131104 | tf_op jit(solution)/shard_map/stats_yz/all_to_all | solution.py:56
  66.9 0.0 copy-start
  66.9 1.1 copy-done
  68.0 3.6 %gradients.1 = (f32[4,1088,128]{2,1,0:T(8,128)S(1)}, f32[16,8,128]{2,1,0:T(8,128)S(1)}) custom-call(s32[5]{0:T(128)S(1)} %stack.16.place_ref, f32[16,8,256]{2,1,0:T(8,128)} %all-to-all-done.1.parts_ref, bf16[4,576,256]{2,1,0:T(8,128)(2,1)S(1)} %make_keys.1.keys_ref, bf16[256,1088]{1,0:T(8,128)(2,1)S(1)} %bitcast.21, bf16[1088,256]{1,0:T(8,128)(2,1)S(1)} %bitcast.22, ...), custom_call_target="tpu_custom_call" | custom-call | flops 1140850688 | bytes 6291456 | tf_op jit(solution)/shard_map/gradients/pallas_call | solution.py:301
  71.5 1.0 row_shares.1
  72.6 5.3 %collective-permute-start.4 = (f32[576,128]{1,0:T(8,128)S(1)}, f32[576,128]{1,0:T(8,128)S(1)}, u32[]{:S(2)}, u32[]{:S(2)}) collective-permute-start(f32[576,128]{1,0:T(8,128)S(1)} %get-tuple-element.14), channel_id=1, source_target_pairs={{0,48},{1,49},{2,50},{3,51},{4,52},{5,53},{6,54},{7,55},{8,56},{9,... | collective-permute-start | bytes 884744 | tf_op jit(solution)/shard_map/shares_x/ppermute | solution.py:52
  77.9 2.7 %collective-permute-start.5 = (f32[576,128]{1,0:T(8,128)S(1)}, f32[576,128]{1,0:T(8,128)S(1)}, u32[]{:S(2)}, u32[]{:S(2)}) collective-permute-start(f32[576,128]{1,0:T(8,128)S(1)} %get-tuple-element.15), channel_id=1, source_target_pairs={{0,32},{1,33},{2,34},{3,35},{4,36},{5,37},{6,38},{7,39},{8,40},{9,... | collective-permute-start | bytes 884744 | tf_op jit(solution)/shard_map/shares_x/ppermute | solution.py:52
  80.7 1.9 %collective-permute-start.6 = (f32[576,128]{1,0:T(8,128)S(1)}, f32[576,128]{1,0:T(8,128)S(1)}, u32[]{:S(2)}, u32[]{:S(2)}) collective-permute-start(f32[576,128]{1,0:T(8,128)S(1)} %get-tuple-element.16), channel_id=1, source_target_pairs={{0,16},{1,17},{2,18},{3,19},{4,20},{5,21},{6,22},{7,23},{8,24},{9,... | collective-permute-start | bytes 884744 | tf_op jit(solution)/shard_map/shares_x/ppermute | solution.py:52
  82.6 15.9 %all_to_all.20.parts_ref = f32[16,8,128]{2,1,0:T(8,128)S(1)} all-to-all(f32[16,8,128]{2,1,0:T(8,128)S(1)} %get-tuple-element.17), channel_id=1, replica_groups={{0,64,128,192,256,320,384,448,1,65,129,193,257,321,385,449},{2,66,130,1..., dimensions={0} | all-to-all | bytes 131072 | tf_op jit(solution)/shard_map/pair_column/all_to_all | solution.py:56
  98.5 0.7 add_pair.1
  99.1 4.4 %all-to-all-start.3 = ((f32[32,8,128]{2,1,0:T(8,128)}), f32[32,8,128]{2,1,0:T(8,128)S(1)}, u32[]{:S(2)}, u32[]{:S(2)}) async-start(f32[32,8,128]{2,1,0:T(8,128)} %add_pair.1), calls=%async_computation.3 | async-start | bytes 262144 | tf_op jit(solution)/shard_map/pair_plane/all_to_all | solution.py:56
  103.6 0.0 collective-permute-done.4
  103.6 0.0 collective-permute-done.5
  103.6 0.0 collective-permute-done.6
  103.6 0.8 add_bitcast_fusion
  104.4 8.3 %all-to-all-done.3 = f32[32,8,128]{2,1,0:T(8,128)S(1)} async-done(((f32[32,8,128]{2,1,0:T(8,128)}), f32[32,8,128]{2,1,0:T(8,128)S(1)}, u32[]{:S(2)}, u32[]{:S(2)}) %all-to-all-start.3) | async-done | bytes 131104 | tf_op jit(solution)/shard_map/pair_plane/all_to_all | solution.py:56
  112.8 0.6 reshape.21
  (1 shorter events, 0.0 us)
Async XLA Ops:
  0.6 32.8 %copy-start.2 = (f32[512]{0:T(512)S(1)}, f32[512]{0:T(512)}, u32[]{:S(2)}) copy-start(f32[512]{0:T(512)} %param.14) | copy-start | bytes 6148
  0.6 33.0 %copy-start.3 = (f32[512]{0:T(512)S(1)}, f32[512]{0:T(512)}, u32[]{:S(2)}) copy-start(f32[512]{0:T(512)} %param.15) | copy-start | bytes 6148
  1.4 13.9 %collective-permute-start = (bf16[16,1088]{1,0:T(8,128)(2,1)S(1)}, bf16[16,1088]{1,0:T(8,128)(2,1)S(1)}, u32[]{:S(2)}, u32[]{:S(2)}) collective-permute-start(bf16[16,1088]{1,0:T(8,128)(2,1)S(1)} %pad_maximum_fusion.1.own_ref), channel_id=1, source_target_pairs={{0,1},{1,0},{2,3},{3,2},{4,5},{5,4},{6,7},{7,6},{8,9},{9,8},{10,11... | collective-permute-start | bytes 104456 | tf_op jit(solution)/shard_map/rows_z/ppermute | solution.py:52
  16.7 26.1 %all-to-all-start = ((bf16[8,2,16,1088]{3,2,1,0:T(8,128)(2,1)}), bf16[8,2,16,1088]{3,2,1,0:T(8,128)(2,1)S(1)}, u32[]{:S(2)}, u32[]{:S(2)}) async-start(bf16[8,2,16,1088]{3,2,1,0:T(8,128)(2,1)} %pair_rows.1), calls=%async_computation | async-start | bytes 1179648 | tf_op jit(solution)/shard_map/rows_y/all_to_all | solution.py:56
  23.5 10.6 %collective-permute-start.2 = (bf16[1152,128]{1,0:T(8,128)(2,1)S(1)}, bf16[1152,128]{1,0:T(8,128)(2,1)S(1)}, u32[]{:S(2)}, u32[]{:S(2)}) collective-permute-start(bf16[1152,128]{1,0:T(8,128)(2,1)S(1)} %pad_maximum_fusion.refs_0_), channel_id=1, source_target_pairs={{0,32},{1,33},{2,34},{3,35},{4,36},{5,37},{6,38},{7,39},{8,40},{9,... | collective-permute-start | bytes 884744 | tf_op jit(solution)/shard_map/keys_x/ppermute | solution.py:52
  28.2 13.0 %collective-permute-start.3 = (bf16[1152,128]{1,0:T(8,128)(2,1)S(1)}, bf16[1152,128]{1,0:T(8,128)(2,1)S(1)}, u32[]{:S(2)}, u32[]{:S(2)}) collective-permute-start(bf16[1152,128]{1,0:T(8,128)(2,1)S(1)} %pad_maximum_fusion.refs_0_), channel_id=1, source_target_pairs={{0,48},{1,49},{2,50},{3,51},{4,52},{5,53},{6,54},{7,55},{8,56},{9,... | collective-permute-start | bytes 884744 | tf_op jit(solution)/shard_map/keys_x/ppermute | solution.py:52
  30.9 10.3 %collective-permute-start.1 = (bf16[1152,128]{1,0:T(8,128)(2,1)S(1)}, bf16[1152,128]{1,0:T(8,128)(2,1)S(1)}, u32[]{:S(2)}, u32[]{:S(2)}) collective-permute-start(bf16[1152,128]{1,0:T(8,128)(2,1)S(1)} %pad_maximum_fusion.refs_0_), channel_id=1, source_target_pairs={{0,16},{1,17},{2,18},{3,19},{4,20},{5,21},{6,22},{7,23},{8,24},{9,... | collective-permute-start | bytes 884744 | tf_op jit(solution)/shard_map/keys_x/ppermute | solution.py:52
  44.6 0.7 copy-start.1
  45.2 21.7 %all-to-all-start.1 = ((f32[16,8,256]{2,1,0:T(8,128)}), f32[16,8,256]{2,1,0:T(8,128)}, u32[]{:S(2)}, u32[]{:S(2)}) async-start(f32[16,8,256]{2,1,0:T(8,128)} %copy-done.1), calls=%async_computation.1 | async-start | bytes 262144 | tf_op jit(solution)/shard_map/stats_yz/all_to_all | solution.py:56
  66.9 1.1 copy-start
  72.6 31.0 %collective-permute-start.4 = (f32[576,128]{1,0:T(8,128)S(1)}, f32[576,128]{1,0:T(8,128)S(1)}, u32[]{:S(2)}, u32[]{:S(2)}) collective-permute-start(f32[576,128]{1,0:T(8,128)S(1)} %get-tuple-element.14), channel_id=1, source_target_pairs={{0,48},{1,49},{2,50},{3,51},{4,52},{5,53},{6,54},{7,55},{8,56},{9,... | collective-permute-start | bytes 884744 | tf_op jit(solution)/shard_map/shares_x/ppermute | solution.py:52
  77.9 25.7 %collective-permute-start.5 = (f32[576,128]{1,0:T(8,128)S(1)}, f32[576,128]{1,0:T(8,128)S(1)}, u32[]{:S(2)}, u32[]{:S(2)}) collective-permute-start(f32[576,128]{1,0:T(8,128)S(1)} %get-tuple-element.15), channel_id=1, source_target_pairs={{0,32},{1,33},{2,34},{3,35},{4,36},{5,37},{6,38},{7,39},{8,40},{9,... | collective-permute-start | bytes 884744 | tf_op jit(solution)/shard_map/shares_x/ppermute | solution.py:52
  80.7 22.9 %collective-permute-start.6 = (f32[576,128]{1,0:T(8,128)S(1)}, f32[576,128]{1,0:T(8,128)S(1)}, u32[]{:S(2)}, u32[]{:S(2)}) collective-permute-start(f32[576,128]{1,0:T(8,128)S(1)} %get-tuple-element.16), channel_id=1, source_target_pairs={{0,16},{1,17},{2,18},{3,19},{4,20},{5,21},{6,22},{7,23},{8,24},{9,... | collective-permute-start | bytes 884744 | tf_op jit(solution)/shard_map/shares_x/ppermute | solution.py:52
  99.1 13.6 %all-to-all-start.3 = ((f32[32,8,128]{2,1,0:T(8,128)}), f32[32,8,128]{2,1,0:T(8,128)S(1)}, u32[]{:S(2)}, u32[]{:S(2)}) async-start(f32[32,8,128]{2,1,0:T(8,128)} %add_pair.1), calls=%async_computation.3 | async-start | bytes 262144 | tf_op jit(solution)/shard_map/pair_plane/all_to_all | solution.py:56

commit v5 on v4

--- a/solution.py
+++ b/solution.py
@@ -158,9 +158,11 @@
     return [columns[:, at : at + 1] for at in range(5)]
 
 
-def grads_kernel(slab, place_ref, parts_ref, keys_ref, rows_ref, turned_ref, *refs):
+def grads_kernel(slab, place_ref, parts_ref, keys_ref, rows_ref, *refs):
     *block_refs, grads_ref, pair_ref = refs
     latent_width = rows_ref.shape[1] - keys_ref.shape[1]
+    turned_cot = rows_ref[:, :latent_width].T
+    turned_query = rows_ref[:, latent_width:].T
     maxima, inv_totals, shift_mean, grad_mean, grad_mean_dot = merged_means(parts_ref)
     gain_grad = gain_grad_dot = 0.0
     for behind in range(X):
@@ -173,9 +175,9 @@
         score_grad = attention * centred
         score_grad_dot = attention_dot * centred + attention * (value_dot - grad_mean_dot)
         right = jnp.concatenate([score_grad, score_grad_dot], axis=1).astype(jnp.bfloat16)
-        by_query = score_scale * dot(turned_ref[latent_width:, :], right)
+        by_query = score_scale * dot(turned_query, right)
         right = jnp.concatenate([attention, attention_dot], axis=1).astype(jnp.bfloat16)
-        by_cot = dot(turned_ref[:latent_width, :], right)
+        by_cot = dot(turned_cot, right)
 
         key_count = scores.shape[1]
         latent_grad = by_query[:latent_width, :key_count] + by_cot[:, :key_count]
@@ -304,14 +306,14 @@
             jax.ShapeDtypeStruct((X, latent_width + full_width, key_count), jnp.float32),
             jax.ShapeDtypeStruct((Z * CORE, SUBLANES, LANES), jnp.float32),
         ],
-        in_specs=smem + in_vmem(4 + X),
+        in_specs=smem + in_vmem(3 + X),
         out_specs=in_vmem(2),
         compiler_params=pltpu.CompilerParams(vmem_limit_bytes=16 * MIB),
         cost_estimate=pl.CostEstimate(
             flops=2 * flops, bytes_accessed=6 * MIB, transcendentals=X * key_count * row_count
         ),
         name="gradients",
-    )(place, sums, keys, rows, rows.T, *blocks)
+    )(place, sums, keys, rows, *blocks)
     shares = pl.pallas_call(
         shares_kernel,
         out_shape=[jax.ShapeDtypeStruct((full_width, key_count), jnp.float32)] * X,
@@ -319,7 +321,7 @@
         out_specs=in_vmem(X),
         compiler_params=pltpu.CompilerParams(vmem_limit_bytes=12 * MIB),
         cost_estimate=pl.CostEstimate(
-            flops=30 * X * key_count * latent_width, bytes_accessed=6 * MIB, transcendentals=0
+            flops=10**10, bytes_accessed=6 * MIB, transcendentals=0
         ),
         name="row_shares",
     )(grads, *gains, *blocks)
@@ -331,6 +333,9 @@
             add_kernel,
             out_shape=jax.ShapeDtypeStruct((X * Y, SUBLANES, LANES), jnp.float32),
             compiler_params=pltpu.CompilerParams(vmem_limit_bytes=2 * MIB),
+            cost_estimate=pl.CostEstimate(
+                flops=10**11, bytes_accessed=MIB // 4, transcendentals=0
+            ),
             name="add_pair",
         )(exchange(pair, ("dp", "ctx"), COLUMNS))
     with jax.named_scope("pair_plane"):

time: 114 us -> 108 us (0.947)
  waiting for transfers between devices: 28.2 us -> 18.1 us
  blocking collectives: 15.9 us -> 21.4 us
  starting transfers between devices: 51.7 us -> 50.1 us
    all_to_all x3, waiting for transfers between devices: 20.8 us -> 0.92 us  [exchange(): return lax.all_to_all(copies, axis, 0, 0, axis_index_groups=groups)]
    ppermute x7, waiting for transfers between devices: 7.43 us -> 17.2 us  [ctx_permute(): return lax.ppermute(value, 'ctx', pairs)]
    all_to_all x1, blocking collectives: 15.9 us -> 21.4 us  [exchange(): return lax.all_to_all(copies, axis, 0, 0, axis_index_groups=groups)]
    ppermute x7, starting transfers between devices: 31.4 us -> 29.7 us  [ctx_permute(): return lax.ppermute(value, 'ctx', pairs)]
    unnamed x8, local copies, waits for them, and re-layouts: 1.72 us -> 3.01 us
  transfers between devices with their start and end apart: 10 -> 10, of which waited for: 5 -> 5; matrix products, arithmetic and copies ran while one was open for 3% -> 2% of each run, Pallas kernels for 1% -> 2%
where the time goes in v5:
time: 108 us
  starting transfers between devices  50.1 us (46%)
  blocking collectives  21.4 us (20%)
  waiting for transfers between devices  18.1 us (17%)
  Pallas kernels  9.39 us (9%)
  local copies, waits for them, and re-layouts  3.99 us (4%)
  other arithmetic  2.56 us (2%)
  between operations  2.1 us (2%)
    ppermute x7, starting transfers between devices, ctx_permute(): return lax.ppermute(value, 'ctx', pairs)  29.7 us
    all_to_all x1, blocking collectives, exchange(): return lax.all_to_all(copies, axis, 0, 0, axis_index_groups=groups)  21.4 us
    all_to_all x3, starting transfers between devices, exchange(): return lax.all_to_all(copies, axis, 0, 0, axis_index_groups=groups)  20.4 us
    ppermute x7, waiting for transfers between devices, ctx_permute(): return lax.ppermute(value, 'ctx', pairs)  17.2 us
    pallas_call x1, Pallas kernels, shards(): pl.pallas_call(functools.partial(grads_kernel, slab), out_shape=[jax.Shap...  3.82 us
    unnamed x8, local copies, waits for them, and re-layouts  3.01 us
  transfers between devices with their start and end apart: 10, of which 5 were waited for; matrix products, arithmetic and copies ran while one was open for 2% of the time, Pallas kernels for 2%

profile of v5, /device:TPU:1, one launch (start us, length us, event | category | flops | bytes accessed | tf_op | source)
XLA Modules:
  0.0 107.5 jit_solution(12676764752638060200)
XLA Ops:
  0.6 0.0 copy-start.2
  0.6 0.0 copy-start.3
  0.7 0.8 pad_maximum_fusion.1.own_ref
  1.4 11.5 %collective-permute-start = (bf16[16,1088]{1,0:T(8,128)(2,1)S(1)}, bf16[16,1088]{1,0:T(8,128)(2,1)S(1)}, u32[]{:S(2)}, u32[]{:S(2)}) collective-permute-start(bf16[16,1088]{1,0:T(8,128)(2,1)S(1)} %pad_maximum_fusion.1.own_ref), channel_id=1, source_target_pairs={{0,1},{1,0},{2,3},{3,2},{4,5},{5,4},{6,7},{7,6},{8,9},{9,8},{10,11... | collective-permute-start | bytes 104456 | tf_op jit(solution)/shard_map/rows_z/ppermute | solution.py:52
  12.9 1.0 pad_maximum_fusion.refs_0_
  15.2 0.1 stack.16.place_ref
  15.3 0.0 collective-permute-done.other_ref
  15.3 1.4 %pair_rows.1 = bf16[8,2,16,1088]{3,2,1,0:T(8,128)(2,1)} custom-call(s32[5]{0:T(128)S(1)} %stack.16.place_ref, bf16[16,1088]{1,0:T(8,128)(2,1)S(1)} %pad_maximum_fusion.1.own_ref, bf16[16,1088]{1,0:T(8,128)(2,1)S(1)} %collective-permute-done.other_ref), custom_call_target="tpu_custom_call" | custom-call | tf_op jit(solution)/shard_map/rows_z/pair_rows/pallas_call | solution.py:262
  16.7 6.8 %all-to-all-start = ((bf16[8,2,16,1088]{3,2,1,0:T(8,128)(2,1)}), bf16[8,2,16,1088]{3,2,1,0:T(8,128)(2,1)S(1)}, u32[]{:S(2)}, u32[]{:S(2)}) async-start(bf16[8,2,16,1088]{3,2,1,0:T(8,128)(2,1)} %pair_rows.1), calls=%async_computation | async-start | bytes 1179648 | tf_op jit(solution)/shard_map/rows_y/all_to_all | solution.py:56
  23.5 4.6 %collective-permute-start.2 = (bf16[1152,128]{1,0:T(8,128)(2,1)S(1)}, bf16[1152,128]{1,0:T(8,128)(2,1)S(1)}, u32[]{:S(2)}, u32[]{:S(2)}) collective-permute-start(bf16[1152,128]{1,0:T(8,128)(2,1)S(1)} %pad_maximum_fusion.refs_0_), channel_id=1, source_target_pairs={{0,32},{1,33},{2,34},{3,35},{4,36},{5,37},{6,38},{7,39},{8,40},{9,... | collective-permute-start | bytes 884744 | tf_op jit(solution)/shard_map/keys_x/ppermute | solution.py:52
  28.2 2.8 %collective-permute-start.3 = (bf16[1152,128]{1,0:T(8,128)(2,1)S(1)}, bf16[1152,128]{1,0:T(8,128)(2,1)S(1)}, u32[]{:S(2)}, u32[]{:S(2)}) collective-permute-start(bf16[1152,128]{1,0:T(8,128)(2,1)S(1)} %pad_maximum_fusion.refs_0_), channel_id=1, source_target_pairs={{0,48},{1,49},{2,50},{3,51},{4,52},{5,53},{6,54},{7,55},{8,56},{9,... | collective-permute-start | bytes 884744 | tf_op jit(solution)/shard_map/keys_x/ppermute | solution.py:52
  30.9 2.5 %collective-permute-start.1 = (bf16[1152,128]{1,0:T(8,128)(2,1)S(1)}, bf16[1152,128]{1,0:T(8,128)(2,1)S(1)}, u32[]{:S(2)}, u32[]{:S(2)}) collective-permute-start(bf16[1152,128]{1,0:T(8,128)(2,1)S(1)} %pad_maximum_fusion.refs_0_), channel_id=1, source_target_pairs={{0,16},{1,17},{2,18},{3,19},{4,20},{5,21},{6,22},{7,23},{8,24},{9,... | collective-permute-start | bytes 884744 | tf_op jit(solution)/shard_map/keys_x/ppermute | solution.py:52
  33.5 0.0 copy-done.2
  33.5 0.1 copy.10.gain_ref
  33.6 0.0 copy-done.3
  33.6 0.1 copy.11.gain_tangent_ref
  33.8 0.4 collective-permute-done.2.refs_2_
  34.2 7.0 %collective-permute-done.3.refs_3_ = bf16[1152,128]{1,0:T(8,128)(2,1)S(1)} collective-permute-done((bf16[1152,128]{1,0:T(8,128)(2,1)S(1)}, bf16[1152,128]{1,0:T(8,128)(2,1)S(1)}, u32[]{:S(2)}, u32[]{:S(2)}) %collective-permute-start.3) | collective-permute-done | bytes 294944 | tf_op jit(solution)/shard_map/keys_x/ppermute | solution.py:52
  41.2 0.0 collective-permute-done.1.refs_1_
  41.2 0.7 make_keys.1.keys_ref
  41.9 0.9 all-to-all-done
  42.8 1.7 %local_stats.1 = f32[16,8,256]{2,1,0:T(8,128)S(1)} custom-call(s32[5]{0:T(128)S(1)} %stack.16.place_ref, bf16[4,576,256]{2,1,0:T(8,128)(2,1)S(1)} %make_keys.1.keys_ref, bf16[256,1088]{1,0:T(8,128)(2,1)S(1)} %bitcast.18), custom_call_target="tpu_custom_call" | custom-call | flops 570425344 | bytes 3145728 | tf_op jit(solution)/shard_map/local_stats/pallas_call | solution.py:289
  44.6 21.4 %all_to_all.20.parts_ref = f32[16,8,256]{2,1,0:T(8,128)S(1)} all-to-all(f32[16,8,256]{2,1,0:T(8,128)S(1)} %local_stats.1), channel_id=1, replica_groups={{0,1,2,3,4,5,6,7,8,9,10,11,12,13,14,15},{16,17,18,19,20,21,22,23,24,25,..., dimensions={0} | all-to-all | bytes 262144 | tf_op jit(solution)/shard_map/stats_yz/all_to_all | solution.py:56
  65.9 3.8 %gradients.1 = (f32[4,1088,128]{2,1,0:T(8,128)S(1)}, f32[16,8,128]{2,1,0:T(8,128)}) custom-call(s32[5]{0:T(128)S(1)} %stack.16.place_ref, f32[16,8,256]{2,1,0:T(8,128)S(1)} %all_to_all.20.parts_ref, bf16[4,576,256]{2,1,0:T(8,128)(2,1)S(1)} %make_keys.1.keys_ref, bf16[256,1088]{1,0:T(8,128)(2,1)S(1)} %bitcast.19, ...), custom_call_target="tpu_custom_call" | custom-call | flops 1140850688 | bytes 6291456 | tf_op jit(solution)/shard_map/gradients/pallas_call | solution.py:303
  69.8 0.0 copy-start
  69.8 1.4 %copy-done = f32[4,1088,128]{2,1,0:T(8,128)} copy-done((f32[4,1088,128]{2,1,0:T(8,128)}, f32[4,1088,128]{2,1,0:T(8,128)S(1)}, u32[]{:S(2)}) %copy-start) | copy-done | bytes 2228248
  71.1 9.1 %all-to-all-start.2 = ((f32[16,8,128]{2,1,0:T(8,128)}), f32[16,8,128]{2,1,0:T(8,128)S(1)}, u32[]{:S(2)}, u32[]{:S(2)}) async-start(f32[16,8,128]{2,1,0:T(8,128)} %get-tuple-element.17), calls=%async_computation.2 | async-start | bytes 131072 | tf_op jit(solution)/shard_map/pair_column/all_to_all | solution.py:56
  80.3 0.0 copy-start.1
  80.3 1.6 %copy-done.1 = f32[4,1088,128]{2,1,0:T(8,128)S(1)} copy-done((f32[4,1088,128]{2,1,0:T(8,128)S(1)}, f32[4,1088,128]{2,1,0:T(8,128)}, u32[]{:S(2)}) %copy-start.1) | copy-done | bytes 2228248
  81.9 1.0 row_shares.1
  82.9 3.4 %collective-permute-start.4 = (f32[576,128]{1,0:T(8,128)S(1)}, f32[576,128]{1,0:T(8,128)S(1)}, u32[]{:S(2)}, u32[]{:S(2)}) collective-permute-start(f32[576,128]{1,0:T(8,128)S(1)} %get-tuple-element.14), channel_id=1, source_target_pairs={{0,48},{1,49},{2,50},{3,51},{4,52},{5,53},{6,54},{7,55},{8,56},{9,... | collective-permute-start | bytes 884744 | tf_op jit(solution)/shard_map/shares_x/ppermute | solution.py:52
  86.4 2.5 %collective-permute-start.5 = (f32[576,128]{1,0:T(8,128)S(1)}, f32[576,128]{1,0:T(8,128)S(1)}, u32[]{:S(2)}, u32[]{:S(2)}) collective-permute-start(f32[576,128]{1,0:T(8,128)S(1)} %get-tuple-element.15), channel_id=1, source_target_pairs={{0,32},{1,33},{2,34},{3,35},{4,36},{5,37},{6,38},{7,39},{8,40},{9,... | collective-permute-start | bytes 884744 | tf_op jit(solution)/shard_map/shares_x/ppermute | solution.py:52
  88.8 2.4 %collective-permute-start.6 = (f32[576,128]{1,0:T(8,128)S(1)}, f32[576,128]{1,0:T(8,128)S(1)}, u32[]{:S(2)}, u32[]{:S(2)}) collective-permute-start(f32[576,128]{1,0:T(8,128)S(1)} %get-tuple-element.16), channel_id=1, source_target_pairs={{0,16},{1,17},{2,18},{3,19},{4,20},{5,21},{6,22},{7,23},{8,24},{9,... | collective-permute-start | bytes 884744 | tf_op jit(solution)/shard_map/shares_x/ppermute | solution.py:52
  91.3 0.0 all-to-all-done.2.parts_ref
  91.3 0.7 add_pair.1
  91.9 4.4 %all-to-all-start.3 = ((f32[32,8,128]{2,1,0:T(8,128)}), f32[32,8,128]{2,1,0:T(8,128)S(1)}, u32[]{:S(2)}, u32[]{:S(2)}) async-start(f32[32,8,128]{2,1,0:T(8,128)} %add_pair.1), calls=%async_computation.3 | async-start | bytes 262144 | tf_op jit(solution)/shard_map/pair_plane/all_to_all | solution.py:56
  96.4 0.0 collective-permute-done.4
  96.4 1.7 %collective-permute-done.5 = f32[576,128]{1,0:T(8,128)S(1)} collective-permute-done((f32[576,128]{1,0:T(8,128)S(1)}, f32[576,128]{1,0:T(8,128)S(1)}, u32[]{:S(2)}, u32[]{:S(2)}) %collective-permute-start.5) | collective-permute-done | bytes 294944 | tf_op jit(solution)/shard_map/shares_x/ppermute | solution.py:52
  98.1 8.1 %collective-permute-done.6 = f32[576,128]{1,0:T(8,128)S(1)} collective-permute-done((f32[576,128]{1,0:T(8,128)S(1)}, f32[576,128]{1,0:T(8,128)S(1)}, u32[]{:S(2)}, u32[]{:S(2)}) %collective-permute-start.6) | collective-permute-done | bytes 294944 | tf_op jit(solution)/shard_map/shares_x/ppermute | solution.py:52
  106.1 0.8 add_bitcast_fusion
  106.9 0.0 all-to-all-done.3
  106.9 0.6 reshape.21
  (1 shorter events, 0.0 us)
Async XLA Ops:
  0.6 32.8 %copy-start.2 = (f32[512]{0:T(512)S(1)}, f32[512]{0:T(512)}, u32[]{:S(2)}) copy-start(f32[512]{0:T(512)} %param.14) | copy-start | bytes 6148
  0.6 33.0 %copy-start.3 = (f32[512]{0:T(512)S(1)}, f32[512]{0:T(512)}, u32[]{:S(2)}) copy-start(f32[512]{0:T(512)} %param.15) | copy-start | bytes 6148
  1.4 13.9 %collective-permute-start = (bf16[16,1088]{1,0:T(8,128)(2,1)S(1)}, bf16[16,1088]{1,0:T(8,128)(2,1)S(1)}, u32[]{:S(2)}, u32[]{:S(2)}) collective-permute-start(bf16[16,1088]{1,0:T(8,128)(2,1)S(1)} %pad_maximum_fusion.1.own_ref), channel_id=1, source_target_pairs={{0,1},{1,0},{2,3},{3,2},{4,5},{5,4},{6,7},{7,6},{8,9},{9,8},{10,11... | collective-permute-start | bytes 104456 | tf_op jit(solution)/shard_map/rows_z/ppermute | solution.py:52
  16.7 26.1 %all-to-all-start = ((bf16[8,2,16,1088]{3,2,1,0:T(8,128)(2,1)}), bf16[8,2,16,1088]{3,2,1,0:T(8,128)(2,1)S(1)}, u32[]{:S(2)}, u32[]{:S(2)}) async-start(bf16[8,2,16,1088]{3,2,1,0:T(8,128)(2,1)} %pair_rows.1), calls=%async_computation | async-start | bytes 1179648 | tf_op jit(solution)/shard_map/rows_y/all_to_all | solution.py:56
  23.5 10.6 %collective-permute-start.2 = (bf16[1152,128]{1,0:T(8,128)(2,1)S(1)}, bf16[1152,128]{1,0:T(8,128)(2,1)S(1)}, u32[]{:S(2)}, u32[]{:S(2)}) collective-permute-start(bf16[1152,128]{1,0:T(8,128)(2,1)S(1)} %pad_maximum_fusion.refs_0_), channel_id=1, source_target_pairs={{0,32},{1,33},{2,34},{3,35},{4,36},{5,37},{6,38},{7,39},{8,40},{9,... | collective-permute-start | bytes 884744 | tf_op jit(solution)/shard_map/keys_x/ppermute | solution.py:52
  28.2 13.0 %collective-permute-start.3 = (bf16[1152,128]{1,0:T(8,128)(2,1)S(1)}, bf16[1152,128]{1,0:T(8,128)(2,1)S(1)}, u32[]{:S(2)}, u32[]{:S(2)}) collective-permute-start(bf16[1152,128]{1,0:T(8,128)(2,1)S(1)} %pad_maximum_fusion.refs_0_), channel_id=1, source_target_pairs={{0,48},{1,49},{2,50},{3,51},{4,52},{5,53},{6,54},{7,55},{8,56},{9,... | collective-permute-start | bytes 884744 | tf_op jit(solution)/shard_map/keys_x/ppermute | solution.py:52
  30.9 10.3 %collective-permute-start.1 = (bf16[1152,128]{1,0:T(8,128)(2,1)S(1)}, bf16[1152,128]{1,0:T(8,128)(2,1)S(1)}, u32[]{:S(2)}, u32[]{:S(2)}) collective-permute-start(bf16[1152,128]{1,0:T(8,128)(2,1)S(1)} %pad_maximum_fusion.refs_0_), channel_id=1, source_target_pairs={{0,16},{1,17},{2,18},{3,19},{4,20},{5,21},{6,22},{7,23},{8,24},{9,... | collective-permute-start | bytes 884744 | tf_op jit(solution)/shard_map/keys_x/ppermute | solution.py:52
  69.8 1.4 %copy-start = (f32[4,1088,128]{2,1,0:T(8,128)}, f32[4,1088,128]{2,1,0:T(8,128)S(1)}, u32[]{:S(2)}) copy-start(f32[4,1088,128]{2,1,0:T(8,128)S(1)} %get-tuple-element.12.grads_ref) | copy-start | bytes 6684676
  71.1 20.1 %all-to-all-start.2 = ((f32[16,8,128]{2,1,0:T(8,128)}), f32[16,8,128]{2,1,0:T(8,128)S(1)}, u32[]{:S(2)}, u32[]{:S(2)}) async-start(f32[16,8,128]{2,1,0:T(8,128)} %get-tuple-element.17), calls=%async_computation.2 | async-start | bytes 131072 | tf_op jit(solution)/shard_map/pair_column/all_to_all | solution.py:56
  80.3 1.6 %copy-start.1 = (f32[4,1088,128]{2,1,0:T(8,128)S(1)}, f32[4,1088,128]{2,1,0:T(8,128)}, u32[]{:S(2)}) copy-start(f32[4,1088,128]{2,1,0:T(8,128)} %copy-done) | copy-start | bytes 6684676
  82.9 13.5 %collective-permute-start.4 = (f32[576,128]{1,0:T(8,128)S(1)}, f32[576,128]{1,0:T(8,128)S(1)}, u32[]{:S(2)}, u32[]{:S(2)}) collective-permute-start(f32[576,128]{1,0:T(8,128)S(1)} %get-tuple-element.14), channel_id=1, source_target_pairs={{0,48},{1,49},{2,50},{3,51},{4,52},{5,53},{6,54},{7,55},{8,56},{9,... | collective-permute-start | bytes 884744 | tf_op jit(solution)/shard_map/shares_x/ppermute | solution.py:52
  86.4 11.7 %collective-permute-start.5 = (f32[576,128]{1,0:T(8,128)S(1)}, f32[576,128]{1,0:T(8,128)S(1)}, u32[]{:S(2)}, u32[]{:S(2)}) collective-permute-start(f32[576,128]{1,0:T(8,128)S(1)} %get-tuple-element.15), channel_id=1, source_target_pairs={{0,32},{1,33},{2,34},{3,35},{4,36},{5,37},{6,38},{7,39},{8,40},{9,... | collective-permute-start | bytes 884744 | tf_op jit(solution)/shard_map/shares_x/ppermute | solution.py:52
  88.8 17.3 %collective-permute-start.6 = (f32[576,128]{1,0:T(8,128)S(1)}, f32[576,128]{1,0:T(8,128)S(1)}, u32[]{:S(2)}, u32[]{:S(2)}) collective-permute-start(f32[576,128]{1,0:T(8,128)S(1)} %get-tuple-element.16), channel_id=1, source_target_pairs={{0,16},{1,17},{2,18},{3,19},{4,20},{5,21},{6,22},{7,23},{8,24},{9,... | collective-permute-start | bytes 884744 | tf_op jit(solution)/shard_map/shares_x/ppermute | solution.py:52
  91.9 14.9 %all-to-all-start.3 = ((f32[32,8,128]{2,1,0:T(8,128)}), f32[32,8,128]{2,1,0:T(8,128)S(1)}, u32[]{:S(2)}, u32[]{:S(2)}) async-start(f32[32,8,128]{2,1,0:T(8,128)} %add_pair.1), calls=%async_computation.3 | async-start | bytes 262144 | tf_op jit(solution)/shard_map/pair_plane/all_to_all | solution.py:56

commit v6 on v3

--- a/solution.py
+++ b/solution.py
@@ -17,6 +17,8 @@
 Z = ZH * ZL
 LANES = 128
 SUBLANES = 8
+SUMS = 5
+MIB = 2**20
 
 
 def ctx_index(x, y, zh):
@@ -139,29 +141,40 @@
         sums[2] += weights * value_grad
         sums[3] += weights * (score_dot * value_grad + value_dot)
     sums = as_rows([maxima] + [jnp.sum(each, axis=1, keepdims=True) for each in sums])
-    for copy in range(out_ref.shape[0]):
-        out_ref[copy] = sums
+    for row in range(SUMS):
+        values = sums[row : row + 1]
+        values = jnp.concatenate([values[:, :LANES], values[:, LANES:]], axis=0)
+        for copy in range(out_ref.shape[0]):
+            out_ref[copy, row] = values
 
 
 def merged_means(parts_ref):
     count = parts_ref.shape[0]
-    maxima = functools.reduce(jnp.maximum, [parts_ref[at, 0:1, :] for at in range(count)])
-    sums = sum(jnp.exp(parts_ref[at, 0:1, :] - maxima) * parts_ref[at] for at in range(count))
-    inv_totals = 1.0 / sums[1:2]
-    shift_mean = sums[2:3] * inv_totals
-    grad_mean = sums[3:4] * inv_totals
-    grad_mean_dot = (sums[4:5] - shift_mean * sums[3:4]) * inv_totals
-    rows = [maxima, inv_totals, shift_mean, grad_mean, grad_mean_dot]
-    rows.append(jnp.zeros((LANES - len(rows), maxima.shape[1]), jnp.float32))
+    maxima = functools.reduce(jnp.maximum, [parts_ref[at, 0] for at in range(count)])
+    scales = [jnp.exp(parts_ref[at, 0] - maxima) for at in range(count)]
+    sums = [
+        sum(scales[at] * parts_ref[at, row] for at in range(count)) for row in range(1, SUMS)
+    ]
+    inv_totals = 1.0 / sums[0]
+    shift_mean = sums[1] * inv_totals
+    grad_mean = sums[2] * inv_totals
+    grad_mean_dot = (sums[3] - shift_mean * sums[2]) * inv_totals
+    rows = [
+        jnp.concatenate([values[0:1], values[1:2]], axis=1)
+        for values in (maxima, inv_totals, shift_mean, grad_mean, grad_mean_dot)
+    ]
+    rows.append(jnp.zeros((LANES - SUMS, 2 * LANES), jnp.float32))
     columns = jnp.concatenate(rows, axis=0).T
-    return [columns[:, at : at + 1] for at in range(5)]
-
-
-def grads_kernel(slab, place_ref, parts_ref, keys_ref, rows_ref, turned_ref, *refs):
+    return [columns[:, at : at + 1] for at in range(SUMS)]
+
+
+def grads_kernel(slab, place_ref, parts_ref, keys_ref, rows_ref, *refs):
     gain_ref, gain_tangent_ref, block_refs = refs[0], refs[1], refs[2 : 2 + X]
-    share_refs, pair_ref = refs[2 + X : 2 + 2 * X], refs[-1]
+    share_refs, pair_ref = refs[2 + X : -1], refs[-1]
     latent_width = gain_ref.shape[0]
     norm_gain, gain_tangent = gain_ref[...], gain_tangent_ref[...]
+    turned_cot = rows_ref[:, :latent_width].T
+    turned_query = rows_ref[:, latent_width:].T
     maxima, inv_totals, shift_mean, grad_mean, grad_mean_dot = merged_means(parts_ref)
     gain_grad = gain_grad_dot = 0.0
     for behind in range(X):
@@ -174,9 +187,9 @@
         score_grad = attention * centred
         score_grad_dot = attention_dot * centred + attention * (value_dot - grad_mean_dot)
         right = jnp.concatenate([score_grad, score_grad_dot], axis=1).astype(jnp.bfloat16)
-        by_query = score_scale * dot(turned_ref[latent_width:, :], right)
+        by_query = score_scale * dot(turned_query, right)
         right = jnp.concatenate([attention, attention_dot], axis=1).astype(jnp.bfloat16)
-        by_cot = dot(turned_ref[:latent_width, :], right)
+        by_cot = dot(turned_cot, right)
 
         key_count = scores.shape[1]
         latent_grad = by_query[:latent_width, :key_count] + by_cot[:, :key_count]
@@ -231,7 +244,6 @@
     packed_width = latent_width + full_width
     row_count = Y * ZH * slab
     smem = [pl.BlockSpec(memory_space=pltpu.SMEM)]
-    limit = pltpu.CompilerParams(vmem_limit_bytes=40 * 2**20)
     flops = 4 * X * key_count * row_count * packed_width
     ctx_at = lax.axis_index("ctx").astype(jnp.int32)
     place = jnp.stack(
@@ -253,33 +265,36 @@
             out_shape=jax.ShapeDtypeStruct((Y, ZH, slab, packed_width), packed.dtype),
             in_specs=smem + in_vmem(2),
             out_specs=pl.BlockSpec(memory_space=pltpu.VMEM),
+            compiler_params=pltpu.CompilerParams(vmem_limit_bytes=4 * MIB),
             name="pair_rows",
         )(place, packed, ctx_permute(packed, dz=1))
     with jax.named_scope("rows_y"):
         block = jnp.concatenate([kv_rows[0].T, kv_tangent[0].T], axis=0)
-        block, copies = lax.optimization_barrier((block, copies))
+        near_block, copies = lax.optimization_barrier((block, copies))
         rows = exchange(copies, "ctx", Y_GROUPS).reshape(row_count, packed_width)
 
     with jax.named_scope("keys_x"):
-        blocks = [block] + [ctx_permute(block, dx=step) for step in range(1, X)]
+        far_block = ctx_permute(block, dx=2)
+        near_blocks = [ctx_permute(near_block, dx=step) for step in (1, -1)]
+        blocks = [block, near_blocks[0], far_block, near_blocks[1]]
     gains = (norm_gain[:, None], gain_tangent[:, None])
     keys = pl.pallas_call(
         keys_kernel,
         out_shape=jax.ShapeDtypeStruct((X, full_width, 2 * key_count), jnp.bfloat16),
         in_specs=in_vmem(2 + X),
         out_specs=pl.BlockSpec(memory_space=pltpu.VMEM),
-        compiler_params=limit,
+        compiler_params=pltpu.CompilerParams(vmem_limit_bytes=8 * MIB),
         name="make_keys",
     )(*gains, *blocks)
 
     sums = pl.pallas_call(
         functools.partial(stats_kernel, slab),
-        out_shape=jax.ShapeDtypeStruct((Y * ZH, SUBLANES, row_count), jnp.float32),
+        out_shape=jax.ShapeDtypeStruct((Y * ZH, SUMS, row_count // LANES, LANES), jnp.float32),
         in_specs=smem + in_vmem(2),
         out_specs=pl.BlockSpec(memory_space=pltpu.VMEM),
-        compiler_params=limit,
+        compiler_params=pltpu.CompilerParams(vmem_limit_bytes=12 * MIB),
         cost_estimate=pl.CostEstimate(
-            flops=flops, bytes_accessed=3 * 2**20, transcendentals=X * key_count * row_count
+            flops=flops, bytes_accessed=3 * MIB, transcendentals=X * key_count * row_count
         ),
         name="local_stats",
     )(place, keys, rows)
@@ -289,26 +304,30 @@
     *shares, pair = pl.pallas_call(
         functools.partial(grads_kernel, slab),
         out_shape=[jax.ShapeDtypeStruct((full_width, key_count), jnp.float32)] * X
-        + [jax.ShapeDtypeStruct((Z * CORE, SUBLANES, LANES), jnp.float32)],
-        in_specs=smem + in_vmem(6 + X),
+        + [jax.ShapeDtypeStruct((X * Y, SUBLANES, LANES), jnp.float32)],
+        in_specs=smem + in_vmem(5 + X),
         out_specs=in_vmem(X + 1),
-        compiler_params=limit,
+        compiler_params=pltpu.CompilerParams(vmem_limit_bytes=16 * MIB),
         cost_estimate=pl.CostEstimate(
-            flops=2 * flops, bytes_accessed=4 * 2**20, transcendentals=X * key_count * row_count
+            flops=2 * flops, bytes_accessed=6 * MIB, transcendentals=X * key_count * row_count
         ),
         name="gradients",
-    )(place, sums, keys, rows, rows.T, *gains, *blocks)
+    )(place, sums, keys, rows, *gains, *blocks)
 
     with jax.named_scope("shares_x"):
-        hv_rows = sum([ctx_permute(shares[step], dx=-step) for step in range(1, X)], shares[0])
-    with jax.named_scope("pair_column"):
+        hv_rows = sum([ctx_permute(shares[step], dx=-step) for step in (2, 3, 1)], shares[0])
+    with jax.named_scope("pair_plane"):
         pair = pl.pallas_call(
             add_kernel,
-            out_shape=jax.ShapeDtypeStruct((X * Y, SUBLANES, LANES), jnp.float32),
+            out_shape=jax.ShapeDtypeStruct((Z * CORE, SUBLANES, LANES), jnp.float32),
+            compiler_params=pltpu.CompilerParams(vmem_limit_bytes=2 * MIB),
+            cost_estimate=pl.CostEstimate(
+                flops=10**11, bytes_accessed=MIB // 4, transcendentals=0
+            ),
             name="add_pair",
-        )(exchange(pair, ("dp", "ctx"), COLUMNS))
-    with jax.named_scope("pair_plane"):
-        pair = jnp.sum(exchange(pair, ("dp", "ctx"), PLANES), axis=0).reshape(2, latent_width)
+        )(exchange(pair, ("dp", "ctx"), PLANES))
+    with jax.named_scope("pair_column"):
+        pair = jnp.sum(exchange(pair, ("dp", "ctx"), COLUMNS), axis=0).reshape(2, latent_width)
     return (hv_rows.T[None], pair)
 
 

time: 123 us -> 107 us (0.87)
  waiting for transfers between devices: 33.1 us -> 15.4 us
  blocking collectives: 15.5 us -> 20.8 us
  starting transfers between devices: 49.8 us -> 53.5 us
  local copies, waits for them, and re-layouts: 6.75 us -> 3.78 us
  Pallas kernels: 10.9 us -> 8.02 us
    all_to_all x3, waiting for transfers between devices: 19.8 us -> 7.92 us  [exchange(): return lax.all_to_all(copies, axis, 0, 0, axis_index_groups=groups)]
    ppermute x7, waiting for transfers between devices: 13.4 us -> 7.43 us  [ctx_permute(): return lax.ppermute(value, 'ctx', pairs)]
    all_to_all x1, blocking collectives: 15.5 us -> 20.8 us  [exchange(): return lax.all_to_all(copies, axis, 0, 0, axis_index_groups=groups)]
    ppermute x7, starting transfers between devices: 28 us -> 32.5 us  [ctx_permute(): return lax.ppermute(value, 'ctx', pairs)]
    unnamed x22 -> x16, local copies, waits for them, and re-layouts: 4.95 us -> 2.81 us
  transfers between devices with their start and end apart: 10 -> 10, of which waited for: 5 -> 4; matrix products, arithmetic and copies ran while one was open for 3% -> 2% of each run, Pallas kernels for 2% -> 1%
where the time goes in v6:
time: 107 us; the launch traced here: 106 us
  starting transfers between devices  53.5 us (50%)
  blocking collectives  20.8 us (19%)
  waiting for transfers between devices  15.4 us (14%)
  Pallas kernels  8.02 us (7%)
  local copies, waits for them, and re-layouts  3.78 us (4%)
  other arithmetic  2.54 us (2%)
  between operations  2.13 us (2%)
    ppermute x7, starting transfers between devices, ctx_permute(): return lax.ppermute(value, 'ctx', pairs)  32.5 us
    all_to_all x3, starting transfers between devices, exchange(): return lax.all_to_all(copies, axis, 0, 0, axis_index_groups=groups)  21 us
    all_to_all x1, blocking collectives, exchange(): return lax.all_to_all(copies, axis, 0, 0, axis_index_groups=groups)  20.8 us
    all_to_all x3, waiting for transfers between devices, exchange(): return lax.all_to_all(copies, axis, 0, 0, axis_index_groups=groups)  7.92 us
    ppermute x7, waiting for transfers between devices, ctx_permute(): return lax.ppermute(value, 'ctx', pairs)  7.43 us
    pallas_call x1, Pallas kernels, shards(): pl.pallas_call(functools.partial(grads_kernel, slab), out_shape=[jax.Shap...  3.49 us
    unnamed x16, local copies, waits for them, and re-layouts  2.81 us
  transfers between devices with their start and end apart: 10, of which 4 were waited for; matrix products, arithmetic and copies ran while one was open for 2% of the time, Pallas kernels for 1%

profile of v6, /device:TPU:1, one launch (start us, length us, event | category | flops | bytes accessed | tf_op | source)
XLA Modules:
  0.0 106.2 jit_solution(8044586539375511393)
XLA Ops:
  0.6 0.7 pad_maximum_fusion.1.own_ref
  1.4 11.5 %collective-permute-start = (bf16[16,1088]{1,0:T(8,128)(2,1)S(1)}, bf16[16,1088]{1,0:T(8,128)(2,1)S(1)}, u32[]{:S(2)}, u32[]{:S(2)}) collective-permute-start(bf16[16,1088]{1,0:T(8,128)(2,1)S(1)} %pad_maximum_fusion.1.own_ref), channel_id=1, source_target_pairs={{0,1},{1,0},{2,3},{3,2},{4,5},{5,4},{6,7},{7,6},{8,9},{9,8},{10,11... | collective-permute-start | bytes 104456 | tf_op jit(solution)/shard_map/rows_z/ppermute | solution.py:53
  12.8 0.0 copy-start.6
  12.8 1.0 pad_maximum_fusion.refs_0_.refs_2_
  13.9 0.0 copy-start.7
  15.2 0.1 stack.16.place_ref
  15.3 0.0 collective-permute-done.other_ref
  15.3 1.4 %pair_rows.1 = bf16[8,2,16,1088]{3,2,1,0:T(8,128)(2,1)} custom-call(s32[5]{0:T(128)S(1)} %stack.16.place_ref, bf16[16,1088]{1,0:T(8,128)(2,1)S(1)} %pad_maximum_fusion.1.own_ref, bf16[16,1088]{1,0:T(8,128)(2,1)S(1)} %collective-permute-done.other_ref), custom_call_target="tpu_custom_call" | custom-call | tf_op jit(solution)/shard_map/rows_z/pair_rows/pallas_call | solution.py:263
  16.7 6.8 %all-to-all-start = ((bf16[8,2,16,1088]{3,2,1,0:T(8,128)(2,1)}), bf16[8,2,16,1088]{3,2,1,0:T(8,128)(2,1)S(1)}, u32[]{:S(2)}, u32[]{:S(2)}) async-start(bf16[8,2,16,1088]{3,2,1,0:T(8,128)(2,1)} %pair_rows.1), calls=%async_computation | async-start | bytes 1179648 | tf_op jit(solution)/shard_map/rows_y/all_to_all | solution.py:57
  23.5 4.6 %collective-permute-start.2 = (bf16[1152,128]{1,0:T(8,128)(2,1)S(1)}, bf16[1152,128]{1,0:T(8,128)(2,1)S(1)}, u32[]{:S(2)}, u32[]{:S(2)}) collective-permute-start(bf16[1152,128]{1,0:T(8,128)(2,1)S(1)} %pad_maximum_fusion.refs_0_.refs_2_), channel_id=1, source_target_pairs={{0,32},{1,33},{2,34},{3,35},{4,36},{5,37},{6,38},{7,39},{8,40},{9,... | collective-permute-start | bytes 884744 | tf_op jit(solution)/shard_map/keys_x/ppermute | solution.py:53
  28.2 2.8 %collective-permute-start.3 = (bf16[1152,128]{1,0:T(8,128)(2,1)S(1)}, bf16[1152,128]{1,0:T(8,128)(2,1)S(1)}, u32[]{:S(2)}, u32[]{:S(2)}) collective-permute-start(bf16[1152,128]{1,0:T(8,128)(2,1)S(1)} %pad_maximum_fusion.refs_0_.refs_2_), channel_id=1, source_target_pairs={{0,48},{1,49},{2,50},{3,51},{4,52},{5,53},{6,54},{7,55},{8,56},{9,... | collective-permute-start | bytes 884744 | tf_op jit(solution)/shard_map/keys_x/ppermute | solution.py:53
  30.9 2.5 %collective-permute-start.1 = (bf16[1152,128]{1,0:T(8,128)(2,1)S(1)}, bf16[1152,128]{1,0:T(8,128)(2,1)S(1)}, u32[]{:S(2)}, u32[]{:S(2)}) collective-permute-start(bf16[1152,128]{1,0:T(8,128)(2,1)S(1)} %pad_maximum_fusion.refs_0_.refs_2_), channel_id=1, source_target_pairs={{0,16},{1,17},{2,18},{3,19},{4,20},{5,21},{6,22},{7,23},{8,24},{9,... | collective-permute-start | bytes 884744 | tf_op jit(solution)/shard_map/keys_x/ppermute | solution.py:53
  33.5 0.0 copy-done.6
  33.5 0.1 copy.10.gain_ref.refs_0_
  33.6 0.0 copy-done.7
  33.6 0.1 copy.11.gain_tangent_ref.refs_1_
  33.8 0.4 collective-permute-done.2.refs_2_.refs_4_
  34.2 7.0 %collective-permute-done.3.refs_3_.refs_5_ = bf16[1152,128]{1,0:T(8,128)(2,1)S(1)} collective-permute-done((bf16[1152,128]{1,0:T(8,128)(2,1)S(1)}, bf16[1152,128]{1,0:T(8,128)(2,1)S(1)}, u32[]{:S(2)}, u32[]{:S(2)}) %collective-permute-start.3) | collective-permute-done | bytes 294944 | tf_op jit(solution)/shard_map/keys_x/ppermute | solution.py:53
  41.2 0.0 collective-permute-done.1.refs_1_.refs_3_
  41.2 0.0 copy-start
  41.2 0.7 make_keys.1.keys_ref
  41.9 0.0 copy-done
  41.9 0.9 all-to-all-done
  42.8 0.0 copy-start.1
  42.8 1.8 %local_stats.1 = f32[16,5,2,128]{3,2,1,0:T(2,128)S(1)} custom-call(s32[5]{0:T(128)S(1)} %stack.16.place_ref, bf16[4,576,256]{2,1,0:T(8,128)(2,1)S(1)} %make_keys.1.keys_ref, bf16[256,1088]{1,0:T(8,128)(2,1)S(1)} %bitcast.18), custom_call_target="tpu_custom_call" | custom-call | flops 570425344 | bytes 3145728 | tf_op jit(solution)/shard_map/local_stats/pallas_call | solution.py:290
  44.6 20.8 %all_to_all.20.parts_ref = f32[16,5,2,128]{3,2,1,0:T(2,128)S(1)} all-to-all(f32[16,5,2,128]{3,2,1,0:T(2,128)S(1)} %local_stats.1), channel_id=1, replica_groups={{0,1,2,3,4,5,6,7,8,9,10,11,12,13,14,15},{16,17,18,19,20,21,22,23,24,25,..., dimensions={0} | all-to-all | bytes 163840 | tf_op jit(solution)/shard_map/stats_yz/all_to_all | solution.py:57
  65.4 0.0 copy-done.1
  65.4 3.5 %gradients.1 = (f32[576,128]{1,0:T(8,128)S(1)}, f32[576,128]{1,0:T(8,128)S(1)}, f32[576,128]{1,0:T(8,128)S(1)}, f32[576,128]{1,0:T(8,128)S(1)}, f32[32,8,128]{2,1,0:T(8,128)S(1)}) custom-call(s32[5]{0:T(128)S(1)} %stack.16.place_ref, f32[16,5,2,128]{3,2,1,0:T(2,128)S(1)} %all_to_all.20.parts_ref, bf16[4,576,256]{2,1,0:T(8,128)(2,1)S(1)} %make_keys.1.keys_ref, ...), custom_call_target="tpu_custom_call" | custom-call | flops 1140850688 | bytes 6291456 | tf_op jit(solution)/shard_map/gradients/pallas_call | solution.py:304
  68.9 0.0 copy-start.2
  68.9 0.7 copy-done.2
  69.6 0.0 copy-start.3
  69.6 0.7 copy-done.3
  70.3 0.0 copy-start.4
  70.3 0.7 copy-done.4
  71.0 0.7 copy-done.5
  71.7 5.5 %all-to-all-start.2 = ((f32[32,8,128]{2,1,0:T(8,128)}), f32[32,8,128]{2,1,0:T(8,128)S(1)}, u32[]{:S(2)}, u32[]{:S(2)}) async-start(f32[32,8,128]{2,1,0:T(8,128)} %copy-done.2), calls=%async_computation.2 | async-start | bytes 262144 | tf_op jit(solution)/shard_map/pair_plane/all_to_all | solution.py:57
  77.2 4.6 %collective-permute-start.4 = (f32[576,128]{1,0:T(8,128)}, f32[576,128]{1,0:T(8,128)S(1)}, u32[]{:S(2)}, u32[]{:S(2)}) collective-permute-start(f32[576,128]{1,0:T(8,128)} %copy-done.5), channel_id=1, source_target_pairs={{0,32},{1,33},{2,34},{3,35},{4,36},{5,37},{6,38},{7,39},{8,40},{9,... | collective-permute-start | bytes 884744 | tf_op jit(solution)/shard_map/shares_x/ppermute | solution.py:53
  81.9 2.2 %collective-permute-start.5 = (f32[576,128]{1,0:T(8,128)}, f32[576,128]{1,0:T(8,128)S(1)}, u32[]{:S(2)}, u32[]{:S(2)}) collective-permute-start(f32[576,128]{1,0:T(8,128)} %copy-done.4), channel_id=1, source_target_pairs={{0,16},{1,17},{2,18},{3,19},{4,20},{5,21},{6,22},{7,23},{8,24},{9,... | collective-permute-start | bytes 884744 | tf_op jit(solution)/shard_map/shares_x/ppermute | solution.py:53
  84.1 4.3 %collective-permute-start.6 = (f32[576,128]{1,0:T(8,128)}, f32[576,128]{1,0:T(8,128)S(1)}, u32[]{:S(2)}, u32[]{:S(2)}) collective-permute-start(f32[576,128]{1,0:T(8,128)} %copy-done.3), channel_id=1, source_target_pairs={{0,48},{1,49},{2,50},{3,51},{4,52},{5,53},{6,54},{7,55},{8,56},{9,... | collective-permute-start | bytes 884744 | tf_op jit(solution)/shard_map/shares_x/ppermute | solution.py:53
  88.4 0.0 all-to-all-done.2.parts_ref
  88.4 0.7 add_pair.1
  89.1 8.7 %all-to-all-start.3 = ((f32[16,8,128]{2,1,0:T(8,128)}), f32[16,8,128]{2,1,0:T(8,128)S(1)}, u32[]{:S(2)}, u32[]{:S(2)}) async-start(f32[16,8,128]{2,1,0:T(8,128)} %add_pair.1), calls=%async_computation.3 | async-start | bytes 131072 | tf_op jit(solution)/shard_map/pair_column/all_to_all | solution.py:57
  97.8 0.0 collective-permute-done.4
  97.8 0.0 collective-permute-done.5
  97.8 0.0 collective-permute-done.6
  97.8 0.8 add_bitcast_fusion
  98.6 7.0 %all-to-all-done.3 = f32[16,8,128]{2,1,0:T(8,128)S(1)} async-done(((f32[16,8,128]{2,1,0:T(8,128)}), f32[16,8,128]{2,1,0:T(8,128)S(1)}, u32[]{:S(2)}, u32[]{:S(2)}) %all-to-all-start.3) | async-done | bytes 65568 | tf_op jit(solution)/shard_map/pair_column/all_to_all | solution.py:57
  105.6 0.6 reshape.21
  (2 shorter events, 0.0 us)
Async XLA Ops:
  1.4 13.9 %collective-permute-start = (bf16[16,1088]{1,0:T(8,128)(2,1)S(1)}, bf16[16,1088]{1,0:T(8,128)(2,1)S(1)}, u32[]{:S(2)}, u32[]{:S(2)}) collective-permute-start(bf16[16,1088]{1,0:T(8,128)(2,1)S(1)} %pad_maximum_fusion.1.own_ref), channel_id=1, source_target_pairs={{0,1},{1,0},{2,3},{3,2},{4,5},{5,4},{6,7},{7,6},{8,9},{9,8},{10,11... | collective-permute-start | bytes 104456 | tf_op jit(solution)/shard_map/rows_z/ppermute | solution.py:53
  12.8 20.6 %copy-start.6 = (f32[512]{0:T(512)S(1)}, f32[512]{0:T(512)}, u32[]{:S(2)}) copy-start(f32[512]{0:T(512)} %param.14) | copy-start | bytes 6148
  13.9 19.8 %copy-start.7 = (f32[512]{0:T(512)S(1)}, f32[512]{0:T(512)}, u32[]{:S(2)}) copy-start(f32[512]{0:T(512)} %param.15) | copy-start | bytes 6148
  16.7 26.1 %all-to-all-start = ((bf16[8,2,16,1088]{3,2,1,0:T(8,128)(2,1)}), bf16[8,2,16,1088]{3,2,1,0:T(8,128)(2,1)S(1)}, u32[]{:S(2)}, u32[]{:S(2)}) async-start(bf16[8,2,16,1088]{3,2,1,0:T(8,128)(2,1)} %pair_rows.1), calls=%async_computation | async-start | bytes 1179648 | tf_op jit(solution)/shard_map/rows_y/all_to_all | solution.py:57
  23.5 10.6 %collective-permute-start.2 = (bf16[1152,128]{1,0:T(8,128)(2,1)S(1)}, bf16[1152,128]{1,0:T(8,128)(2,1)S(1)}, u32[]{:S(2)}, u32[]{:S(2)}) collective-permute-start(bf16[1152,128]{1,0:T(8,128)(2,1)S(1)} %pad_maximum_fusion.refs_0_.refs_2_), channel_id=1, source_target_pairs={{0,32},{1,33},{2,34},{3,35},{4,36},{5,37},{6,38},{7,39},{8,40},{9,... | collective-permute-start | bytes 884744 | tf_op jit(solution)/shard_map/keys_x/ppermute | solution.py:53
  28.2 13.0 %collective-permute-start.3 = (bf16[1152,128]{1,0:T(8,128)(2,1)S(1)}, bf16[1152,128]{1,0:T(8,128)(2,1)S(1)}, u32[]{:S(2)}, u32[]{:S(2)}) collective-permute-start(bf16[1152,128]{1,0:T(8,128)(2,1)S(1)} %pad_maximum_fusion.refs_0_.refs_2_), channel_id=1, source_target_pairs={{0,48},{1,49},{2,50},{3,51},{4,52},{5,53},{6,54},{7,55},{8,56},{9,... | collective-permute-start | bytes 884744 | tf_op jit(solution)/shard_map/keys_x/ppermute | solution.py:53
  30.9 10.3 %collective-permute-start.1 = (bf16[1152,128]{1,0:T(8,128)(2,1)S(1)}, bf16[1152,128]{1,0:T(8,128)(2,1)S(1)}, u32[]{:S(2)}, u32[]{:S(2)}) collective-permute-start(bf16[1152,128]{1,0:T(8,128)(2,1)S(1)} %pad_maximum_fusion.refs_0_.refs_2_), channel_id=1, source_target_pairs={{0,16},{1,17},{2,18},{3,19},{4,20},{5,21},{6,22},{7,23},{8,24},{9,... | collective-permute-start | bytes 884744 | tf_op jit(solution)/shard_map/keys_x/ppermute | solution.py:53
  41.2 0.7 copy-start
  42.8 22.6 %copy-start.1 = (bf16[1152,128]{1,0:T(8,128)(2,1)S(1)}, bf16[1152,128]{1,0:T(8,128)(2,1)}, u32[]{:S(2)}) copy-start(bf16[1152,128]{1,0:T(8,128)(2,1)} %copy-done) | copy-start | bytes 884740
  68.9 0.7 copy-start.2
  69.6 0.7 copy-start.3
  70.3 0.7 copy-start.4
  71.0 0.7 copy-start.5
  71.7 16.7 %all-to-all-start.2 = ((f32[32,8,128]{2,1,0:T(8,128)}), f32[32,8,128]{2,1,0:T(8,128)S(1)}, u32[]{:S(2)}, u32[]{:S(2)}) async-start(f32[32,8,128]{2,1,0:T(8,128)} %copy-done.2), calls=%async_computation.2 | async-start | bytes 262144 | tf_op jit(solution)/shard_map/pair_plane/all_to_all | solution.py:57
  77.2 20.5 %collective-permute-start.4 = (f32[576,128]{1,0:T(8,128)}, f32[576,128]{1,0:T(8,128)S(1)}, u32[]{:S(2)}, u32[]{:S(2)}) collective-permute-start(f32[576,128]{1,0:T(8,128)} %copy-done.5), channel_id=1, source_target_pairs={{0,32},{1,33},{2,34},{3,35},{4,36},{5,37},{6,38},{7,39},{8,40},{9,... | collective-permute-start | bytes 884744 | tf_op jit(solution)/shard_map/shares_x/ppermute | solution.py:53
  81.9 15.9 %collective-permute-start.5 = (f32[576,128]{1,0:T(8,128)}, f32[576,128]{1,0:T(8,128)S(1)}, u32[]{:S(2)}, u32[]{:S(2)}) collective-permute-start(f32[576,128]{1,0:T(8,128)} %copy-done.4), channel_id=1, source_target_pairs={{0,16},{1,17},{2,18},{3,19},{4,20},{5,21},{6,22},{7,23},{8,24},{9,... | collective-permute-start | bytes 884744 | tf_op jit(solution)/shard_map/shares_x/ppermute | solution.py:53
  84.1 13.7 %collective-permute-start.6 = (f32[576,128]{1,0:T(8,128)}, f32[576,128]{1,0:T(8,128)S(1)}, u32[]{:S(2)}, u32[]{:S(2)}) collective-permute-start(f32[576,128]{1,0:T(8,128)} %copy-done.3), channel_id=1, source_target_pairs={{0,48},{1,49},{2,50},{3,51},{4,52},{5,53},{6,54},{7,55},{8,56},{9,... | collective-permute-start | bytes 884744 | tf_op jit(solution)/shard_map/shares_x/ppermute | solution.py:53
  89.1 16.5 %all-to-all-start.3 = ((f32[16,8,128]{2,1,0:T(8,128)}), f32[16,8,128]{2,1,0:T(8,128)S(1)}, u32[]{:S(2)}, u32[]{:S(2)}) async-start(f32[16,8,128]{2,1,0:T(8,128)} %add_pair.1), calls=%async_computation.3 | async-start | bytes 131072 | tf_op jit(solution)/shard_map/pair_column/all_to_all | solution.py:57

commit v7 on v6

--- a/solution.py
+++ b/solution.py
@@ -170,14 +170,15 @@
 
 def grads_kernel(slab, place_ref, parts_ref, keys_ref, rows_ref, *refs):
     gain_ref, gain_tangent_ref, block_refs = refs[0], refs[1], refs[2 : 2 + X]
-    share_refs, pair_ref = refs[2 + X : -1], refs[-1]
+    *share_refs, pair_ref, shares_ref, sems = refs[2 + X :]
     latent_width = gain_ref.shape[0]
     norm_gain, gain_tangent = gain_ref[...], gain_tangent_ref[...]
     turned_cot = rows_ref[:, :latent_width].T
     turned_query = rows_ref[:, latent_width:].T
     maxima, inv_totals, shift_mean, grad_mean, grad_mean_dot = merged_means(parts_ref)
     gain_grad = gain_grad_dot = 0.0
-    for behind in range(X):
+    writes = []
+    for behind in (2, 3, 1, 0):
         scores, score_dot, value_grad, value_dot, visible = block_terms(
             behind, slab, place_ref, keys_ref, rows_ref
         )
@@ -207,13 +208,16 @@
         )
         rms_cubed = inv_rms * inv_rms * inv_rms
         rms_cubed_dot = 3.0 * inv_rms * inv_rms * inv_dot
-        share_refs[behind][:latent_width, :] = (
+        shares_ref[behind, :latent_width, :] = (
             inv_dot * normed_grad
             + inv_rms * normed_grad_dot
             - (rms_cubed_dot * inner_grad + rms_cubed * inner_grad_dot) * latent
             - (rms_cubed * inner_grad) * latent_dot
         )
-        share_refs[behind][latent_width:, :] = by_query[latent_width:, key_count:]
+        shares_ref[behind, latent_width:, :] = by_query[latent_width:, key_count:]
+        write = pltpu.make_async_copy(shares_ref.at[behind], share_refs[behind], sems.at[behind])
+        write.start()
+        writes.append(write)
     pair = as_rows([jnp.sum(each, axis=1, keepdims=True) for each in (gain_grad, gain_grad_dot)])
     pair = jnp.concatenate(
         [
@@ -225,6 +229,8 @@
     )
     for copy in range(pair_ref.shape[0]):
         pair_ref[copy] = pair
+    for write in writes:
+        write.wait()
 
 
 def add_kernel(parts_ref, out_ref):
@@ -303,10 +309,14 @@
 
     *shares, pair = pl.pallas_call(
         functools.partial(grads_kernel, slab),
-        out_shape=[jax.ShapeDtypeStruct((full_width, key_count), jnp.float32)] * X
+        out_shape=[pltpu.HBM((full_width, key_count), jnp.float32)] * X
         + [jax.ShapeDtypeStruct((X * Y, SUBLANES, LANES), jnp.float32)],
         in_specs=smem + in_vmem(5 + X),
-        out_specs=in_vmem(X + 1),
+        out_specs=[pl.BlockSpec(memory_space=pltpu.HBM)] * X + in_vmem(1),
+        scratch_shapes=[
+            pltpu.VMEM((X, full_width, key_count), jnp.float32),
+            pltpu.SemaphoreType.DMA((X,)),
+        ],
         compiler_params=pltpu.CompilerParams(vmem_limit_bytes=16 * MIB),
         cost_estimate=pl.CostEstimate(
             flops=2 * flops, bytes_accessed=6 * MIB, transcendentals=X * key_count * row_count

time: 107 us -> 105 us (0.981)
  local copies, waits for them, and re-layouts: 3.78 us -> 1.63 us
    unnamed x16 -> x8, local copies, waits for them, and re-layouts: 2.81 us -> 0.65 us
where the time goes in v7:
time: 105 us
  starting transfers between devices  53.7 us (51%)
  blocking collectives  20.8 us (20%)
  waiting for transfers between devices  15.4 us (15%)
  Pallas kernels  8.6 us (8%)
  other arithmetic  2.54 us (2%)
  between operations  2.14 us (2%)
  local copies, waits for them, and re-layouts  1.63 us (2%)
    ppermute x7, starting transfers between devices, ctx_permute(): return lax.ppermute(value, 'ctx', pairs)  32.6 us
    all_to_all x3, starting transfers between devices, exchange(): return lax.all_to_all(copies, axis, 0, 0, axis_index_groups=groups)  21 us
    all_to_all x1, blocking collectives, exchange(): return lax.all_to_all(copies, axis, 0, 0, axis_index_groups=groups)  20.8 us
    all_to_all x3, waiting for transfers between devices, exchange(): return lax.all_to_all(copies, axis, 0, 0, axis_index_groups=groups)  7.92 us
    ppermute x7, waiting for transfers between devices, ctx_permute(): return lax.ppermute(value, 'ctx', pairs)  7.43 us
    pallas_call x1, Pallas kernels, shards(): pl.pallas_call(functools.partial(grads_kernel, slab), out_shape=[pltpu.HB...  4.08 us
  transfers between devices with their start and end apart: 10, of which 4 were waited for; matrix products, arithmetic and copies ran while one was open for 2% of the time, Pallas kernels for 1%

profile of v7, /device:TPU:1, one launch (start us, length us, event | category | flops | bytes accessed | tf_op | source)
XLA Modules:
  0.0 104.8 jit_solution(10320539423004804779)
XLA Ops:
  0.6 0.7 pad_maximum_fusion.1.own_ref
  1.4 11.5 %collective-permute-start = (bf16[16,1088]{1,0:T(8,128)(2,1)S(1)}, bf16[16,1088]{1,0:T(8,128)(2,1)S(1)}, u32[]{:S(2)}, u32[]{:S(2)}) collective-permute-start(bf16[16,1088]{1,0:T(8,128)(2,1)S(1)} %pad_maximum_fusion.1.own_ref), channel_id=1, source_target_pairs={{0,1},{1,0},{2,3},{3,2},{4,5},{5,4},{6,7},{7,6},{8,9},{9,8},{10,11... | collective-permute-start | bytes 104456 | tf_op jit(solution)/shard_map/rows_z/ppermute | solution.py:53
  12.8 0.0 copy-start.2
  12.8 1.0 pad_maximum_fusion.refs_0_.refs_2_
  13.9 0.0 copy-start.3
  15.2 0.1 stack.16.place_ref
  15.3 0.0 collective-permute-done.other_ref
  15.3 1.4 %pair_rows.1 = bf16[8,2,16,1088]{3,2,1,0:T(8,128)(2,1)} custom-call(s32[5]{0:T(128)S(1)} %stack.16.place_ref, bf16[16,1088]{1,0:T(8,128)(2,1)S(1)} %pad_maximum_fusion.1.own_ref, bf16[16,1088]{1,0:T(8,128)(2,1)S(1)} %collective-permute-done.other_ref), custom_call_target="tpu_custom_call" | custom-call | tf_op jit(solution)/shard_map/rows_z/pair_rows/pallas_call | solution.py:269
  16.7 6.8 %all-to-all-start = ((bf16[8,2,16,1088]{3,2,1,0:T(8,128)(2,1)}), bf16[8,2,16,1088]{3,2,1,0:T(8,128)(2,1)S(1)}, u32[]{:S(2)}, u32[]{:S(2)}) async-start(bf16[8,2,16,1088]{3,2,1,0:T(8,128)(2,1)} %pair_rows.1), calls=%async_computation | async-start | bytes 1179648 | tf_op jit(solution)/shard_map/rows_y/all_to_all | solution.py:57
  23.5 4.6 %collective-permute-start.2 = (bf16[1152,128]{1,0:T(8,128)(2,1)S(1)}, bf16[1152,128]{1,0:T(8,128)(2,1)S(1)}, u32[]{:S(2)}, u32[]{:S(2)}) collective-permute-start(bf16[1152,128]{1,0:T(8,128)(2,1)S(1)} %pad_maximum_fusion.refs_0_.refs_2_), channel_id=1, source_target_pairs={{0,32},{1,33},{2,34},{3,35},{4,36},{5,37},{6,38},{7,39},{8,40},{9,... | collective-permute-start | bytes 884744 | tf_op jit(solution)/shard_map/keys_x/ppermute | solution.py:53
  28.2 2.8 %collective-permute-start.3 = (bf16[1152,128]{1,0:T(8,128)(2,1)S(1)}, bf16[1152,128]{1,0:T(8,128)(2,1)S(1)}, u32[]{:S(2)}, u32[]{:S(2)}) collective-permute-start(bf16[1152,128]{1,0:T(8,128)(2,1)S(1)} %pad_maximum_fusion.refs_0_.refs_2_), channel_id=1, source_target_pairs={{0,48},{1,49},{2,50},{3,51},{4,52},{5,53},{6,54},{7,55},{8,56},{9,... | collective-permute-start | bytes 884744 | tf_op jit(solution)/shard_map/keys_x/ppermute | solution.py:53
  30.9 2.5 %collective-permute-start.1 = (bf16[1152,128]{1,0:T(8,128)(2,1)S(1)}, bf16[1152,128]{1,0:T(8,128)(2,1)S(1)}, u32[]{:S(2)}, u32[]{:S(2)}) collective-permute-start(bf16[1152,128]{1,0:T(8,128)(2,1)S(1)} %pad_maximum_fusion.refs_0_.refs_2_), channel_id=1, source_target_pairs={{0,16},{1,17},{2,18},{3,19},{4,20},{5,21},{6,22},{7,23},{8,24},{9,... | collective-permute-start | bytes 884744 | tf_op jit(solution)/shard_map/keys_x/ppermute | solution.py:53
  33.5 0.0 copy-done.2
  33.5 0.1 copy.10.gain_ref.refs_0_
  33.6 0.0 copy-done.3
  33.6 0.1 copy.11.gain_tangent_ref.refs_1_
  33.8 0.4 collective-permute-done.2.refs_2_.refs_4_
  34.2 7.0 %collective-permute-done.3.refs_3_.refs_5_ = bf16[1152,128]{1,0:T(8,128)(2,1)S(1)} collective-permute-done((bf16[1152,128]{1,0:T(8,128)(2,1)S(1)}, bf16[1152,128]{1,0:T(8,128)(2,1)S(1)}, u32[]{:S(2)}, u32[]{:S(2)}) %collective-permute-start.3) | collective-permute-done | bytes 294944 | tf_op jit(solution)/shard_map/keys_x/ppermute | solution.py:53
  41.2 0.0 collective-permute-done.1.refs_1_.refs_3_
  41.2 0.7 make_keys.1.keys_ref
  41.9 0.9 all-to-all-done
  42.8 1.8 %local_stats.1 = f32[16,5,2,128]{3,2,1,0:T(2,128)S(1)} custom-call(s32[5]{0:T(128)S(1)} %stack.16.place_ref, bf16[4,576,256]{2,1,0:T(8,128)(2,1)S(1)} %make_keys.1.keys_ref, bf16[256,1088]{1,0:T(8,128)(2,1)S(1)} %bitcast.18), custom_call_target="tpu_custom_call" | custom-call | flops 570425344 | bytes 3145728 | tf_op jit(solution)/shard_map/local_stats/pallas_call | solution.py:296
  44.6 20.8 %all_to_all.20.parts_ref = f32[16,5,2,128]{3,2,1,0:T(2,128)S(1)} all-to-all(f32[16,5,2,128]{3,2,1,0:T(2,128)S(1)} %local_stats.1), channel_id=1, replica_groups={{0,1,2,3,4,5,6,7,8,9,10,11,12,13,14,15},{16,17,18,19,20,21,22,23,24,25,..., dimensions={0} | all-to-all | bytes 163840 | tf_op jit(solution)/shard_map/stats_yz/all_to_all | solution.py:57
  65.4 4.1 %gradients.1 = (f32[576,128]{1,0:T(8,128)}, f32[576,128]{1,0:T(8,128)}, f32[576,128]{1,0:T(8,128)}, f32[576,128]{1,0:T(8,128)}, f32[32,8,128]{2,1,0:T(8,128)S(1)}) custom-call(s32[5]{0:T(128)S(1)} %stack.16.place_ref, f32[16,5,2,128]{3,2,1,0:T(2,128)S(1)} %all_to_all.20.parts_ref, bf16[4,576,256]{2,1,0:T(8,128)(2,1)S(1)} %make_keys.1.keys_ref, ...), custom_call_target="tpu_custom_call" | custom-call | flops 1140850688 | bytes 6291456 | tf_op jit(solution)/shard_map/gradients/pallas_call | solution.py:310
  69.5 0.0 copy-start
  69.5 0.6 copy-done
  70.1 5.5 %all-to-all-start.2 = ((f32[32,8,128]{2,1,0:T(8,128)}), f32[32,8,128]{2,1,0:T(8,128)S(1)}, u32[]{:S(2)}, u32[]{:S(2)}) async-start(f32[32,8,128]{2,1,0:T(8,128)} %copy-done), calls=%async_computation.2 | async-start | bytes 262144 | tf_op jit(solution)/shard_map/pair_plane/all_to_all | solution.py:57
  75.7 4.6 %collective-permute-start.4 = (f32[576,128]{1,0:T(8,128)}, f32[576,128]{1,0:T(8,128)S(1)}, u32[]{:S(2)}, u32[]{:S(2)}) collective-permute-start(f32[576,128]{1,0:T(8,128)} %get-tuple-element.12), channel_id=1, source_target_pairs={{0,32},{1,33},{2,34},{3,35},{4,36},{5,37},{6,38},{7,39},{8,40},{9,... | collective-permute-start | bytes 884744 | tf_op jit(solution)/shard_map/shares_x/ppermute | solution.py:53
  80.3 2.2 %collective-permute-start.5 = (f32[576,128]{1,0:T(8,128)}, f32[576,128]{1,0:T(8,128)S(1)}, u32[]{:S(2)}, u32[]{:S(2)}) collective-permute-start(f32[576,128]{1,0:T(8,128)} %get-tuple-element.13), channel_id=1, source_target_pairs={{0,16},{1,17},{2,18},{3,19},{4,20},{5,21},{6,22},{7,23},{8,24},{9,... | collective-permute-start | bytes 884744 | tf_op jit(solution)/shard_map/shares_x/ppermute | solution.py:53
  82.5 0.0 copy-start.1
  82.6 4.4 %collective-permute-start.6 = (f32[576,128]{1,0:T(8,128)}, f32[576,128]{1,0:T(8,128)S(1)}, u32[]{:S(2)}, u32[]{:S(2)}) collective-permute-start(f32[576,128]{1,0:T(8,128)} %get-tuple-element.14), channel_id=1, source_target_pairs={{0,48},{1,49},{2,50},{3,51},{4,52},{5,53},{6,54},{7,55},{8,56},{9,... | collective-permute-start | bytes 884744 | tf_op jit(solution)/shard_map/shares_x/ppermute | solution.py:53
  87.0 0.0 all-to-all-done.2.parts_ref
  87.0 0.7 add_pair.1
  87.6 8.7 %all-to-all-start.3 = ((f32[16,8,128]{2,1,0:T(8,128)}), f32[16,8,128]{2,1,0:T(8,128)S(1)}, u32[]{:S(2)}, u32[]{:S(2)}) async-start(f32[16,8,128]{2,1,0:T(8,128)} %add_pair.1), calls=%async_computation.3 | async-start | bytes 131072 | tf_op jit(solution)/shard_map/pair_column/all_to_all | solution.py:57
  96.3 0.0 collective-permute-done.4
  96.3 0.0 collective-permute-done.5
  96.3 0.0 collective-permute-done.6
  96.4 0.0 copy-done.1
  96.4 0.8 add_bitcast_fusion
  97.1 7.0 %all-to-all-done.3 = f32[16,8,128]{2,1,0:T(8,128)S(1)} async-done(((f32[16,8,128]{2,1,0:T(8,128)}), f32[16,8,128]{2,1,0:T(8,128)S(1)}, u32[]{:S(2)}, u32[]{:S(2)}) %all-to-all-start.3) | async-done | bytes 65568 | tf_op jit(solution)/shard_map/pair_column/all_to_all | solution.py:57
  104.2 0.6 reshape.21
  (1 shorter events, 0.0 us)
Async XLA Ops:
  1.4 13.9 %collective-permute-start = (bf16[16,1088]{1,0:T(8,128)(2,1)S(1)}, bf16[16,1088]{1,0:T(8,128)(2,1)S(1)}, u32[]{:S(2)}, u32[]{:S(2)}) collective-permute-start(bf16[16,1088]{1,0:T(8,128)(2,1)S(1)} %pad_maximum_fusion.1.own_ref), channel_id=1, source_target_pairs={{0,1},{1,0},{2,3},{3,2},{4,5},{5,4},{6,7},{7,6},{8,9},{9,8},{10,11... | collective-permute-start | bytes 104456 | tf_op jit(solution)/shard_map/rows_z/ppermute | solution.py:53
  12.8 20.6 %copy-start.2 = (f32[512]{0:T(512)S(1)}, f32[512]{0:T(512)}, u32[]{:S(2)}) copy-start(f32[512]{0:T(512)} %param.14) | copy-start | bytes 6148
  13.9 19.8 %copy-start.3 = (f32[512]{0:T(512)S(1)}, f32[512]{0:T(512)}, u32[]{:S(2)}) copy-start(f32[512]{0:T(512)} %param.15) | copy-start | bytes 6148
  16.7 26.1 %all-to-all-start = ((bf16[8,2,16,1088]{3,2,1,0:T(8,128)(2,1)}), bf16[8,2,16,1088]{3,2,1,0:T(8,128)(2,1)S(1)}, u32[]{:S(2)}, u32[]{:S(2)}) async-start(bf16[8,2,16,1088]{3,2,1,0:T(8,128)(2,1)} %pair_rows.1), calls=%async_computation | async-start | bytes 1179648 | tf_op jit(solution)/shard_map/rows_y/all_to_all | solution.py:57
  23.5 10.6 %collective-permute-start.2 = (bf16[1152,128]{1,0:T(8,128)(2,1)S(1)}, bf16[1152,128]{1,0:T(8,128)(2,1)S(1)}, u32[]{:S(2)}, u32[]{:S(2)}) collective-permute-start(bf16[1152,128]{1,0:T(8,128)(2,1)S(1)} %pad_maximum_fusion.refs_0_.refs_2_), channel_id=1, source_target_pairs={{0,32},{1,33},{2,34},{3,35},{4,36},{5,37},{6,38},{7,39},{8,40},{9,... | collective-permute-start | bytes 884744 | tf_op jit(solution)/shard_map/keys_x/ppermute | solution.py:53
  28.2 13.0 %collective-permute-start.3 = (bf16[1152,128]{1,0:T(8,128)(2,1)S(1)}, bf16[1152,128]{1,0:T(8,128)(2,1)S(1)}, u32[]{:S(2)}, u32[]{:S(2)}) collective-permute-start(bf16[1152,128]{1,0:T(8,128)(2,1)S(1)} %pad_maximum_fusion.refs_0_.refs_2_), channel_id=1, source_target_pairs={{0,48},{1,49},{2,50},{3,51},{4,52},{5,53},{6,54},{7,55},{8,56},{9,... | collective-permute-start | bytes 884744 | tf_op jit(solution)/shard_map/keys_x/ppermute | solution.py:53
  30.9 10.3 %collective-permute-start.1 = (bf16[1152,128]{1,0:T(8,128)(2,1)S(1)}, bf16[1152,128]{1,0:T(8,128)(2,1)S(1)}, u32[]{:S(2)}, u32[]{:S(2)}) collective-permute-start(bf16[1152,128]{1,0:T(8,128)(2,1)S(1)} %pad_maximum_fusion.refs_0_.refs_2_), channel_id=1, source_target_pairs={{0,16},{1,17},{2,18},{3,19},{4,20},{5,21},{6,22},{7,23},{8,24},{9,... | collective-permute-start | bytes 884744 | tf_op jit(solution)/shard_map/keys_x/ppermute | solution.py:53
  69.5 0.6 copy-start
  70.1 16.9 %all-to-all-start.2 = ((f32[32,8,128]{2,1,0:T(8,128)}), f32[32,8,128]{2,1,0:T(8,128)S(1)}, u32[]{:S(2)}, u32[]{:S(2)}) async-start(f32[32,8,128]{2,1,0:T(8,128)} %copy-done), calls=%async_computation.2 | async-start | bytes 262144 | tf_op jit(solution)/shard_map/pair_plane/all_to_all | solution.py:57
  75.7 20.7 %collective-permute-start.4 = (f32[576,128]{1,0:T(8,128)}, f32[576,128]{1,0:T(8,128)S(1)}, u32[]{:S(2)}, u32[]{:S(2)}) collective-permute-start(f32[576,128]{1,0:T(8,128)} %get-tuple-element.12), channel_id=1, source_target_pairs={{0,32},{1,33},{2,34},{3,35},{4,36},{5,37},{6,38},{7,39},{8,40},{9,... | collective-permute-start | bytes 884744 | tf_op jit(solution)/shard_map/shares_x/ppermute | solution.py:53
  80.3 16.0 %collective-permute-start.5 = (f32[576,128]{1,0:T(8,128)}, f32[576,128]{1,0:T(8,128)S(1)}, u32[]{:S(2)}, u32[]{:S(2)}) collective-permute-start(f32[576,128]{1,0:T(8,128)} %get-tuple-element.13), channel_id=1, source_target_pairs={{0,16},{1,17},{2,18},{3,19},{4,20},{5,21},{6,22},{7,23},{8,24},{9,... | collective-permute-start | bytes 884744 | tf_op jit(solution)/shard_map/shares_x/ppermute | solution.py:53
  82.5 13.8 %copy-start.1 = (f32[576,128]{1,0:T(8,128)S(1)}, f32[576,128]{1,0:T(8,128)}, u32[]{:S(2)}) copy-start(f32[576,128]{1,0:T(8,128)} %get-tuple-element.11) | copy-start | bytes 884740
  82.6 13.8 %collective-permute-start.6 = (f32[576,128]{1,0:T(8,128)}, f32[576,128]{1,0:T(8,128)S(1)}, u32[]{:S(2)}, u32[]{:S(2)}) collective-permute-start(f32[576,128]{1,0:T(8,128)} %get-tuple-element.14), channel_id=1, source_target_pairs={{0,48},{1,49},{2,50},{3,51},{4,52},{5,53},{6,54},{7,55},{8,56},{9,... | collective-permute-start | bytes 884744 | tf_op jit(solution)/shard_map/shares_x/ppermute | solution.py:53
  87.6 16.5 %all-to-all-start.3 = ((f32[16,8,128]{2,1,0:T(8,128)}), f32[16,8,128]{2,1,0:T(8,128)S(1)}, u32[]{:S(2)}, u32[]{:S(2)}) async-start(f32[16,8,128]{2,1,0:T(8,128)} %add_pair.1), calls=%async_computation.3 | async-start | bytes 131072 | tf_op jit(solution)/shard_map/pair_column/all_to_all | solution.py:57

commit v8 on v7

--- a/solution.py
+++ b/solution.py
@@ -29,7 +29,6 @@
     return (z % ZL * CORE + core) * CTX + ctx_index(x, y, z // ZL)
 
 
-Y_GROUPS = [[ctx_index(x, y, z) for y in range(Y)] for x in range(X) for z in range(ZH)]
 YZ_GROUPS = [[ctx_index(x, y, z) for y in range(Y) for z in range(ZH)] for x in range(X)]
 COLUMNS = [
     [device_index(x, y, z, core) for z in range(Z) for core in range(CORE)]
@@ -43,9 +42,9 @@
 ]
 
 
-def ctx_permute(value, dx=0, dz=0):
+def ctx_permute(value, dx):
     pairs = [
-        (ctx_index(x, y, z), ctx_index((x + dx) % X, y, (z + dz) % ZH))
+        (ctx_index(x, y, z), ctx_index((x + dx) % X, y, z))
         for x in range(X)
         for y in range(Y)
         for z in range(ZH)
@@ -61,16 +60,14 @@
     return jnp.dot(left, right, preferred_element_type=jnp.float32)
 
 
-def pair_kernel(latent_width, place_ref, own_ref, other_ref, out_ref):
-    z, live_count = place_ref[1], place_ref[3]
-    shape = own_ref.shape
-    row = lax.broadcasted_iota(jnp.int32, shape, 0)
-    column = lax.broadcasted_iota(jnp.int32, shape, 1)
-    kept = (row < live_count) | (column >= latent_width)
-    for at, ref in ((z, own_ref), (1 - z, other_ref)):
-        rows = jnp.where(kept, ref[...].astype(jnp.float32), 0.0).astype(ref.dtype)
-        for copy in range(Y):
-            out_ref[copy, at] = rows
+def pack_kernel(place_ref, cot_ref, query_ref, out_ref):
+    row = lax.broadcasted_iota(jnp.int32, cot_ref.shape, 0)
+    cot = jnp.where(row < place_ref[2], cot_ref[...].astype(jnp.float32), 0.0)
+    cot, query = cot.astype(cot_ref.dtype), query_ref[...]
+    width = cot.shape[1]
+    for copy in range(out_ref.shape[0]):
+        out_ref[copy, :, :width] = cot
+        out_ref[copy, :, width:] = query
 
 
 def norm_side(block_ref, latent_width):
@@ -107,10 +104,10 @@
     by_query = score_scale * dot(rows_ref[:, latent_width:], keys)
     by_cot = dot(rows_ref[:, :latent_width], keys[:latent_width])
     x = lax.rem(place_ref[0] + (X - behind), X)
-    key_pos = (x * (Y * ZH) + place_ref[4]) * key_count
+    key_pos = (x * (Y * ZH) + place_ref[3]) * key_count
     key_pos += lax.broadcasted_iota(jnp.int32, (row_count, key_count), 1)
     slab_row = lax.broadcasted_iota(jnp.int32, (row_count, key_count), 0) % slab
-    visible = key_pos <= place_ref[2] + slab_row
+    visible = key_pos <= place_ref[1] + slab_row
     return (
         by_query[:, :key_count],
         by_query[:, key_count:],
@@ -255,29 +252,24 @@
     place = jnp.stack(
         [
             ctx_at // (Y * ZH),
-            ctx_at % ZH,
             offsets[0],
             lengths[0] - offsets[0],
             ctx_at % (Y * ZH),
         ]
     )
 
-    packed = jnp.concatenate(
-        [cotangent.reshape(slab, latent_width), queries.reshape(slab, full_width)], axis=1
-    )
-    with jax.named_scope("rows_z"):
+    with jax.named_scope("rows_yz"):
         copies = pl.pallas_call(
-            functools.partial(pair_kernel, latent_width),
-            out_shape=jax.ShapeDtypeStruct((Y, ZH, slab, packed_width), packed.dtype),
+            pack_kernel,
+            out_shape=jax.ShapeDtypeStruct((Y * ZH, slab, packed_width), queries.dtype),
             in_specs=smem + in_vmem(2),
             out_specs=pl.BlockSpec(memory_space=pltpu.VMEM),
             compiler_params=pltpu.CompilerParams(vmem_limit_bytes=4 * MIB),
-            name="pair_rows",
-        )(place, packed, ctx_permute(packed, dz=1))
-    with jax.named_scope("rows_y"):
+            name="pack_rows",
+        )(place, cotangent.reshape(slab, latent_width), queries.reshape(slab, full_width))
         block = jnp.concatenate([kv_rows[0].T, kv_tangent[0].T], axis=0)
         near_block, copies = lax.optimization_barrier((block, copies))
-        rows = exchange(copies, "ctx", Y_GROUPS).reshape(row_count, packed_width)
+        rows = exchange(copies, "ctx", YZ_GROUPS).reshape(row_count, packed_width)
 
     with jax.named_scope("keys_x"):
         far_block = ctx_permute(block, dx=2)

time: 105 us -> 105 us (level)
  waiting for transfers between devices: 15.4 us -> 18.6 us
  starting transfers between devices: 53.7 us -> 50.8 us
  blocking collectives: 20.8 us -> 19.1 us
  local copies, waits for them, and re-layouts: 1.63 us -> 3 us
    ppermute x7 -> x6, starting transfers between devices: 32.6 us -> 21.2 us  [ctx_permute(): return lax.ppermute(value, 'ctx', pairs)]
    all_to_all x3, starting transfers between devices: 21 us -> 29.6 us  [exchange(): return lax.all_to_all(copies, axis, 0, 0, axis_index_groups=groups)]
    all_to_all x3, waiting for transfers between devices: 7.92 us -> 11.1 us  [exchange(): return lax.all_to_all(copies, axis, 0, 0, axis_index_groups=groups)]
    all_to_all x1, blocking collectives: 20.8 us -> 19.1 us  [exchange(): return lax.all_to_all(copies, axis, 0, 0, axis_index_groups=groups)]
    unnamed x8 -> x12, local copies, waits for them, and re-layouts: 0.65 us -> 2.11 us
    ppermute x7 -> x6, waiting for transfers between devices: 7.43 us -> 7.44 us  [ctx_permute(): return lax.ppermute(value, 'ctx', pairs)]
  transfers between devices with their start and end apart: 10 -> 9, of which waited for: 4 -> 4; matrix products, arithmetic and copies ran while one was open for 2% -> 1% of each run, Pallas kernels for 1% -> 1%
where the time goes in v8:
time: 105 us; the launch traced here: 104 us
  starting transfers between devices  50.8 us (48%)
  blocking collectives  19.1 us (18%)
  waiting for transfers between devices  18.6 us (18%)
  Pallas kernels  8.76 us (8%)
  local copies, waits for them, and re-layouts  3 us (3%)
  between operations  2.13 us (2%)
  other arithmetic  1.88 us (2%)
    all_to_all x3, starting transfers between devices, exchange(): return lax.all_to_all(copies, axis, 0, 0, axis_index_groups=groups)  29.6 us
    ppermute x6, starting transfers between devices, ctx_permute(): return lax.ppermute(value, 'ctx', pairs)  21.2 us
    all_to_all x1, blocking collectives, exchange(): return lax.all_to_all(copies, axis, 0, 0, axis_index_groups=groups)  19.1 us
    all_to_all x3, waiting for transfers between devices, exchange(): return lax.all_to_all(copies, axis, 0, 0, axis_index_groups=groups)  11.1 us
    ppermute x6, waiting for transfers between devices, ctx_permute(): return lax.ppermute(value, 'ctx', pairs)  7.44 us
    pallas_call x1, Pallas kernels, shards(): pl.pallas_call(functools.partial(grads_kernel, slab), out_shape=[pltpu.HB...  4.22 us
    unnamed x12, local copies, waits for them, and re-layouts  2.11 us
  transfers between devices with their start and end apart: 9, of which 4 were waited for; matrix products, arithmetic and copies ran while one was open for 1% of the time, Pallas kernels for 1%

profile of v8, /device:TPU:1, one launch (start us, length us, event | category | flops | bytes accessed | tf_op | source)
XLA Modules:
  0.0 104.2 jit_solution(1310451183541147962)
XLA Ops:
  1.9 0.0 copy-start.4
  2.0 1.0 pad_maximum_fusion.refs_0_.refs_2_
  3.0 0.0 copy-start.5
  3.0 0.1 pad_add_fusion.place_ref
  3.1 0.0 copy-start.1
  3.1 0.7 copy-done.1
  3.8 0.0 copy-start.2
  3.8 0.7 copy-done.2
  4.5 1.4 %pack_rows.1 = bf16[16,16,1088]{2,1,0:T(8,128)(2,1)} custom-call(s32[4]{0:T(128)S(1)} %pad_add_fusion.place_ref, bf16[16,512]{1,0:T(8,128)(2,1)S(1)} %bitcast.20, bf16[16,576]{1,0:T(8,128)(2,1)S(1)} %bitcast.19), custom_call_target="tpu_custom_call" | custom-call | tf_op jit(solution)/shard_map/rows_yz/pack_rows/pallas_call | solution.py:262
  5.9 16.2 %all-to-all-start = ((bf16[16,16,1088]{2,1,0:T(8,128)(2,1)}), bf16[16,16,1088]{2,1,0:T(8,128)(2,1)S(1)}, u32[]{:S(2)}, u32[]{:S(2)}) async-start(bf16[16,16,1088]{2,1,0:T(8,128)(2,1)} %pack_rows.1), calls=%async_computation | async-start | bytes 1179648 | tf_op jit(solution)/shard_map/rows_yz/all_to_all | solution.py:56
  22.1 4.7 %collective-permute-start.1 = (bf16[1152,128]{1,0:T(8,128)(2,1)S(1)}, bf16[1152,128]{1,0:T(8,128)(2,1)S(1)}, u32[]{:S(2)}, u32[]{:S(2)}) collective-permute-start(bf16[1152,128]{1,0:T(8,128)(2,1)S(1)} %pad_maximum_fusion.refs_0_.refs_2_), channel_id=1, source_target_pairs={{0,32},{1,33},{2,34},{3,35},{4,36},{5,37},{6,38},{7,39},{8,40},{9,... | collective-permute-start | bytes 884744 | tf_op jit(solution)/shard_map/keys_x/ppermute | solution.py:52
  26.8 2.8 %collective-permute-start.2 = (bf16[1152,128]{1,0:T(8,128)(2,1)S(1)}, bf16[1152,128]{1,0:T(8,128)(2,1)S(1)}, u32[]{:S(2)}, u32[]{:S(2)}) collective-permute-start(bf16[1152,128]{1,0:T(8,128)(2,1)S(1)} %pad_maximum_fusion.refs_0_.refs_2_), channel_id=1, source_target_pairs={{0,48},{1,49},{2,50},{3,51},{4,52},{5,53},{6,54},{7,55},{8,56},{9,... | collective-permute-start | bytes 884744 | tf_op jit(solution)/shard_map/keys_x/ppermute | solution.py:52
  29.5 2.5 %collective-permute-start = (bf16[1152,128]{1,0:T(8,128)(2,1)S(1)}, bf16[1152,128]{1,0:T(8,128)(2,1)S(1)}, u32[]{:S(2)}, u32[]{:S(2)}) collective-permute-start(bf16[1152,128]{1,0:T(8,128)(2,1)S(1)} %pad_maximum_fusion.refs_0_.refs_2_), channel_id=1, source_target_pairs={{0,16},{1,17},{2,18},{3,19},{4,20},{5,21},{6,22},{7,23},{8,24},{9,... | collective-permute-start | bytes 884744 | tf_op jit(solution)/shard_map/keys_x/ppermute | solution.py:52
  32.1 0.0 copy-done.4
  32.1 0.1 copy.10.gain_ref.refs_0_
  32.2 0.0 copy-done.5
  32.2 0.1 copy.11.gain_tangent_ref.refs_1_
  32.4 0.7 collective-permute-done.1.refs_2_.refs_4_
  33.1 6.8 %collective-permute-done.2.refs_3_.refs_5_ = bf16[1152,128]{1,0:T(8,128)(2,1)S(1)} collective-permute-done((bf16[1152,128]{1,0:T(8,128)(2,1)S(1)}, bf16[1152,128]{1,0:T(8,128)(2,1)S(1)}, u32[]{:S(2)}, u32[]{:S(2)}) %collective-permute-start.2) | collective-permute-done | bytes 294944 | tf_op jit(solution)/shard_map/keys_x/ppermute | solution.py:52
  39.8 0.0 collective-permute-done.refs_1_.refs_3_
  39.8 0.7 make_keys.1.keys_ref
  40.6 4.1 %all-to-all-done = bf16[16,16,1088]{2,1,0:T(8,128)(2,1)S(1)} async-done(((bf16[16,16,1088]{2,1,0:T(8,128)(2,1)}), bf16[16,16,1088]{2,1,0:T(8,128)(2,1)S(1)}, u32[]{:S(2)}, u32[]{:S(2)}) %all-to-all-start) | async-done | bytes 557088 | tf_op jit(solution)/shard_map/rows_yz/all_to_all | solution.py:56
  44.7 1.8 %local_stats.1 = f32[16,5,2,128]{3,2,1,0:T(2,128)S(1)} custom-call(s32[4]{0:T(128)S(1)} %pad_add_fusion.place_ref, bf16[4,576,256]{2,1,0:T(8,128)(2,1)S(1)} %make_keys.1.keys_ref, bf16[256,1088]{1,0:T(8,128)(2,1)S(1)} %bitcast.17), custom_call_target="tpu_custom_call" | custom-call | flops 570425344 | bytes 3145728 | tf_op jit(solution)/shard_map/local_stats/pallas_call | solution.py:288
  46.5 19.1 %all_to_all.20.parts_ref = f32[16,5,2,128]{3,2,1,0:T(2,128)S(1)} all-to-all(f32[16,5,2,128]{3,2,1,0:T(2,128)S(1)} %local_stats.1), channel_id=1, replica_groups={{0,1,2,3,4,5,6,7,8,9,10,11,12,13,14,15},{16,17,18,19,20,21,22,23,24,25,..., dimensions={0} | all-to-all | bytes 163840 | tf_op jit(solution)/shard_map/stats_yz/all_to_all | solution.py:56
  65.6 4.2 %gradients.1 = (f32[576,128]{1,0:T(8,128)}, f32[576,128]{1,0:T(8,128)}, f32[576,128]{1,0:T(8,128)}, f32[576,128]{1,0:T(8,128)}, f32[32,8,128]{2,1,0:T(8,128)S(1)}) custom-call(s32[4]{0:T(128)S(1)} %pad_add_fusion.place_ref, f32[16,5,2,128]{3,2,1,0:T(2,128)S(1)} %all_to_all.20.parts_ref, bf16[4,576,256]{2,1,0:T(8,128)(2,1)S(1)} %make_keys.1.keys_ref, ...), custom_call_target="tpu_custom_call" | custom-call | flops 1140850688 | bytes 6291456 | tf_op jit(solution)/shard_map/gradients/pallas_call | solution.py:302
  69.8 0.0 copy-start
  69.8 0.6 copy-done
  70.4 5.5 %all-to-all-start.2 = ((f32[32,8,128]{2,1,0:T(8,128)}), f32[32,8,128]{2,1,0:T(8,128)S(1)}, u32[]{:S(2)}, u32[]{:S(2)}) async-start(f32[32,8,128]{2,1,0:T(8,128)} %copy-done), calls=%async_computation.2 | async-start | bytes 262144 | tf_op jit(solution)/shard_map/pair_plane/all_to_all | solution.py:56
  76.0 4.6 %collective-permute-start.3 = (f32[576,128]{1,0:T(8,128)}, f32[576,128]{1,0:T(8,128)S(1)}, u32[]{:S(2)}, u32[]{:S(2)}) collective-permute-start(f32[576,128]{1,0:T(8,128)} %get-tuple-element.12), channel_id=1, source_target_pairs={{0,32},{1,33},{2,34},{3,35},{4,36},{5,37},{6,38},{7,39},{8,40},{9,... | collective-permute-start | bytes 884744 | tf_op jit(solution)/shard_map/shares_x/ppermute | solution.py:52
  80.6 2.2 %collective-permute-start.4 = (f32[576,128]{1,0:T(8,128)}, f32[576,128]{1,0:T(8,128)S(1)}, u32[]{:S(2)}, u32[]{:S(2)}) collective-permute-start(f32[576,128]{1,0:T(8,128)} %get-tuple-element.13), channel_id=1, source_target_pairs={{0,16},{1,17},{2,18},{3,19},{4,20},{5,21},{6,22},{7,23},{8,24},{9,... | collective-permute-start | bytes 884744 | tf_op jit(solution)/shard_map/shares_x/ppermute | solution.py:52
  82.9 0.0 copy-start.3
  82.9 4.4 %collective-permute-start.5 = (f32[576,128]{1,0:T(8,128)}, f32[576,128]{1,0:T(8,128)S(1)}, u32[]{:S(2)}, u32[]{:S(2)}) collective-permute-start(f32[576,128]{1,0:T(8,128)} %get-tuple-element.14), channel_id=1, source_target_pairs={{0,48},{1,49},{2,50},{3,51},{4,52},{5,53},{6,54},{7,55},{8,56},{9,... | collective-permute-start | bytes 884744 | tf_op jit(solution)/shard_map/shares_x/ppermute | solution.py:52
  87.3 0.0 all-to-all-done.2.parts_ref
  87.3 0.7 add_pair.1
  87.9 7.9 %all-to-all-start.3 = ((f32[16,8,128]{2,1,0:T(8,128)}), f32[16,8,128]{2,1,0:T(8,128)S(1)}, u32[]{:S(2)}, u32[]{:S(2)}) async-start(f32[16,8,128]{2,1,0:T(8,128)} %add_pair.1), calls=%async_computation.3 | async-start | bytes 131072 | tf_op jit(solution)/shard_map/pair_column/all_to_all | solution.py:56
  95.8 0.0 collective-permute-done.3
  95.8 0.0 collective-permute-done.4
  95.8 0.0 collective-permute-done.5
  95.8 0.0 copy-done.3
  95.9 0.8 add_bitcast_fusion
  96.6 7.0 %all-to-all-done.3 = f32[16,8,128]{2,1,0:T(8,128)S(1)} async-done(((f32[16,8,128]{2,1,0:T(8,128)}), f32[16,8,128]{2,1,0:T(8,128)S(1)}, u32[]{:S(2)}, u32[]{:S(2)}) %all-to-all-start.3) | async-done | bytes 65568 | tf_op jit(solution)/shard_map/pair_column/all_to_all | solution.py:56
  103.6 0.6 reshape.21
  (1 shorter events, 0.0 us)
Async XLA Ops:
  1.9 30.1 %copy-start.4 = (f32[512]{0:T(512)S(1)}, f32[512]{0:T(512)}, u32[]{:S(2)}) copy-start(f32[512]{0:T(512)} %param.14) | copy-start | bytes 6148
  3.0 29.3 %copy-start.5 = (f32[512]{0:T(512)S(1)}, f32[512]{0:T(512)}, u32[]{:S(2)}) copy-start(f32[512]{0:T(512)} %param.15) | copy-start | bytes 6148
  3.1 0.7 copy-start.1
  3.8 0.7 copy-start.2
  5.9 38.8 %all-to-all-start = ((bf16[16,16,1088]{2,1,0:T(8,128)(2,1)}), bf16[16,16,1088]{2,1,0:T(8,128)(2,1)S(1)}, u32[]{:S(2)}, u32[]{:S(2)}) async-start(bf16[16,16,1088]{2,1,0:T(8,128)(2,1)} %pack_rows.1), calls=%async_computation | async-start | bytes 1179648 | tf_op jit(solution)/shard_map/rows_yz/all_to_all | solution.py:56
  22.1 11.0 %collective-permute-start.1 = (bf16[1152,128]{1,0:T(8,128)(2,1)S(1)}, bf16[1152,128]{1,0:T(8,128)(2,1)S(1)}, u32[]{:S(2)}, u32[]{:S(2)}) collective-permute-start(bf16[1152,128]{1,0:T(8,128)(2,1)S(1)} %pad_maximum_fusion.refs_0_.refs_2_), channel_id=1, source_target_pairs={{0,32},{1,33},{2,34},{3,35},{4,36},{5,37},{6,38},{7,39},{8,40},{9,... | collective-permute-start | bytes 884744 | tf_op jit(solution)/shard_map/keys_x/ppermute | solution.py:52
  26.8 13.1 %collective-permute-start.2 = (bf16[1152,128]{1,0:T(8,128)(2,1)S(1)}, bf16[1152,128]{1,0:T(8,128)(2,1)S(1)}, u32[]{:S(2)}, u32[]{:S(2)}) collective-permute-start(bf16[1152,128]{1,0:T(8,128)(2,1)S(1)} %pad_maximum_fusion.refs_0_.refs_2_), channel_id=1, source_target_pairs={{0,48},{1,49},{2,50},{3,51},{4,52},{5,53},{6,54},{7,55},{8,56},{9,... | collective-permute-start | bytes 884744 | tf_op jit(solution)/shard_map/keys_x/ppermute | solution.py:52
  29.5 10.3 %collective-permute-start = (bf16[1152,128]{1,0:T(8,128)(2,1)S(1)}, bf16[1152,128]{1,0:T(8,128)(2,1)S(1)}, u32[]{:S(2)}, u32[]{:S(2)}) collective-permute-start(bf16[1152,128]{1,0:T(8,128)(2,1)S(1)} %pad_maximum_fusion.refs_0_.refs_2_), channel_id=1, source_target_pairs={{0,16},{1,17},{2,18},{3,19},{4,20},{5,21},{6,22},{7,23},{8,24},{9,... | collective-permute-start | bytes 884744 | tf_op jit(solution)/shard_map/keys_x/ppermute | solution.py:52
  69.8 0.7 copy-start
  70.4 16.8 %all-to-all-start.2 = ((f32[32,8,128]{2,1,0:T(8,128)}), f32[32,8,128]{2,1,0:T(8,128)S(1)}, u32[]{:S(2)}, u32[]{:S(2)}) async-start(f32[32,8,128]{2,1,0:T(8,128)} %copy-done), calls=%async_computation.2 | async-start | bytes 262144 | tf_op jit(solution)/shard_map/pair_plane/all_to_all | solution.py:56
  76.0 19.9 %collective-permute-start.3 = (f32[576,128]{1,0:T(8,128)}, f32[576,128]{1,0:T(8,128)S(1)}, u32[]{:S(2)}, u32[]{:S(2)}) collective-permute-start(f32[576,128]{1,0:T(8,128)} %get-tuple-element.12), channel_id=1, source_target_pairs={{0,32},{1,33},{2,34},{3,35},{4,36},{5,37},{6,38},{7,39},{8,40},{9,... | collective-permute-start | bytes 884744 | tf_op jit(solution)/shard_map/shares_x/ppermute | solution.py:52
  80.6 15.2 %collective-permute-start.4 = (f32[576,128]{1,0:T(8,128)}, f32[576,128]{1,0:T(8,128)S(1)}, u32[]{:S(2)}, u32[]{:S(2)}) collective-permute-start(f32[576,128]{1,0:T(8,128)} %get-tuple-element.13), channel_id=1, source_target_pairs={{0,16},{1,17},{2,18},{3,19},{4,20},{5,21},{6,22},{7,23},{8,24},{9,... | collective-permute-start | bytes 884744 | tf_op jit(solution)/shard_map/shares_x/ppermute | solution.py:52
  82.9 13.0 %copy-start.3 = (f32[576,128]{1,0:T(8,128)S(1)}, f32[576,128]{1,0:T(8,128)}, u32[]{:S(2)}) copy-start(f32[576,128]{1,0:T(8,128)} %get-tuple-element.11) | copy-start | bytes 884740
  82.9 13.0 %collective-permute-start.5 = (f32[576,128]{1,0:T(8,128)}, f32[576,128]{1,0:T(8,128)S(1)}, u32[]{:S(2)}, u32[]{:S(2)}) collective-permute-start(f32[576,128]{1,0:T(8,128)} %get-tuple-element.14), channel_id=1, source_target_pairs={{0,48},{1,49},{2,50},{3,51},{4,52},{5,53},{6,54},{7,55},{8,56},{9,... | collective-permute-start | bytes 884744 | tf_op jit(solution)/shard_map/shares_x/ppermute | solution.py:52
  87.9 15.7 %all-to-all-start.3 = ((f32[16,8,128]{2,1,0:T(8,128)}), f32[16,8,128]{2,1,0:T(8,128)S(1)}, u32[]{:S(2)}, u32[]{:S(2)}) async-start(f32[16,8,128]{2,1,0:T(8,128)} %add_pair.1), calls=%async_computation.3 | async-start | bytes 131072 | tf_op jit(solution)/shard_map/pair_column/all_to_all | solution.py:56

commit v9 on v8

--- a/solution.py
+++ b/solution.py
@@ -264,16 +264,15 @@
             out_shape=jax.ShapeDtypeStruct((Y * ZH, slab, packed_width), queries.dtype),
             in_specs=smem + in_vmem(2),
             out_specs=pl.BlockSpec(memory_space=pltpu.VMEM),
-            compiler_params=pltpu.CompilerParams(vmem_limit_bytes=4 * MIB),
             name="pack_rows",
         )(place, cotangent.reshape(slab, latent_width), queries.reshape(slab, full_width))
+        kv_rows, kv_tangent, copies = lax.optimization_barrier((kv_rows, kv_tangent, copies))
         block = jnp.concatenate([kv_rows[0].T, kv_tangent[0].T], axis=0)
-        near_block, copies = lax.optimization_barrier((block, copies))
         rows = exchange(copies, "ctx", YZ_GROUPS).reshape(row_count, packed_width)
 
     with jax.named_scope("keys_x"):
         far_block = ctx_permute(block, dx=2)
-        near_blocks = [ctx_permute(near_block, dx=step) for step in (1, -1)]
+        near_blocks = [ctx_permute(block, dx=step) for step in (1, -1)]
         blocks = [block, near_blocks[0], far_block, near_blocks[1]]
     gains = (norm_gain[:, None], gain_tangent[:, None])
     keys = pl.pallas_call(

time: 105 us -> 107 us (1.019)
  blocking collectives: 19.1 us -> 23.2 us
  starting transfers between devices: 50.8 us -> 48.2 us
  waiting for transfers between devices: 18.6 us -> 20.4 us
  local copies, waits for them, and re-layouts: 3 us -> 1.56 us
    ppermute x6, waiting for transfers between devices: 7.44 us -> 13.4 us  [ctx_permute(): return lax.ppermute(value, 'ctx', pairs)]
    all_to_all x1, blocking collectives: 19.1 us -> 23.2 us  [exchange(): return lax.all_to_all(copies, axis, 0, 0, axis_index_groups=groups)]
    all_to_all x3, waiting for transfers between devices: 11.1 us -> 7.01 us  [exchange(): return lax.all_to_all(copies, axis, 0, 0, axis_index_groups=groups)]
    all_to_all x3, starting transfers between devices: 29.6 us -> 27.6 us  [exchange(): return lax.all_to_all(copies, axis, 0, 0, axis_index_groups=groups)]
    unnamed x12 -> x14, local copies, waits for them, and re-layouts: 2.11 us -> 0.67 us
where the time goes in v9:
time: 107 us; the launch traced here: 106 us
  starting transfers between devices  48.2 us (45%)
  blocking collectives  23.2 us (22%)
  waiting for transfers between devices  20.4 us (19%)
  Pallas kernels  8.92 us (8%)
  between operations  2.22 us (2%)
  local copies, waits for them, and re-layouts  1.56 us (1%)
  other arithmetic  1.39 us (1%)
    all_to_all x3, starting transfers between devices, exchange(): return lax.all_to_all(copies, axis, 0, 0, axis_index_groups=groups)  27.6 us
    all_to_all x1, blocking collectives, exchange(): return lax.all_to_all(copies, axis, 0, 0, axis_index_groups=groups)  23.2 us
    ppermute x6, starting transfers between devices, ctx_permute(): return lax.ppermute(value, 'ctx', pairs)  20.6 us
    ppermute x6, waiting for transfers between devices, ctx_permute(): return lax.ppermute(value, 'ctx', pairs)  13.4 us
    all_to_all x3, waiting for transfers between devices, exchange(): return lax.all_to_all(copies, axis, 0, 0, axis_index_groups=groups)  7.01 us
    pallas_call x1, Pallas kernels, shards(): pl.pallas_call(functools.partial(grads_kernel, slab), out_shape=[pltpu.HB...  4.12 us
  transfers between devices with their start and end apart: 9, of which 4 were waited for; matrix products, arithmetic and copies ran while one was open for 1% of the time, Pallas kernels for 1%

profile of v9, /device:TPU:1, one launch (start us, length us, event | category | flops | bytes accessed | tf_op | source)
XLA Modules:
  0.0 105.9 jit_solution(912073531329144294)
XLA Ops:
  0.6 0.0 copy-start.3
  0.6 0.0 copy-start.4
  2.0 0.6 pad_add_fusion.place_ref
  2.6 0.0 copy-start.5
  2.6 0.0 copy-start.6
  2.6 1.7 %pack_rows.1 = bf16[16,16,1088]{2,1,0:T(8,128)(2,1)} custom-call(s32[4]{0:T(128)} %pad_add_fusion.place_ref, bf16[16,512]{1,0:T(8,128)(2,1)} %bitcast.22, bf16[16,576]{1,0:T(8,128)(2,1)} %bitcast.21), custom_call_target="tpu_custom_call" | custom-call | tf_op jit(solution)/shard_map/rows_yz/pack_rows/pallas_call | solution.py:262
  4.3 16.2 %all-to-all-start = ((bf16[16,16,1088]{2,1,0:T(8,128)(2,1)}), bf16[16,16,1088]{2,1,0:T(8,128)(2,1)S(1)}, u32[]{:S(2)}, u32[]{:S(2)}) async-start(bf16[16,16,1088]{2,1,0:T(8,128)(2,1)} %pack_rows.1), calls=%async_computation | async-start | bytes 1179648 | tf_op jit(solution)/shard_map/rows_yz/all_to_all | solution.py:56
  20.5 0.0 copy-done.3
  20.5 0.0 copy-done.4
  20.5 4.4 %collective-permute-start.2 = (bf16[1152,128]{1,0:T(8,128)(2,1)S(1)}, bf16[1152,128]{1,0:T(8,128)(2,1)S(1)}, u32[]{:S(2)}, u32[]{:S(2)}) collective-permute-start(bf16[1152,128]{1,0:T(8,128)(2,1)S(1)} %pad_maximum_fusion.refs_0_.refs_2_), channel_id=1, source_target_pairs={{0,48},{1,49},{2,50},{3,51},{4,52},{5,53},{6,54},{7,55},{8,56},{9,... | collective-permute-start | bytes 884744 | tf_op jit(solution)/shard_map/keys_x/ppermute | solution.py:52
  24.9 2.4 %collective-permute-start.1 = (bf16[1152,128]{1,0:T(8,128)(2,1)S(1)}, bf16[1152,128]{1,0:T(8,128)(2,1)S(1)}, u32[]{:S(2)}, u32[]{:S(2)}) collective-permute-start(bf16[1152,128]{1,0:T(8,128)(2,1)S(1)} %pad_maximum_fusion.refs_0_.refs_2_), channel_id=1, source_target_pairs={{0,32},{1,33},{2,34},{3,35},{4,36},{5,37},{6,38},{7,39},{8,40},{9,... | collective-permute-start | bytes 884744 | tf_op jit(solution)/shard_map/keys_x/ppermute | solution.py:52
  27.3 2.5 %collective-permute-start = (bf16[1152,128]{1,0:T(8,128)(2,1)S(1)}, bf16[1152,128]{1,0:T(8,128)(2,1)S(1)}, u32[]{:S(2)}, u32[]{:S(2)}) collective-permute-start(bf16[1152,128]{1,0:T(8,128)(2,1)S(1)} %pad_maximum_fusion.refs_0_.refs_2_), channel_id=1, source_target_pairs={{0,16},{1,17},{2,18},{3,19},{4,20},{5,21},{6,22},{7,23},{8,24},{9,... | collective-permute-start | bytes 884744 | tf_op jit(solution)/shard_map/keys_x/ppermute | solution.py:52
  29.9 0.0 copy-done.5
  29.9 0.1 copy.10.gain_ref.refs_0_
  30.0 0.0 copy-done.6
  30.0 0.1 copy.11.gain_tangent_ref.refs_1_
  30.2 0.0 copy-start.1
  30.2 0.8 collective-permute-done.2.refs_3_.refs_5_
  31.0 4.6 %collective-permute-done.1.refs_2_.refs_4_ = bf16[1152,128]{1,0:T(8,128)(2,1)S(1)} collective-permute-done((bf16[1152,128]{1,0:T(8,128)(2,1)S(1)}, bf16[1152,128]{1,0:T(8,128)(2,1)S(1)}, u32[]{:S(2)}, u32[]{:S(2)}) %collective-permute-start.1) | collective-permute-done | bytes 294944 | tf_op jit(solution)/shard_map/keys_x/ppermute | solution.py:52
  35.6 7.9 %collective-permute-done.refs_1_.refs_3_ = bf16[1152,128]{1,0:T(8,128)(2,1)S(1)} collective-permute-done((bf16[1152,128]{1,0:T(8,128)(2,1)S(1)}, bf16[1152,128]{1,0:T(8,128)(2,1)S(1)}, u32[]{:S(2)}, u32[]{:S(2)}) %collective-permute-start) | collective-permute-done | bytes 294944 | tf_op jit(solution)/shard_map/keys_x/ppermute | solution.py:52
  43.6 0.7 make_keys.1.keys_ref
  44.3 0.0 all-to-all-done
  44.3 0.0 copy-done.1
  44.3 1.8 %local_stats.1 = f32[16,5,2,128]{3,2,1,0:T(2,128)S(1)} custom-call(s32[4]{0:T(128)S(1)} %copy-done.1, bf16[4,576,256]{2,1,0:T(8,128)(2,1)S(1)} %make_keys.1.keys_ref, bf16[256,1088]{1,0:T(8,128)(2,1)S(1)} %bitcast.17), custom_call_target="tpu_custom_call" | custom-call | flops 570425344 | bytes 3145728 | tf_op jit(solution)/shard_map/local_stats/pallas_call | solution.py:287
  46.1 23.2 %all_to_all.20.parts_ref = f32[16,5,2,128]{3,2,1,0:T(2,128)S(1)} all-to-all(f32[16,5,2,128]{3,2,1,0:T(2,128)S(1)} %local_stats.1), channel_id=1, replica_groups={{0,1,2,3,4,5,6,7,8,9,10,11,12,13,14,15},{16,17,18,19,20,21,22,23,24,25,..., dimensions={0} | all-to-all | bytes 163840 | tf_op jit(solution)/shard_map/stats_yz/all_to_all | solution.py:56
  69.3 4.1 %gradients.1 = (f32[576,128]{1,0:T(8,128)}, f32[576,128]{1,0:T(8,128)}, f32[576,128]{1,0:T(8,128)}, f32[576,128]{1,0:T(8,128)}, f32[32,8,128]{2,1,0:T(8,128)S(1)}) custom-call(s32[4]{0:T(128)S(1)} %copy-done.1, f32[16,5,2,128]{3,2,1,0:T(2,128)S(1)} %all_to_all.20.parts_ref, bf16[4,576,256]{2,1,0:T(8,128)(2,1)S(1)} %make_keys.1.keys_ref, ...), custom_call_target="tpu_custom_call" | custom-call | flops 1140850688 | bytes 6291456 | tf_op jit(solution)/shard_map/gradients/pallas_call | solution.py:301
  73.4 0.0 copy-start
  73.4 0.6 copy-done
  74.1 3.8 %all-to-all-start.2 = ((f32[32,8,128]{2,1,0:T(8,128)}), f32[32,8,128]{2,1,0:T(8,128)S(1)}, u32[]{:S(2)}, u32[]{:S(2)}) async-start(f32[32,8,128]{2,1,0:T(8,128)} %copy-done), calls=%async_computation.2 | async-start | bytes 262144 | tf_op jit(solution)/shard_map/pair_plane/all_to_all | solution.py:56
  77.9 4.6 %collective-permute-start.3 = (f32[576,128]{1,0:T(8,128)}, f32[576,128]{1,0:T(8,128)S(1)}, u32[]{:S(2)}, u32[]{:S(2)}) collective-permute-start(f32[576,128]{1,0:T(8,128)} %get-tuple-element.14), channel_id=1, source_target_pairs={{0,32},{1,33},{2,34},{3,35},{4,36},{5,37},{6,38},{7,39},{8,40},{9,... | collective-permute-start | bytes 884744 | tf_op jit(solution)/shard_map/shares_x/ppermute | solution.py:52
  82.6 2.2 %collective-permute-start.4 = (f32[576,128]{1,0:T(8,128)}, f32[576,128]{1,0:T(8,128)S(1)}, u32[]{:S(2)}, u32[]{:S(2)}) collective-permute-start(f32[576,128]{1,0:T(8,128)} %get-tuple-element.15), channel_id=1, source_target_pairs={{0,16},{1,17},{2,18},{3,19},{4,20},{5,21},{6,22},{7,23},{8,24},{9,... | collective-permute-start | bytes 884744 | tf_op jit(solution)/shard_map/shares_x/ppermute | solution.py:52
  84.8 0.0 copy-start.2
  84.8 4.4 %collective-permute-start.5 = (f32[576,128]{1,0:T(8,128)}, f32[576,128]{1,0:T(8,128)S(1)}, u32[]{:S(2)}, u32[]{:S(2)}) collective-permute-start(f32[576,128]{1,0:T(8,128)} %get-tuple-element.16), channel_id=1, source_target_pairs={{0,48},{1,49},{2,50},{3,51},{4,52},{5,53},{6,54},{7,55},{8,56},{9,... | collective-permute-start | bytes 884744 | tf_op jit(solution)/shard_map/shares_x/ppermute | solution.py:52
  89.2 0.0 all-to-all-done.2.parts_ref
  89.2 0.7 add_pair.1
  89.9 7.6 %all-to-all-start.3 = ((f32[16,8,128]{2,1,0:T(8,128)}), f32[16,8,128]{2,1,0:T(8,128)S(1)}, u32[]{:S(2)}, u32[]{:S(2)}) async-start(f32[16,8,128]{2,1,0:T(8,128)} %add_pair.1), calls=%async_computation.3 | async-start | bytes 131072 | tf_op jit(solution)/shard_map/pair_column/all_to_all | solution.py:56
  97.5 0.0 collective-permute-done.3
  97.5 0.0 collective-permute-done.4
  97.5 0.0 collective-permute-done.5
  97.5 0.0 copy-done.2
  97.5 0.8 add_bitcast_fusion
  98.3 7.0 %all-to-all-done.3 = f32[16,8,128]{2,1,0:T(8,128)S(1)} async-done(((f32[16,8,128]{2,1,0:T(8,128)}), f32[16,8,128]{2,1,0:T(8,128)S(1)}, u32[]{:S(2)}, u32[]{:S(2)}) %all-to-all-start.3) | async-done | bytes 65568 | tf_op jit(solution)/shard_map/pair_column/all_to_all | solution.py:56
  105.3 0.6 reshape.21
  (2 shorter events, 0.0 us)
Async XLA Ops:
  0.6 19.8 %copy-start.3 = (bf16[1,128,576]{1,2,0:T(8,128)(2,1)S(1)}, bf16[1,128,576]{1,2,0:T(8,128)(2,1)}, u32[]{:S(2)}) copy-start(bf16[1,128,576]{1,2,0:T(8,128)(2,1)} %param.13) | copy-start | bytes 442372
  0.6 19.8 %copy-start.4 = (bf16[1,128,576]{1,2,0:T(8,128)(2,1)S(1)}, bf16[1,128,576]{1,2,0:T(8,128)(2,1)}, u32[]{:S(2)}) copy-start(bf16[1,128,576]{1,2,0:T(8,128)(2,1)} %param.12) | copy-start | bytes 442372
  2.6 27.3 %copy-start.5 = (f32[512]{0:T(512)S(1)}, f32[512]{0:T(512)}, u32[]{:S(2)}) copy-start(f32[512]{0:T(512)} %param.14) | copy-start | bytes 6148
  2.6 27.4 %copy-start.6 = (f32[512]{0:T(512)S(1)}, f32[512]{0:T(512)}, u32[]{:S(2)}) copy-start(f32[512]{0:T(512)} %param.15) | copy-start | bytes 6148
  4.3 40.0 %all-to-all-start = ((bf16[16,16,1088]{2,1,0:T(8,128)(2,1)}), bf16[16,16,1088]{2,1,0:T(8,128)(2,1)S(1)}, u32[]{:S(2)}, u32[]{:S(2)}) async-start(bf16[16,16,1088]{2,1,0:T(8,128)(2,1)} %pack_rows.1), calls=%async_computation | async-start | bytes 1179648 | tf_op jit(solution)/shard_map/rows_yz/all_to_all | solution.py:56
  20.5 10.5 %collective-permute-start.2 = (bf16[1152,128]{1,0:T(8,128)(2,1)S(1)}, bf16[1152,128]{1,0:T(8,128)(2,1)S(1)}, u32[]{:S(2)}, u32[]{:S(2)}) collective-permute-start(bf16[1152,128]{1,0:T(8,128)(2,1)S(1)} %pad_maximum_fusion.refs_0_.refs_2_), channel_id=1, source_target_pairs={{0,48},{1,49},{2,50},{3,51},{4,52},{5,53},{6,54},{7,55},{8,56},{9,... | collective-permute-start | bytes 884744 | tf_op jit(solution)/shard_map/keys_x/ppermute | solution.py:52
  24.9 10.7 %collective-permute-start.1 = (bf16[1152,128]{1,0:T(8,128)(2,1)S(1)}, bf16[1152,128]{1,0:T(8,128)(2,1)S(1)}, u32[]{:S(2)}, u32[]{:S(2)}) collective-permute-start(bf16[1152,128]{1,0:T(8,128)(2,1)S(1)} %pad_maximum_fusion.refs_0_.refs_2_), channel_id=1, source_target_pairs={{0,32},{1,33},{2,34},{3,35},{4,36},{5,37},{6,38},{7,39},{8,40},{9,... | collective-permute-start | bytes 884744 | tf_op jit(solution)/shard_map/keys_x/ppermute | solution.py:52
  27.3 16.2 %collective-permute-start = (bf16[1152,128]{1,0:T(8,128)(2,1)S(1)}, bf16[1152,128]{1,0:T(8,128)(2,1)S(1)}, u32[]{:S(2)}, u32[]{:S(2)}) collective-permute-start(bf16[1152,128]{1,0:T(8,128)(2,1)S(1)} %pad_maximum_fusion.refs_0_.refs_2_), channel_id=1, source_target_pairs={{0,16},{1,17},{2,18},{3,19},{4,20},{5,21},{6,22},{7,23},{8,24},{9,... | collective-permute-start | bytes 884744 | tf_op jit(solution)/shard_map/keys_x/ppermute | solution.py:52
  30.2 14.1 %copy-start.1 = (s32[4]{0:T(128)S(1)}, s32[4]{0:T(128)}, u32[]{:S(2)}) copy-start(s32[4]{0:T(128)} %pad_add_fusion.place_ref) | copy-start | bytes 52
  73.4 0.7 copy-start
  74.1 15.1 %all-to-all-start.2 = ((f32[32,8,128]{2,1,0:T(8,128)}), f32[32,8,128]{2,1,0:T(8,128)S(1)}, u32[]{:S(2)}, u32[]{:S(2)}) async-start(f32[32,8,128]{2,1,0:T(8,128)} %copy-done), calls=%async_computation.2 | async-start | bytes 262144 | tf_op jit(solution)/shard_map/pair_plane/all_to_all | solution.py:56
  77.9 19.6 %collective-permute-start.3 = (f32[576,128]{1,0:T(8,128)}, f32[576,128]{1,0:T(8,128)S(1)}, u32[]{:S(2)}, u32[]{:S(2)}) collective-permute-start(f32[576,128]{1,0:T(8,128)} %get-tuple-element.14), channel_id=1, source_target_pairs={{0,32},{1,33},{2,34},{3,35},{4,36},{5,37},{6,38},{7,39},{8,40},{9,... | collective-permute-start | bytes 884744 | tf_op jit(solution)/shard_map/shares_x/ppermute | solution.py:52
  82.6 14.9 %collective-permute-start.4 = (f32[576,128]{1,0:T(8,128)}, f32[576,128]{1,0:T(8,128)S(1)}, u32[]{:S(2)}, u32[]{:S(2)}) collective-permute-start(f32[576,128]{1,0:T(8,128)} %get-tuple-element.15), channel_id=1, source_target_pairs={{0,16},{1,17},{2,18},{3,19},{4,20},{5,21},{6,22},{7,23},{8,24},{9,... | collective-permute-start | bytes 884744 | tf_op jit(solution)/shard_map/shares_x/ppermute | solution.py:52
  84.8 12.7 %copy-start.2 = (f32[576,128]{1,0:T(8,128)S(1)}, f32[576,128]{1,0:T(8,128)}, u32[]{:S(2)}) copy-start(f32[576,128]{1,0:T(8,128)} %get-tuple-element.13) | copy-start | bytes 884740
  84.8 12.7 %collective-permute-start.5 = (f32[576,128]{1,0:T(8,128)}, f32[576,128]{1,0:T(8,128)S(1)}, u32[]{:S(2)}, u32[]{:S(2)}) collective-permute-start(f32[576,128]{1,0:T(8,128)} %get-tuple-element.16), channel_id=1, source_target_pairs={{0,48},{1,49},{2,50},{3,51},{4,52},{5,53},{6,54},{7,55},{8,56},{9,... | collective-permute-start | bytes 884744 | tf_op jit(solution)/shard_map/shares_x/ppermute | solution.py:52
  89.9 15.4 %all-to-all-start.3 = ((f32[16,8,128]{2,1,0:T(8,128)}), f32[16,8,128]{2,1,0:T(8,128)S(1)}, u32[]{:S(2)}, u32[]{:S(2)}) async-start(f32[16,8,128]{2,1,0:T(8,128)} %add_pair.1), calls=%async_computation.3 | async-start | bytes 131072 | tf_op jit(solution)/shard_map/pair_column/all_to_all | solution.py:56
